TPU v7x, 1024 devices: a whole 4x4x32 slice. The times are simulated.
1024 devices in a mesh: rep: 64 (over z, x_lo), tp: 16 (over x_hi, y, core).
Axes of the slice: x: 4 (x_hi: 2, x_lo: 2; x = x_hi * 2 + x_lo), y: 4, z: 32, core: 2. Of those that a mesh axis runs over, the one named last changes fastest.
Arguments:
- stream_in: bfloat16 [256, 4, 8192], P('rep', None, 'tp'), may hold values from -6 to 6
- queries: bfloat16 [256, 4, 4096], P('rep'), may hold values from -90 to 90
- new_keys: bfloat16 [256, 4, 4, 128], P('rep'), may hold values from -4 to 4
- new_values: bfloat16 [256, 4, 4, 128], P('rep'), may hold values from -4 to 4
- key_cache: bfloat16 [256, 4096, 4, 128], P('rep', 'tp'), may hold values from -4.1 to 4.1
- value_cache: bfloat16 [256, 4096, 4, 128], P('rep', 'tp'), may hold values from -4 to 4
- lengths: int32 [256], P('rep'), may hold values from 2 to 4096
- out_weight: bfloat16 [4096, 8192], P('tp', 'rep'), may hold values from -0.09375 to 0.09375
- norm_gain: bfloat16 [8192], P('tp'), may hold values from 0.5 to 1.5
Outputs:
- stream_out: bfloat16 [256, 4, 8192], P('rep', None, 'tp')
- normed: bfloat16 [256, 4, 8192], P('rep', None, 'tp')
All inputs are finite; a program needn't handle non-finite values.
Results may differ from a plain program's by a relative error of at most 0.0065.
Values may be sent and summed in bfloat16 or wider, within the bound.
No kernel may reach another device: no remote copies, remote signals or barrier semaphores. Data moves between devices by JAX's collectives and lax.ppermute only.
A program may use at most 32 MiB of HBM per device.

v0:
```python
import math

import jax
import jax.numpy as jnp
from jax import lax
from jax.sharding import Mesh
from jax.sharding import PartitionSpec as P

D = 8192
REP = ("rep_0", "rep_1")


def sent_to_all(shard, axis):
    copies = jnp.broadcast_to(shard, (lax.axis_size(axis), *shard.shape))
    return lax.all_to_all(copies, axis, split_axis=0, concat_axis=0, tiled=True)


def of_everyone(shard, axis):
    return sent_to_all(shard, axis).max(axis=0)


def cut_along(shard, dim, devices):
    before, after = (shard.shape[:dim], shard.shape[dim + 1 :])
    return jnp.moveaxis(shard.reshape(*before, devices, -1, *after), dim, 0)


def sent_and_summed(shard, axis, dim):
    devices = lax.axis_size(axis)
    parts = lax.all_to_all(cut_along(shard, dim, devices), axis, 0, 0, tiled=True)
    return jnp.sum(parts.astype(jnp.float32), axis=0)


def side_by_side(arrays, axis, dim, along):
    columns = [a.reshape(*a.shape[:along], -1) for a in arrays]
    both = jnp.concatenate(columns, axis=along)
    filled, at, gathered = (sent_and_summed(both, axis, dim), 0, [])
    for a, column in zip(arrays, columns):
        share = filled[..., at : at + column.shape[along]]
        gathered.append(share.reshape(*share.shape[:along], *a.shape[along:]))
        at += column.shape[along]
    return tuple(gathered)


def whole_of(shard, axes, dim):
    for axis in reversed(axes):
        shard = lax.all_gather(shard, axis, axis=dim, tiled=True)
    return shard


def taken_together(shard, axis):
    return sent_to_all(shard, axis).sum(axis=0)


def on_device(
    stream_in, queries, new_keys, new_values, key_cache, value_cache, lengths, out_weight, norm_gain
):
    row_count, step_count, width = queries.shape
    kv_heads, head_dim = (key_cache.shape[2], key_cache.shape[3])
    block_len = key_cache.shape[1]
    group_size = width // head_dim // kv_heads
    tp_index = lax.axis_index("tp")
    scaling = 1.0 / math.sqrt(head_dim)
    grouped = queries.reshape(row_count, step_count, kv_heads, group_size, head_dim)
    cached = (
        jnp.einsum("bsgjd,bpgd->bsgjp", grouped, key_cache, preferred_element_type=jnp.float32)
        * scaling
    )
    positions = tp_index * block_len + jnp.arange(block_len, dtype=jnp.int32)
    visible = positions[None, :] < lengths[:, None]
    cached = jnp.where(visible[:, None, None, None, :], cached, -1e30)
    fresh = (
        jnp.einsum("bsgjd,btgd->bsgjt", grouped, new_keys, preferred_element_type=jnp.float32)
        * scaling
    )
    causal = (jnp.arange(step_count)[None, :] <= jnp.arange(step_count)[:, None]) & (tp_index == 0)
    fresh = jnp.where(causal[None, :, None, None, :], fresh, -1e30)
    local_maxima = jnp.maximum(cached.max(-1), fresh.max(-1))
    maxima = of_everyone(local_maxima, "tp")
    weights_cached = jnp.exp(cached - maxima[..., None])
    weights_fresh = jnp.exp(fresh - maxima[..., None])
    denominator = weights_cached.sum(-1) + weights_fresh.sum(-1)
    numerator = jnp.einsum(
        "bsgjp,bpgd->bsgjd",
        weights_cached.astype(jnp.bfloat16),
        value_cache,
        preferred_element_type=jnp.float32,
    )
    numerator = numerator + jnp.einsum(
        "bsgjt,btgd->bsgjd",
        weights_fresh.astype(jnp.bfloat16),
        new_values,
        preferred_element_type=jnp.float32,
    )
    numerator = numerator.reshape(row_count, step_count, kv_heads * group_size, head_dim)
    denominator = denominator.reshape(row_count, step_count, kv_heads * group_size)
    numerator, denominator = side_by_side(
        (numerator.astype(jnp.bfloat16), denominator.astype(jnp.bfloat16)), "tp", 2, 3
    )
    attended = (numerator / denominator[..., None]).astype(jnp.bfloat16)
    attended = attended.reshape(row_count * step_count, -1)
    projected = jnp.dot(
        whole_of(attended, REP, 0), out_weight, preferred_element_type=jnp.float32
    ).astype(jnp.bfloat16)
    partial_value = lax.all_to_all(projected, REP, split_axis=0, concat_axis=1, tiled=True).astype(
        jnp.float32
    )
    summed = sent_and_summed(partial_value.astype(jnp.bfloat16), "tp", 1)
    hidden = stream_in.reshape(row_count * step_count, -1).astype(jnp.float32) + summed
    squares = taken_together(jnp.sum(hidden * hidden, axis=1), "tp")
    inverse = lax.rsqrt(squares / D + 1e-06)
    normed = hidden * inverse[:, None] * norm_gain.astype(jnp.float32)[None, :]
    stream_out = hidden.astype(jnp.bfloat16).reshape(row_count, step_count, -1)
    return (stream_out, normed.astype(jnp.bfloat16).reshape(row_count, step_count, -1))


def solution(mesh):
    finer = Mesh(mesh.devices.reshape(32, 2, mesh.shape["tp"]), ("rep_0", "rep_1", "tp"))
    in_specs = (
        P(REP, None, "tp"),
        P(REP, None, None),
        P(REP, None, None, None),
        P(REP, None, None, None),
        P(REP, "tp", None, None),
        P(REP, "tp", None, None),
        P(REP),
        P("tp", REP),
        P("tp"),
    )
    out_specs = (P(REP, None, "tp"), P(REP, None, "tp"))
    return jax.shard_map(
        on_device, mesh=finer, in_specs=in_specs, out_specs=out_specs, check_vma=False
    )
```

profile of v0, /device:TPU:1, one launch (start us, length us, event | category | flops | bytes accessed | tf_op | source)
XLA Modules:
  0.0 187.3 jit_solution(18072662797087358496)
XLA Ops:
  0.6 0.0 copy-start
  0.6 1.1 reshape.128
  1.8 0.0 copy-start.5
  1.8 0.6 copy-done.5
  2.5 0.1 broadcast_compare_fusion
  2.6 1.8 fusion.24
  4.3 0.0 copy-done.6
  4.3 0.7 fusion.25
  5.1 0.1 broadcast_in_dim.46
  5.2 0.5 reshape.135
  5.7 23.9 %all_to_all.37 = f32[16,1,512]{2,1,0:T(1,128)S(1)} all-to-all(f32[16,1,512]{2,1,0:T(1,128)S(1)} %reshape.135), channel_id=1, replica_groups=mesh['rep_0'=32,'rep_1'=2,'tp'=16] {'tp'}, dimensions={0} | all-to-all | bytes 65536 | tf_op jit(solution)/shard_map/all_to_all | solution.py:15
  29.7 0.5 broadcast.69
  30.2 0.7 reduce.2
  30.9 0.6 reshape.136
  31.5 0.1 reduce_max.29
  31.7 0.3 fusion.9
  32.0 0.0 copy-done
  32.0 0.3 fusion.6
  32.3 0.0 copy-start.3
  32.3 0.1 fusion.15
  32.5 0.6 copy-done.3
  33.0 0.3 fusion.3
  33.3 0.2 copy.71
  33.5 1.0 copy.72
  34.5 0.3 maximum_bitcast_fusion
  34.9 0.2 copy.73
  35.1 11.6 %all_to_all.38 = bf16[16,4,4,2,129]{4,3,2,1,0:T(2,128)(2,1)S(1)} all-to-all(bf16[16,4,4,2,129]{4,3,2,1,0:T(2,128)(2,1)S(1)} %copy.73), channel_id=1, replica_groups=mesh['rep_0'=32,'rep_1'=2,'tp'=16] {'tp'}, dimensions={0} | all-to-all | bytes 264192 | tf_op jit(solution)/shard_map/all_to_all | solution.py:29
  46.7 0.3 convert_reduce_fusion.1
  47.0 0.2 copy.91
  47.2 0.1 fusion.21
  47.3 3.2 %all_gather.6 = bf16[32,256]{1,0:T(8,128)(2,1)S(1)} all-gather(bf16[16,256]{1,0:T(8,128)(2,1)S(1)} %bitcast.35), channel_id=1, replica_groups=mesh['rep_0'=32,'rep_1'=2,'tp'=16] {'rep_1'}, dimensions={0}, use_global_device_ids=true | all-gather | bytes 24576 | tf_op jit(solution)/shard_map/all_gather | solution.py:46
  50.5 48.4 %all_gather.7 = bf16[1024,256]{1,0:T(8,128)(2,1)S(1)} all-gather(bf16[32,256]{1,0:T(8,128)(2,1)S(1)} %all_gather.6), channel_id=1, replica_groups=mesh['rep_0'=32,'rep_1'=2,'tp'=16] {'rep_0'}, dimensions={0}, use_global_device_ids=true | all-gather | bytes 540672 | tf_op jit(solution)/shard_map/all_gather | solution.py:46
  98.9 0.0 copy-done.2
  98.9 0.3 convolution_convert_fusion
  99.2 44.8 %all_to_all.39 = bf16[64,16,128]{2,1,0:T(8,128)(2,1)S(1)} all-to-all(bf16[64,16,128]{2,1,0:T(8,128)(2,1)S(1)} %bitcast.30), channel_id=1, replica_groups=mesh['rep_0'=32,'rep_1'=2,'tp'=16] {'rep_0','rep_1'}, dimensions={0} | all-to-all | bytes 524288 | tf_op jit(solution)/shard_map/all_to_all | solution.py:104
  144.0 0.1 copy.76
  144.1 0.2 reshape.130
  144.2 0.2 copy.77
  144.4 29.2 %all_to_all.40 = bf16[16,16,512]{2,1,0:T(8,128)(2,1)S(1)} all-to-all(bf16[16,16,512]{2,1,0:T(8,128)(2,1)S(1)} %copy.77), channel_id=1, replica_groups=mesh['rep_0'=32,'rep_1'=2,'tp'=16] {'tp'}, dimensions={0} | all-to-all | bytes 524288 | tf_op jit(solution)/shard_map/all_to_all | solution.py:29
  173.6 0.0 copy-start.1
  173.6 0.7 copy-done.1
  174.3 0.1 multiply_reduce_fusion
  174.4 0.1 broadcast_in_dim.47
  174.5 0.6 broadcast_in_dim.48
  175.1 4.4 %all-to-all-start.4 = ((f32[16,1,16]{2,1,0:T(1,128)}), f32[16,1,16]{2,1,0:T(1,128)S(1)}, u32[]{:S(2)}, u32[]{:S(2)}) async-start(f32[16,1,16]{2,1,0:T(1,128)} %broadcast_in_dim.48), calls=%async_computation.4 | async-start | bytes 16384 | tf_op jit(solution)/shard_map/all_to_all | solution.py:15
  179.5 7.0 %all-to-all-done.4 = f32[16,1,16]{2,1,0:T(1,128)S(1)} async-done(((f32[16,1,16]{2,1,0:T(1,128)}), f32[16,1,16]{2,1,0:T(1,128)S(1)}, u32[]{:S(2)}, u32[]{:S(2)}) %all-to-all-start.4) | async-done | bytes 1056 | tf_op jit(solution)/shard_map/all_to_all | solution.py:15
  186.5 0.1 rsqrt.11
  186.6 0.7 multiply_convert_fusion
  (18 shorter events, 0.2 us)
Async XLA Ops:
  0.6 31.4 %copy-start = (bf16[4,256,4,128]{3,2,1,0:T(4,128)(2,1)S(1)}, bf16[4,256,4,128]{3,2,1,0:T(4,128)(2,1)}, u32[]{:S(2)}) copy-start(bf16[4,256,4,128]{3,2,1,0:T(4,128)(2,1)} %param.14) | copy-start | bytes 3145732
  1.8 0.7 copy-start.5
  2.6 1.8 copy-start.6
  32.3 0.7 copy-start.3
  50.5 48.4 %copy-start.2 = (bf16[256,128]{1,0:T(8,128)(2,1)S(1)}, bf16[256,128]{1,0:T(8,128)(2,1)}, u32[]{:S(2)}) copy-start(bf16[256,128]{1,0:T(8,128)(2,1)} %param.16) | copy-start | bytes 196612
  173.6 0.7 copy-start.1
  175.1 4.4 %copy-start.4 = (bf16[512]{0:T(512)(128)(2,1)S(1)}, bf16[512]{0:T(512)(128)(2,1)}, u32[]{:S(2)}) copy-start(bf16[512]{0:T(512)(128)(2,1)} %param.17) | copy-start | bytes 3076
  175.1 11.4 %all-to-all-start.4 = ((f32[16,1,16]{2,1,0:T(1,128)}), f32[16,1,16]{2,1,0:T(1,128)S(1)}, u32[]{:S(2)}, u32[]{:S(2)}) async-start(f32[16,1,16]{2,1,0:T(1,128)} %broadcast_in_dim.48), calls=%async_computation.4 | async-start | bytes 16384 | tf_op jit(solution)/shard_map/all_to_all | solution.py:15
where the time goes:
time: 188 us; the launch traced here: 187 us
  blocking collectives  161 us (86%)
  local copies, waits for them, and re-layouts  7.72 us (4%)
  waiting for transfers between devices  6.97 us (4%)
  starting transfers between devices  4.37 us (2%)
  matrix products  3.33 us (2%)
  other arithmetic  2.94 us (2%)
    all_gather x2, blocking collectives, whole_of(): shard = lax.all_gather(shard, axis, axis=dim, tiled=True)  51.6 us
    all_to_all x1, blocking collectives, on_device(): lax.all_to_all(projected, REP, split_axis=0, concat_axis=1, tiled=True)  44.8 us
    all_to_all x2, blocking collectives, sent_and_summed(): lax.all_to_all(cut_along(shard, dim, devices), axis, 0, 0, tiled=True)  40.7 us
    all_to_all x1, blocking collectives, sent_to_all(): return lax.all_to_all(copies, axis, split_axis=0, concat_axis=0, tiled=True)  23.9 us
    all_to_all x1, waiting for transfers between devices, sent_to_all(): return lax.all_to_all(copies, axis, split_axis=0, concat_axis=0, tiled=True)  6.97 us
    all_to_all x1, starting transfers between devices, sent_to_all(): return lax.all_to_all(copies, axis, split_axis=0, concat_axis=0, tiled=True)  4.37 us
  transfers between devices with their start and end apart: 1, of which 1 were waited for; matrix products, arithmetic and copies ran while one was open for 0% of the time, Pallas kernels for 0%

commit v1 on v0

v1 whole, which is shorter than its diff:
```python
import math

import jax
import jax.numpy as jnp
from jax import lax
from jax.experimental import pallas as pl
from jax.experimental.pallas import tpu as pltpu
from jax.sharding import Mesh
from jax.sharding import PartitionSpec as P

D = 8192
REP = ("ra", "rb", "rc")
FAR = ("ra", "rb")
NEAR = "rc"
MASKED = -1e30
F32, BF16 = jnp.float32, jnp.bfloat16


def exchanged(pieces, axes):
    return lax.all_to_all(pieces, axes, split_axis=0, concat_axis=0, tiled=True)


def permuted(array, axes, count, target):
    return lax.ppermute(array, axes, [(i, target(i)) for i in range(count)])


def dot_rows(a, b):
    return lax.dot_general(a, b, (((1,), (1,)), ((), ())), preferred_element_type=F32)


def stacked(pieces, axis=0):
    return jnp.concatenate(pieces, axis=axis)


def attend_kernel(len_ref, q_ref, nk_ref, nv_ref, k_ref, v_ref, out_ref, stats_ref):
    b = pl.program_id(0)
    rows_b = pl.num_programs(0)
    _, steps, width = q_ref.shape
    head_dim = k_ref.shape[2]
    kv_heads = nk_ref.shape[1] // steps
    heads = width // head_dim
    rows = heads * steps
    columns = k_ref.shape[1]
    block_len = columns // kv_heads
    scaling = 1.0 / math.sqrt(head_dim)
    tp = lax.axis_index("tp")

    def own_head(count):
        row = lax.broadcasted_iota(jnp.int32, (rows, count), 0)
        column = lax.broadcasted_iota(jnp.int32, (rows, count), 1)
        same = (column % kv_heads) == (row // (rows // kv_heads))
        return row, column // kv_heads, same

    _, position, same = own_head(columns)
    visible = same & (position < len_ref[b] - tp * block_len)
    row, fresh_at, same = own_head(nk_ref.shape[1])
    fresh_visible = same & (fresh_at <= row % steps) & (tp == 0)
    wide = q_ref[0].astype(F32)
    q = stacked([wide[:, h * head_dim : (h + 1) * head_dim] for h in range(heads)]).astype(BF16)
    scores = jnp.where(visible, dot_rows(q, k_ref[0]) * scaling, MASKED)
    fresh = jnp.where(fresh_visible, dot_rows(q, nk_ref[0]) * scaling, MASKED)
    top = jnp.maximum(scores.max(1, keepdims=True), fresh.max(1, keepdims=True))
    shift = top.astype(BF16).astype(F32)
    weights = jnp.where(visible, jnp.exp(scores - shift), 0.0)
    fresh_weights = jnp.where(fresh_visible, jnp.exp(fresh - shift), 0.0)
    total = weights.sum(1, keepdims=True) + fresh_weights.sum(1, keepdims=True)
    numerator = jnp.dot(weights.astype(BF16), v_ref[0], preferred_element_type=F32)
    numerator += jnp.dot(fresh_weights.astype(BF16), nv_ref[0], preferred_element_type=F32)
    out_ref[:, b] = numerator.astype(BF16).reshape(-1, 8, head_dim)
    high = total.astype(BF16).astype(F32)
    lane = lax.broadcasted_iota(jnp.int32, (rows, head_dim), 1)
    stats = jnp.where(b == 0, jnp.zeros((rows, head_dim), F32), stats_ref[...])
    stats = jnp.where(lane == 3 * b, shift, stats)
    stats = jnp.where(lane == 3 * b + 1, high, stats)
    stats = jnp.where(lane == 3 * b + 2, total - high, stats)
    stats_ref[...] = stats
    out_ref[:, rows_b] = stats.astype(BF16).reshape(-1, 8, head_dim)


def attend(queries, new_keys, new_values, keys, values, lengths, outs):
    def of_row(a):
        return pl.BlockSpec((1, *a.shape[1:]), lambda b: (b, 0, 0))

    return pl.pallas_call(
        attend_kernel,
        grid=(queries.shape[0],),
        out_shape=outs,
        in_specs=[
            pl.BlockSpec(memory_space=pltpu.SMEM),
            *(of_row(a) for a in (queries, new_keys, new_values, keys, values)),
        ],
        out_specs=pl.BlockSpec(outs.shape, lambda b: (0, 0, 0, 0)),
        scratch_shapes=[pltpu.VMEM((outs.shape[0] * outs.shape[2], outs.shape[3]), F32)],
        compiler_params=pltpu.CompilerParams(vmem_limit_bytes=60 * 1024 * 1024),
        cost_estimate=pl.CostEstimate(
            flops=300_000_000, bytes_accessed=2 * keys.size * 2, transcendentals=600_000
        ),
    )(lengths, queries, new_keys, new_values, keys, values)


def combine_kernel(parts_ref, out_ref):
    rows_b = parts_ref.shape[1] - 1
    half = parts_ref.shape[2] // 2
    stats = parts_ref[:, rows_b].astype(F32)
    first, second = [], []
    for b in range(rows_b):
        shift, high, low = (stats[:, :, 3 * b + i : 3 * b + i + 1] for i in range(3))
        scale = jnp.exp(shift - shift.max(0, keepdims=True))
        total = jnp.sum(scale * (high + low), axis=0)
        numerator = jnp.sum(scale * parts_ref[:, b].astype(F32), axis=0)
        attended = numerator / total
        first.append(attended[:half])
        second.append(attended[half:])
    attended = stacked([stacked(first), stacked(second)], 1).astype(BF16)
    for i in range(out_ref.shape[0]):
        out_ref[i] = attended


def project_kernel(x_ref, w_ref, out_ref):
    x = x_ref[...].reshape(-1, x_ref.shape[2])
    for j in range(w_ref.shape[0]):
        part = jnp.dot(x, w_ref[j], preferred_element_type=F32).astype(BF16)
        out_ref[:, :, j * 128 : (j + 1) * 128] = part.reshape(*out_ref.shape[:2], 128)


def sum_kernel(parts_ref, out_ref):
    out_ref[...] = jnp.sum(parts_ref[...].astype(F32), axis=0).astype(BF16)


def hidden_kernel(summed_ref, stream_ref, hidden_ref, squares_ref):
    stream = stacked([stream_ref[b].astype(F32) for b in range(stream_ref.shape[0])])
    hidden = stream + summed_ref[...].astype(F32)
    hidden_ref[...] = hidden
    squares = hidden * hidden
    squares = sum(squares[:, j : j + 128] for j in range(0, squares.shape[1], 128))
    for i in range(squares_ref.shape[0]):
        squares_ref[i] = squares


def norm_kernel(squares_ref, hidden_ref, gain_ref, stream_ref, normed_ref):
    squares = jnp.sum(jnp.sum(squares_ref[...], axis=0), axis=1, keepdims=True)
    hidden = hidden_ref[...]
    normed = hidden * lax.rsqrt(squares / D + 1e-06) * gain_ref[...].astype(F32)
    rows_b, steps, _ = stream_ref.shape
    for b in range(rows_b):
        stream_ref[b] = hidden[b * steps : (b + 1) * steps].astype(BF16)
        normed_ref[b] = normed[b * steps : (b + 1) * steps].astype(BF16)


def call(kernel, outs, *args, flops=0):
    single = not isinstance(outs, list)
    size = sum(a.size * a.dtype.itemsize for a in args)
    vmem = pl.BlockSpec(memory_space=pltpu.VMEM)
    return pl.pallas_call(
        kernel,
        out_shape=outs,
        in_specs=[vmem] * len(args),
        out_specs=vmem if single else [vmem] * len(outs),
        compiler_params=pltpu.CompilerParams(vmem_limit_bytes=32 * 1024 * 1024),
        cost_estimate=pl.CostEstimate(flops=flops, bytes_accessed=size, transcendentals=0),
    )(*args)


def on_device(
    stream_in, queries, new_keys, new_values, key_cache, value_cache, lengths, out_weight, norm_gain
):
    rows_b, steps, width = queries.shape
    kv_heads, head_dim = key_cache.shape[2:]
    n_tp, n_far = lax.axis_size("tp"), lax.axis_size(FAR)
    n_near = lax.axis_size(NEAR)
    n_devices = n_far * n_near * n_tp
    rows = rows_b * steps
    columns = stream_in.shape[2]
    share = width // n_tp

    with jax.named_scope("weights"):
        weight = exchanged(jnp.broadcast_to(out_weight, (n_near, *out_weight.shape)), NEAR)

    with jax.named_scope("attention"):
        flat = lambda a: a.reshape(rows_b, -1, head_dim)
        parts = attend(
            queries, flat(new_keys), flat(new_values), flat(key_cache), flat(value_cache), lengths,
            jax.ShapeDtypeStruct((n_tp, rows_b + 1, 8, head_dim), BF16),
        )
        parts, weight = lax.optimization_barrier((parts, weight))
        parts = exchanged(parts, "tp")
        attended = call(combine_kernel, jax.ShapeDtypeStruct((n_far, rows, share), BF16), parts)
        attended = exchanged(attended, FAR)

    with jax.named_scope("projection"):
        projected = call(
            project_kernel, jax.ShapeDtypeStruct((n_far, rows, columns), BF16), attended, weight,
            flops=2 * n_far * rows * share * columns,
        )
        partials = exchanged(projected, "tp")
        summed = call(sum_kernel, jax.ShapeDtypeStruct((rows, columns), BF16), partials)

        def home(i):
            far, near, p = i // (n_near * n_tp), i // n_tp % n_near, i % n_tp
            return (p * n_near + near) * n_tp + far

        summed = permuted(summed, (*REP, "tp"), n_devices, home)

    with jax.named_scope("norm"):
        hidden, squares = call(
            hidden_kernel,
            [
                jax.ShapeDtypeStruct((rows, columns), F32),
                jax.ShapeDtypeStruct((n_tp, rows, 128), F32),
            ],
            summed, stream_in,
        )
        squares = exchanged(squares, "tp")
        out = jax.ShapeDtypeStruct(stream_in.shape, BF16)
        return tuple(call(norm_kernel, [out, out], squares, hidden, norm_gain.reshape(1, -1)))


def solution(mesh):
    finer = Mesh(mesh.devices.reshape(4, 4, 4, mesh.shape["tp"]), (*REP, "tp"))
    in_specs = (
        P(REP, None, "tp"),
        P(REP, None, None),
        P(REP, None, None, None),
        P(REP, None, None, None),
        P(REP, "tp", None, None),
        P(REP, "tp", None, None),
        P(REP),
        P("tp", REP),
        P("tp"),
    )
    out_specs = (P(REP, None, "tp"), P(REP, None, "tp"))
    return jax.shard_map(
        on_device, mesh=finer, in_specs=in_specs, out_specs=out_specs, check_vma=False
    )
```

time: 188 us -> 133 us (0.71)
  blocking collectives: 161 us -> 81.6 us
  starting transfers between devices: 4.37 us -> 32.6 us
  Pallas kernels: 0 us -> 6.87 us
  local copies, waits for them, and re-layouts: 7.72 us -> 1.58 us
  matrix products: 3.33 us -> 0 us
  other arithmetic: 2.94 us -> 0 us
  waiting for transfers between devices: 6.97 us -> 9.04 us
    all_gather x2 -> x0, blocking collectives: 51.6 us -> none  [whole_of(): shard = lax.all_gather(shard, axis, axis=dim, tiled=True)]
    all_to_all x4 -> x3, blocking collectives: 109 us -> 81.6 us  [exchanged(): return lax.all_to_all(pieces, axes, split_axis=0, concat_axis=0, tiled=True)]
    all_to_all x1 -> x2, starting transfers between devices: 4.37 us -> 26.4 us  [exchanged(): return lax.all_to_all(pieces, axes, split_axis=0, concat_axis=0, tiled=True)]
    pallas_call x0 -> x6, Pallas kernels: none -> 6.87 us  [the longest x1 4.91 us: attend(): pl.pallas_call(attend_kernel, grid=(queries.shape[0],), out_shape=outs, i...]
    ppermute x0 -> x1, starting transfers between devices: none -> 6.19 us  [permuted(): return lax.ppermute(array, axes, [(i, target(i)) for i in range(count)])]
    dot_general x5 -> x0, matrix products: 3.33 us -> none  [the longest x1 1.77 us: on_device(): jnp.einsum('bsgjd,bpgd->bsgjp', grouped, key_cache, preferred_element_typ...]
    unnamed x17 -> x4, local copies, waits for them, and re-layouts: 3.12 us -> 0.01 us
    all_to_all x1 -> x2, waiting for transfers between devices: 6.97 us -> 7.63 us  [exchanged(): return lax.all_to_all(pieces, axes, split_axis=0, concat_axis=0, tiled=True)]
  transfers between devices with their start and end apart: 1 -> 3, of which waited for: 1 -> 2; matrix products, arithmetic and copies ran while one was open for 0% -> 0% of each run, Pallas kernels for 0% -> 4%
where the time goes in v1:
time: 133 us; the launch traced here: 132 us
  blocking collectives  81.6 us (61%)
  starting transfers between devices  32.6 us (25%)
  waiting for transfers between devices  9.04 us (7%)
  Pallas kernels  6.87 us (5%)
  local copies, waits for them, and re-layouts  1.58 us (1%)
    all_to_all x3, blocking collectives, exchanged(): return lax.all_to_all(pieces, axes, split_axis=0, concat_axis=0, tiled=True)  81.6 us
    all_to_all x2, starting transfers between devices, exchanged(): return lax.all_to_all(pieces, axes, split_axis=0, concat_axis=0, tiled=True)  26.4 us
    all_to_all x2, waiting for transfers between devices, exchanged(): return lax.all_to_all(pieces, axes, split_axis=0, concat_axis=0, tiled=True)  7.63 us
    ppermute x1, starting transfers between devices, permuted(): return lax.ppermute(array, axes, [(i, target(i)) for i in range(count)])  6.19 us
    pallas_call x1, Pallas kernels, attend(): pl.pallas_call(attend_kernel, grid=(queries.shape[0],), out_shape=outs, i...  4.91 us
  transfers between devices with their start and end apart: 3, of which 2 were waited for; matrix products, arithmetic and copies ran while one was open for 0% of the time, Pallas kernels for 4%

profile of v1, /device:TPU:1, one launch (start us, length us, event | category | flops | bytes accessed | tf_op | source)
XLA Modules:
  0.0 132.4 jit_solution(17348955328893134164)
XLA Ops:
  0.6 1.6 %broadcast_in_dim.3 = bf16[4,256,128]{2,1,0:T(8,128)(2,1)} broadcast(bf16[256,128]{1,0:T(8,128)(2,1)} %param.16), dimensions={1,2} | broadcast | bytes 327680 | tf_op jit(solution)/shard_map/weights/broadcast_in_dim | solution.py:177
  2.2 4.7 %all-to-all-start = ((bf16[4,256,128]{2,1,0:T(8,128)(2,1)}), bf16[4,256,128]{2,1,0:T(8,128)(2,1)S(1)}, u32[]{:S(2)}, u32[]{:S(2)}) async-start(bf16[4,256,128]{2,1,0:T(8,128)(2,1)} %broadcast_in_dim.3), calls=%async_computation | async-start | bytes 524288 | tf_op jit(solution)/shard_map/weights/all_to_all | solution.py:20
  6.9 4.9 %attention.2 = bf16[16,5,8,128]{3,2,1,0:T(8,128)(2,1)} custom-call(s32[4]{0:T(128)} %len_ref.1, bf16[4,4,4096]{2,1,0:T(4,128)(2,1)} %q_ref.1, bf16[4,16,128]{2,1,0:T(8,128)(2,1)} %bitcast.6, bf16[4,16,128]{2,1,0:T(8,128)(2,1)} %bitcast.7, bf16[4,1024,128]{2,1,0:T(8,128)(2,1)} %bitcast.4, bf16[4,1024,128]{2,1,0:T(8,128)(2,1)} %bitcast.5), custom_call_target="tpu_custom_call" | custom-call | flops 300000000 | bytes 2097152 | tf_op jit(solution)/shard_map/attention/pallas_call | solution.py:84
  11.8 0.0 all-to-all-done.w_ref
  11.8 24.6 %all_to_all.25.parts_ref = bf16[16,5,8,128]{3,2,1,0:T(8,128)(2,1)S(1)} all-to-all(bf16[16,5,8,128]{3,2,1,0:T(8,128)(2,1)} %attention.2), channel_id=1, replica_groups=mesh['ra'=4,'rb'=4,'rc'=4,'tp'=16] {'tp'}, dimensions={0} | all-to-all | bytes 327680 | tf_op jit(solution)/shard_map/attention/all_to_all | solution.py:20
  36.4 0.3 attention.3
  36.7 41.4 %all_to_all.26.x_ref = bf16[16,16,256]{2,1,0:T(8,128)(2,1)S(1)} all-to-all(bf16[16,16,256]{2,1,0:T(8,128)(2,1)S(1)} %attention.3), channel_id=1, replica_groups=mesh['ra'=4,'rb'=4,'rc'=4,'tp'=16] {'ra','rb'}, dimensions={0} | all-to-all | bytes 262144 | tf_op jit(solution)/shard_map/attention/all_to_all | solution.py:20
  78.1 0.3 projection.2
  78.4 15.6 %all_to_all.27.parts_ref = bf16[16,16,512]{2,1,0:T(8,128)(2,1)S(1)} all-to-all(bf16[16,16,512]{2,1,0:T(8,128)(2,1)S(1)} %projection.2), channel_id=1, replica_groups=mesh['ra'=4,'rb'=4,'rc'=4,'tp'=16] {'tp'}, dimensions={0} | all-to-all | bytes 524288 | tf_op jit(solution)/shard_map/projection/all_to_all | solution.py:20
  94.0 0.0 copy-start
  94.0 6.2 %collective-permute-start = (bf16[16,512]{1,0:T(8,128)(2,1)S(1)}, bf16[16,512]{1,0:T(8,128)(2,1)S(1)}, u32[]{:S(2)}, u32[]{:S(2)}) collective-permute-start(bf16[16,512]{1,0:T(8,128)(2,1)S(1)} %projection.3), channel_id=1, source_target_pairs={{0,0},{1,64},{2,128},{3,192},{4,256},{5,320},{6,384},{7,448},{8,51... | collective-permute-start | bytes 49160 | tf_op jit(solution)/shard_map/projection/ppermute | solution.py:24
  100.2 1.4 %collective-permute-done.summed_ref = bf16[16,512]{1,0:T(8,128)(2,1)S(1)} collective-permute-done((bf16[16,512]{1,0:T(8,128)(2,1)S(1)}, bf16[16,512]{1,0:T(8,128)(2,1)S(1)}, u32[]{:S(2)}, u32[]{:S(2)}) %collective-permute-start) | collective-permute-done | bytes 16416 | tf_op jit(solution)/shard_map/projection/ppermute | solution.py:24
  101.6 0.0 copy-done
  101.6 0.7 norm.2
  102.3 0.0 copy-start.1
  102.3 21.8 %all-to-all-start.4 = ((f32[16,16,128]{2,1,0:T(8,128)}), f32[16,16,128]{2,1,0:T(8,128)S(1)}, u32[]{:S(2)}, u32[]{:S(2)}) async-start(f32[16,16,128]{2,1,0:T(8,128)} %get-tuple-element.8), calls=%async_computation.4 | async-start | bytes 262144 | tf_op jit(solution)/shard_map/norm/all_to_all | solution.py:20
  124.1 0.0 copy-done.1
  124.1 7.6 %all-to-all-done.4.squares_ref = f32[16,16,128]{2,1,0:T(8,128)S(1)} async-done(((f32[16,16,128]{2,1,0:T(8,128)}), f32[16,16,128]{2,1,0:T(8,128)S(1)}, u32[]{:S(2)}, u32[]{:S(2)}) %all-to-all-start.4) | async-done | bytes 131104 | tf_op jit(solution)/shard_map/norm/all_to_all | solution.py:20
  131.7 0.7 norm.3
  (2 shorter events, 0.0 us)
Async XLA Ops:
  2.2 9.6 %all-to-all-start = ((bf16[4,256,128]{2,1,0:T(8,128)(2,1)}), bf16[4,256,128]{2,1,0:T(8,128)(2,1)S(1)}, u32[]{:S(2)}, u32[]{:S(2)}) async-start(bf16[4,256,128]{2,1,0:T(8,128)(2,1)} %broadcast_in_dim.3), calls=%async_computation | async-start | bytes 524288 | tf_op jit(solution)/shard_map/weights/all_to_all | solution.py:20
  94.0 7.7 %copy-start = (bf16[4,4,512]{2,1,0:T(4,128)(2,1)S(1)}, bf16[4,4,512]{2,1,0:T(4,128)(2,1)}, u32[]{:S(2)}) copy-start(bf16[4,4,512]{2,1,0:T(4,128)(2,1)} %stream_ref.1) | copy-start | bytes 49156
  94.0 7.6 %collective-permute-start = (bf16[16,512]{1,0:T(8,128)(2,1)S(1)}, bf16[16,512]{1,0:T(8,128)(2,1)S(1)}, u32[]{:S(2)}, u32[]{:S(2)}) collective-permute-start(bf16[16,512]{1,0:T(8,128)(2,1)S(1)} %projection.3), channel_id=1, source_target_pairs={{0,0},{1,64},{2,128},{3,192},{4,256},{5,320},{6,384},{7,448},{8,51... | collective-permute-start | bytes 49160 | tf_op jit(solution)/shard_map/projection/ppermute | solution.py:24
  102.3 21.8 %copy-start.1 = (bf16[512]{0:T(512)(128)(2,1)S(1)}, bf16[512]{0:T(512)(128)(2,1)}, u32[]{:S(2)}) copy-start(bf16[512]{0:T(512)(128)(2,1)} %param.17) | copy-start | bytes 3076
  102.3 29.4 %all-to-all-start.4 = ((f32[16,16,128]{2,1,0:T(8,128)}), f32[16,16,128]{2,1,0:T(8,128)S(1)}, u32[]{:S(2)}, u32[]{:S(2)}) async-start(f32[16,16,128]{2,1,0:T(8,128)} %get-tuple-element.8), calls=%async_computation.4 | async-start | bytes 262144 | tf_op jit(solution)/shard_map/norm/all_to_all | solution.py:20

commit v2 on v1

--- a/solution.py
+++ b/solution.py
@@ -10,9 +10,10 @@
 
 D = 8192
 REP = ("ra", "rb", "rc")
-FAR = ("ra", "rb")
-NEAR = "rc"
+ARC = ("rb", "rc")
+QUAD = "rc"
 MASKED = -1e30
+NONE_VISIBLE = -1e29
 F32, BF16 = jnp.float32, jnp.bfloat16
 
 
@@ -42,7 +43,7 @@
     rows = heads * steps
     columns = k_ref.shape[1]
     block_len = columns // kv_heads
-    scaling = 1.0 / math.sqrt(head_dim)
+    to_log2 = math.log2(math.e) / math.sqrt(head_dim)
     tp = lax.axis_index("tp")
 
     def own_head(count):
@@ -50,6 +51,9 @@
         column = lax.broadcasted_iota(jnp.int32, (rows, count), 1)
         same = (column % kv_heads) == (row // (rows // kv_heads))
         return row, column // kv_heads, same
+
+    def masked(key_ref, visible):
+        return jnp.where(visible, dot_rows(q, key_ref[0]) * to_log2, MASKED)
 
     _, position, same = own_head(columns)
     visible = same & (position < len_ref[b] - tp * block_len)
@@ -57,12 +61,10 @@
     fresh_visible = same & (fresh_at <= row % steps) & (tp == 0)
     wide = q_ref[0].astype(F32)
     q = stacked([wide[:, h * head_dim : (h + 1) * head_dim] for h in range(heads)]).astype(BF16)
-    scores = jnp.where(visible, dot_rows(q, k_ref[0]) * scaling, MASKED)
-    fresh = jnp.where(fresh_visible, dot_rows(q, nk_ref[0]) * scaling, MASKED)
+    scores, fresh = masked(k_ref, visible), masked(nk_ref, fresh_visible)
     top = jnp.maximum(scores.max(1, keepdims=True), fresh.max(1, keepdims=True))
-    shift = top.astype(BF16).astype(F32)
-    weights = jnp.where(visible, jnp.exp(scores - shift), 0.0)
-    fresh_weights = jnp.where(fresh_visible, jnp.exp(fresh - shift), 0.0)
+    shift = jnp.maximum(top, NONE_VISIBLE).astype(BF16).astype(F32)
+    weights, fresh_weights = jnp.exp2(scores - shift), jnp.exp2(fresh - shift)
     total = weights.sum(1, keepdims=True) + fresh_weights.sum(1, keepdims=True)
     numerator = jnp.dot(weights.astype(BF16), v_ref[0], preferred_element_type=F32)
     numerator += jnp.dot(fresh_weights.astype(BF16), nv_ref[0], preferred_element_type=F32)
@@ -105,7 +107,7 @@
     first, second = [], []
     for b in range(rows_b):
         shift, high, low = (stats[:, :, 3 * b + i : 3 * b + i + 1] for i in range(3))
-        scale = jnp.exp(shift - shift.max(0, keepdims=True))
+        scale = jnp.exp2(shift - shift.max(0, keepdims=True))
         total = jnp.sum(scale * (high + low), axis=0)
         numerator = jnp.sum(scale * parts_ref[:, b].astype(F32), axis=0)
         attended = numerator / total
@@ -116,11 +118,15 @@
         out_ref[i] = attended
 
 
+def side_by_side_kernel(blocks_ref, out_ref):
+    for j in range(blocks_ref.shape[0]):
+        out_ref[:, j * 128 : (j + 1) * 128] = blocks_ref[j]
+
+
 def project_kernel(x_ref, w_ref, out_ref):
     x = x_ref[...].reshape(-1, x_ref.shape[2])
-    for j in range(w_ref.shape[0]):
-        part = jnp.dot(x, w_ref[j], preferred_element_type=F32).astype(BF16)
-        out_ref[:, :, j * 128 : (j + 1) * 128] = part.reshape(*out_ref.shape[:2], 128)
+    projected = jnp.dot(x, w_ref[...], preferred_element_type=F32)
+    out_ref[...] = projected.astype(BF16).reshape(out_ref.shape)
 
 
 def sum_kernel(parts_ref, out_ref):
@@ -166,15 +172,15 @@
 ):
     rows_b, steps, width = queries.shape
     kv_heads, head_dim = key_cache.shape[2:]
-    n_tp, n_far = lax.axis_size("tp"), lax.axis_size(FAR)
-    n_near = lax.axis_size(NEAR)
-    n_devices = n_far * n_near * n_tp
+    n_tp, n_arc = lax.axis_size("tp"), lax.axis_size(ARC)
+    n_quad = lax.axis_size(QUAD)
+    n_rep = n_arc * lax.axis_size("ra")
     rows = rows_b * steps
     columns = stream_in.shape[2]
     share = width // n_tp
 
     with jax.named_scope("weights"):
-        weight = exchanged(jnp.broadcast_to(out_weight, (n_near, *out_weight.shape)), NEAR)
+        quad = exchanged(jnp.broadcast_to(out_weight, (n_quad, *out_weight.shape)), QUAD)
 
     with jax.named_scope("attention"):
         flat = lambda a: a.reshape(rows_b, -1, head_dim)
@@ -182,24 +188,28 @@
             queries, flat(new_keys), flat(new_values), flat(key_cache), flat(value_cache), lengths,
             jax.ShapeDtypeStruct((n_tp, rows_b + 1, 8, head_dim), BF16),
         )
-        parts, weight = lax.optimization_barrier((parts, weight))
+        parts, quad = lax.optimization_barrier((parts, quad))
+        weight = permuted(quad, REP, n_rep, lambda r: (r % n_quad) * n_arc + r // n_quad)
+        weight = call(
+            side_by_side_kernel, jax.ShapeDtypeStruct((share, columns), BF16), weight, flops=20_000_000_000
+        )
         parts = exchanged(parts, "tp")
-        attended = call(combine_kernel, jax.ShapeDtypeStruct((n_far, rows, share), BF16), parts)
-        attended = exchanged(attended, FAR)
+        attended = call(combine_kernel, jax.ShapeDtypeStruct((n_arc, rows, share), BF16), parts)
+        attended = exchanged(attended, ARC)
 
     with jax.named_scope("projection"):
         projected = call(
-            project_kernel, jax.ShapeDtypeStruct((n_far, rows, columns), BF16), attended, weight,
-            flops=2 * n_far * rows * share * columns,
+            project_kernel, jax.ShapeDtypeStruct((n_arc, rows, columns), BF16), attended, weight,
+            flops=2 * n_arc * rows * share * columns,
         )
         partials = exchanged(projected, "tp")
         summed = call(sum_kernel, jax.ShapeDtypeStruct((rows, columns), BF16), partials)
 
         def home(i):
-            far, near, p = i // (n_near * n_tp), i // n_tp % n_near, i % n_tp
-            return (p * n_near + near) * n_tp + far
-
-        summed = permuted(summed, (*REP, "tp"), n_devices, home)
+            r, p = i // n_tp, i % n_tp
+            return (r // n_arc * n_arc + p) * n_tp + r % n_arc
+
+        summed = permuted(summed, (*REP, "tp"), n_rep * n_tp, home)
 
     with jax.named_scope("norm"):
         hidden, squares = call(

time: 133 us -> 124 us (0.932)
  the two profiles are of different devices: /device:TPU:1 before, /device:TPU:257 now
where the time goes in v2:
time: 124 us; the launch traced here: 123 us
  starting transfers between devices  54.7 us (44%)
  blocking collectives  32.9 us (27%)
  waiting for transfers between devices  26.1 us (21%)
  Pallas kernels  7.33 us (6%)
  local copies, waits for them, and re-layouts  1.6 us (1%)
    all_to_all x3, starting transfers between devices, exchanged(): return lax.all_to_all(pieces, axes, split_axis=0, concat_axis=0, tiled=True)  50.9 us
    all_to_all x2, blocking collectives, exchanged(): return lax.all_to_all(pieces, axes, split_axis=0, concat_axis=0, tiled=True)  32.9 us
    all_to_all x3, waiting for transfers between devices, exchanged(): return lax.all_to_all(pieces, axes, split_axis=0, concat_axis=0, tiled=True)  23 us
    pallas_call x1, Pallas kernels, attend(): pl.pallas_call(attend_kernel, grid=(queries.shape[0],), out_shape=outs, i...  4.75 us
    ppermute x2, starting transfers between devices, permuted(): return lax.ppermute(array, axes, [(i, target(i)) for i in range(count)])  3.83 us
    ppermute x2, waiting for transfers between devices, permuted(): return lax.ppermute(array, axes, [(i, target(i)) for i in range(count)])  3.13 us
    pallas_call x6, Pallas kernels, call(): pl.pallas_call(kernel, out_shape=outs, in_specs=[vmem] * len(args), out_s...  2.59 us
  transfers between devices with their start and end apart: 5, of which 3 were waited for; matrix products, arithmetic and copies ran while one was open for 0% of the time, Pallas kernels for 5%

profile of v2, /device:TPU:257, one launch (start us, length us, event | category | flops | bytes accessed | tf_op | source)
XLA Modules:
  0.0 123.3 jit_solution(17606333366576499773)
XLA Ops:
  0.6 1.6 %broadcast_in_dim.3 = bf16[4,256,128]{2,1,0:T(8,128)(2,1)} broadcast(bf16[256,128]{1,0:T(8,128)(2,1)} %param.16), dimensions={1,2} | broadcast | bytes 327680 | tf_op jit(solution)/shard_map/weights/broadcast_in_dim | solution.py:183
  2.2 3.8 %all-to-all-start = ((bf16[4,256,128]{2,1,0:T(8,128)(2,1)}), bf16[4,256,128]{2,1,0:T(8,128)(2,1)S(1)}, u32[]{:S(2)}, u32[]{:S(2)}) async-start(bf16[4,256,128]{2,1,0:T(8,128)(2,1)} %broadcast_in_dim.3), calls=%async_computation | async-start | bytes 524288 | tf_op jit(solution)/shard_map/weights/all_to_all | solution.py:21
  6.0 4.7 %attention.3 = bf16[16,5,8,128]{3,2,1,0:T(8,128)(2,1)} custom-call(s32[4]{0:T(128)} %len_ref.1, bf16[4,4,4096]{2,1,0:T(4,128)(2,1)} %q_ref.1, bf16[4,16,128]{2,1,0:T(8,128)(2,1)} %bitcast.6, bf16[4,16,128]{2,1,0:T(8,128)(2,1)} %bitcast.7, bf16[4,1024,128]{2,1,0:T(8,128)(2,1)} %bitcast.4, bf16[4,1024,128]{2,1,0:T(8,128)(2,1)} %bitcast.5), custom_call_target="tpu_custom_call" | custom-call | flops 300000000 | bytes 2097152 | tf_op jit(solution)/shard_map/attention/pallas_call | solution.py:86
  10.8 0.0 all-to-all-done
  10.8 1.9 %collective-permute-start = (bf16[4,256,128]{2,1,0:T(8,128)(2,1)S(1)}, bf16[4,256,128]{2,1,0:T(8,128)(2,1)S(1)}, u32[]{:S(2)}, u32[]{:S(2)}) collective-permute-start(bf16[4,256,128]{2,1,0:T(8,128)(2,1)S(1)} %all-to-all-done), channel_id=1, source_target_pairs={{0,0},{16,256},{32,512},{48,768},{64,16},{80,272},{96,528},{112,78... | collective-permute-start | bytes 786440 | tf_op jit(solution)/shard_map/attention/ppermute | solution.py:25
  12.7 16.4 %all_to_all.25.parts_ref = bf16[16,5,8,128]{3,2,1,0:T(8,128)(2,1)S(1)} all-to-all(bf16[16,5,8,128]{3,2,1,0:T(8,128)(2,1)} %attention.3), channel_id=1, replica_groups=mesh['ra'=4,'rb'=4,'rc'=4,'tp'=16] {'tp'}, dimensions={0} | all-to-all | bytes 327680 | tf_op jit(solution)/shard_map/attention/all_to_all | solution.py:21
  29.1 0.9 attention.4
  30.0 20.8 %all-to-all-start.2 = ((bf16[16,16,256]{2,1,0:T(8,128)(2,1)}), bf16[16,16,256]{2,1,0:T(8,128)(2,1)S(1)}, u32[]{:S(2)}, u32[]{:S(2)}) async-start(bf16[16,16,256]{2,1,0:T(8,128)(2,1)} %attention.4), calls=%async_computation.2 | async-start | bytes 262144 | tf_op jit(solution)/shard_map/attention/all_to_all | solution.py:21
  50.8 0.0 collective-permute-done.blocks_ref
  50.9 15.4 %all-to-all-done.2.x_ref = bf16[16,16,256]{2,1,0:T(8,128)(2,1)S(1)} async-done(((bf16[16,16,256]{2,1,0:T(8,128)(2,1)}), bf16[16,16,256]{2,1,0:T(8,128)(2,1)S(1)}, u32[]{:S(2)}, u32[]{:S(2)}) %all-to-all-start.2) | async-done | bytes 131104 | tf_op jit(solution)/shard_map/attention/all_to_all | solution.py:21
  66.2 0.2 projection.2
  66.5 16.5 %all_to_all.26.parts_ref = bf16[16,16,512]{2,1,0:T(8,128)(2,1)S(1)} all-to-all(bf16[16,16,512]{2,1,0:T(8,128)(2,1)S(1)} %projection.2), channel_id=1, replica_groups=mesh['ra'=4,'rb'=4,'rc'=4,'tp'=16] {'tp'}, dimensions={0} | all-to-all | bytes 524288 | tf_op jit(solution)/shard_map/projection/all_to_all | solution.py:21
  83.0 0.0 copy-start
  83.0 1.9 %collective-permute-start.1 = (bf16[16,512]{1,0:T(8,128)(2,1)S(1)}, bf16[16,512]{1,0:T(8,128)(2,1)S(1)}, u32[]{:S(2)}, u32[]{:S(2)}) collective-permute-start(bf16[16,512]{1,0:T(8,128)(2,1)S(1)} %projection.3), channel_id=1, source_target_pairs={{0,0},{1,16},{2,32},{3,48},{4,64},{5,80},{6,96},{7,112},{8,128},{9... | collective-permute-start | bytes 49160 | tf_op jit(solution)/shard_map/projection/ppermute | solution.py:25
  84.9 3.1 %collective-permute-done.1.summed_ref = bf16[16,512]{1,0:T(8,128)(2,1)S(1)} collective-permute-done((bf16[16,512]{1,0:T(8,128)(2,1)S(1)}, bf16[16,512]{1,0:T(8,128)(2,1)S(1)}, u32[]{:S(2)}, u32[]{:S(2)}) %collective-permute-start.1) | collective-permute-done | bytes 16416 | tf_op jit(solution)/shard_map/projection/ppermute | solution.py:25
  88.1 0.0 copy-done
  88.1 0.7 norm.2
  88.7 0.0 copy-start.1
  88.7 26.2 %all-to-all-start.4 = ((f32[16,16,128]{2,1,0:T(8,128)}), f32[16,16,128]{2,1,0:T(8,128)S(1)}, u32[]{:S(2)}, u32[]{:S(2)}) async-start(f32[16,16,128]{2,1,0:T(8,128)} %get-tuple-element.8), calls=%async_computation.4 | async-start | bytes 262144 | tf_op jit(solution)/shard_map/norm/all_to_all | solution.py:21
  115.0 0.0 copy-done.1
  115.0 7.6 %all-to-all-done.4.squares_ref = f32[16,16,128]{2,1,0:T(8,128)S(1)} async-done(((f32[16,16,128]{2,1,0:T(8,128)}), f32[16,16,128]{2,1,0:T(8,128)S(1)}, u32[]{:S(2)}, u32[]{:S(2)}) %all-to-all-start.4) | async-done | bytes 131104 | tf_op jit(solution)/shard_map/norm/all_to_all | solution.py:21
  122.6 0.7 norm.3
  (3 shorter events, 0.1 us)
Async XLA Ops:
  2.2 8.6 %all-to-all-start = ((bf16[4,256,128]{2,1,0:T(8,128)(2,1)}), bf16[4,256,128]{2,1,0:T(8,128)(2,1)S(1)}, u32[]{:S(2)}, u32[]{:S(2)}) async-start(bf16[4,256,128]{2,1,0:T(8,128)(2,1)} %broadcast_in_dim.3), calls=%async_computation | async-start | bytes 524288 | tf_op jit(solution)/shard_map/weights/all_to_all | solution.py:21
  10.8 40.0 %collective-permute-start = (bf16[4,256,128]{2,1,0:T(8,128)(2,1)S(1)}, bf16[4,256,128]{2,1,0:T(8,128)(2,1)S(1)}, u32[]{:S(2)}, u32[]{:S(2)}) collective-permute-start(bf16[4,256,128]{2,1,0:T(8,128)(2,1)S(1)} %all-to-all-done), channel_id=1, source_target_pairs={{0,0},{16,256},{32,512},{48,768},{64,16},{80,272},{96,528},{112,78... | collective-permute-start | bytes 786440 | tf_op jit(solution)/shard_map/attention/ppermute | solution.py:25
  30.0 36.2 %all-to-all-start.2 = ((bf16[16,16,256]{2,1,0:T(8,128)(2,1)}), bf16[16,16,256]{2,1,0:T(8,128)(2,1)S(1)}, u32[]{:S(2)}, u32[]{:S(2)}) async-start(bf16[16,16,256]{2,1,0:T(8,128)(2,1)} %attention.4), calls=%async_computation.2 | async-start | bytes 262144 | tf_op jit(solution)/shard_map/attention/all_to_all | solution.py:21
  83.0 5.1 %copy-start = (bf16[4,4,512]{2,1,0:T(4,128)(2,1)S(1)}, bf16[4,4,512]{2,1,0:T(4,128)(2,1)}, u32[]{:S(2)}) copy-start(bf16[4,4,512]{2,1,0:T(4,128)(2,1)} %stream_ref.1) | copy-start | bytes 49156
  83.0 5.1 %collective-permute-start.1 = (bf16[16,512]{1,0:T(8,128)(2,1)S(1)}, bf16[16,512]{1,0:T(8,128)(2,1)S(1)}, u32[]{:S(2)}, u32[]{:S(2)}) collective-permute-start(bf16[16,512]{1,0:T(8,128)(2,1)S(1)} %projection.3), channel_id=1, source_target_pairs={{0,0},{1,16},{2,32},{3,48},{4,64},{5,80},{6,96},{7,112},{8,128},{9... | collective-permute-start | bytes 49160 | tf_op jit(solution)/shard_map/projection/ppermute | solution.py:25
  88.7 26.2 %copy-start.1 = (bf16[512]{0:T(512)(128)(2,1)S(1)}, bf16[512]{0:T(512)(128)(2,1)}, u32[]{:S(2)}) copy-start(bf16[512]{0:T(512)(128)(2,1)} %param.17) | copy-start | bytes 3076
  88.7 33.9 %all-to-all-start.4 = ((f32[16,16,128]{2,1,0:T(8,128)}), f32[16,16,128]{2,1,0:T(8,128)S(1)}, u32[]{:S(2)}, u32[]{:S(2)}) async-start(f32[16,16,128]{2,1,0:T(8,128)} %get-tuple-element.8), calls=%async_computation.4 | async-start | bytes 262144 | tf_op jit(solution)/shard_map/norm/all_to_all | solution.py:21

commit v3 on v2

--- a/solution.py
+++ b/solution.py
@@ -21,8 +21,9 @@
     return lax.all_to_all(pieces, axes, split_axis=0, concat_axis=0, tiled=True)
 
 
-def permuted(array, axes, count, target):
-    return lax.ppermute(array, axes, [(i, target(i)) for i in range(count)])
+def permuted(array, target):
+    axes = (*REP, "tp")
+    return lax.ppermute(array, axes, [(i, target(i)) for i in range(lax.axis_size(axes))])
 
 
 def dot_rows(a, b):
@@ -113,9 +114,12 @@
         attended = numerator / total
         first.append(attended[:half])
         second.append(attended[half:])
-    attended = stacked([stacked(first), stacked(second)], 1).astype(BF16)
+    out_ref[...] = stacked([stacked(first), stacked(second)], 1).astype(BF16)
+
+
+def copies_kernel(in_ref, out_ref):
     for i in range(out_ref.shape[0]):
-        out_ref[i] = attended
+        out_ref[i] = in_ref[...]
 
 
 def side_by_side_kernel(blocks_ref, out_ref):
@@ -129,13 +133,9 @@
     out_ref[...] = projected.astype(BF16).reshape(out_ref.shape)
 
 
-def sum_kernel(parts_ref, out_ref):
-    out_ref[...] = jnp.sum(parts_ref[...].astype(F32), axis=0).astype(BF16)
-
-
-def hidden_kernel(summed_ref, stream_ref, hidden_ref, squares_ref):
+def hidden_kernel(partials_ref, stream_ref, hidden_ref, squares_ref):
     stream = stacked([stream_ref[b].astype(F32) for b in range(stream_ref.shape[0])])
-    hidden = stream + summed_ref[...].astype(F32)
+    hidden = stream + jnp.sum(partials_ref[...].astype(F32), axis=0)
     hidden_ref[...] = hidden
     squares = hidden * hidden
     squares = sum(squares[:, j : j + 128] for j in range(0, squares.shape[1], 128))
@@ -174,10 +174,17 @@
     kv_heads, head_dim = key_cache.shape[2:]
     n_tp, n_arc = lax.axis_size("tp"), lax.axis_size(ARC)
     n_quad = lax.axis_size(QUAD)
-    n_rep = n_arc * lax.axis_size("ra")
     rows = rows_b * steps
     columns = stream_in.shape[2]
     share = width // n_tp
+
+    def swapped(i):
+        arc, place, p = i // (n_arc * n_tp), i // n_tp % n_arc, i % n_tp
+        return (arc * n_arc + p) * n_tp + place
+
+    def weight_home(i):
+        quad, arc, p = i // (n_quad * n_tp), i // n_tp % n_quad, i % n_tp
+        return (arc * n_arc + p) * n_tp + quad
 
     with jax.named_scope("weights"):
         quad = exchanged(jnp.broadcast_to(out_weight, (n_quad, *out_weight.shape)), QUAD)
@@ -189,27 +196,24 @@
             jax.ShapeDtypeStruct((n_tp, rows_b + 1, 8, head_dim), BF16),
         )
         parts, quad = lax.optimization_barrier((parts, quad))
-        weight = permuted(quad, REP, n_rep, lambda r: (r % n_quad) * n_arc + r // n_quad)
+        weight = permuted(quad, weight_home)
         weight = call(
             side_by_side_kernel, jax.ShapeDtypeStruct((share, columns), BF16), weight, flops=20_000_000_000
         )
         parts = exchanged(parts, "tp")
-        attended = call(combine_kernel, jax.ShapeDtypeStruct((n_arc, rows, share), BF16), parts)
-        attended = exchanged(attended, ARC)
+        attended = call(combine_kernel, jax.ShapeDtypeStruct((rows, share), BF16), parts)
+        attended = permuted(attended, swapped)
+        attended = call(
+            copies_kernel, jax.ShapeDtypeStruct((n_tp, rows, share), BF16), attended
+        )
+        attended = exchanged(attended, "tp")
 
     with jax.named_scope("projection"):
         projected = call(
             project_kernel, jax.ShapeDtypeStruct((n_arc, rows, columns), BF16), attended, weight,
             flops=2 * n_arc * rows * share * columns,
         )
-        partials = exchanged(projected, "tp")
-        summed = call(sum_kernel, jax.ShapeDtypeStruct((rows, columns), BF16), partials)
-
-        def home(i):
-            r, p = i // n_tp, i % n_tp
-            return (r // n_arc * n_arc + p) * n_tp + r % n_arc
-
-        summed = permuted(summed, (*REP, "tp"), n_rep * n_tp, home)
+        partials = exchanged(projected, ARC)
 
     with jax.named_scope("norm"):
         hidden, squares = call(
@@ -218,7 +222,7 @@
                 jax.ShapeDtypeStruct((rows, columns), F32),
                 jax.ShapeDtypeStruct((n_tp, rows, 128), F32),
             ],
-            summed, stream_in,
+            partials, stream_in,
         )
         squares = exchanged(squares, "tp")
         out = jax.ShapeDtypeStruct(stream_in.shape, BF16)

time: 124 us -> 144 us (1.16)
  the two profiles are of different devices: /device:TPU:257 before, /device:TPU:1 now
where the time goes in v3:
time: 144 us; the launch traced here: 143 us
  starting transfers between devices  86.3 us (60%)
  blocking collectives  29 us (20%)
  waiting for transfers between devices  18.3 us (13%)
  Pallas kernels  7.32 us (5%)
  local copies, waits for them, and re-layouts  1.6 us (1%)
    ppermute x2, starting transfers between devices, permuted(): lax.ppermute(array, axes, [(i, target(i)) for i in range(lax.axis_size(ax...  53.7 us
    all_to_all x3, starting transfers between devices, exchanged(): return lax.all_to_all(pieces, axes, split_axis=0, concat_axis=0, tiled=True)  32.6 us
    all_to_all x2, blocking collectives, exchanged(): return lax.all_to_all(pieces, axes, split_axis=0, concat_axis=0, tiled=True)  29 us
    all_to_all x3, waiting for transfers between devices, exchanged(): return lax.all_to_all(pieces, axes, split_axis=0, concat_axis=0, tiled=True)  15.3 us
    pallas_call x1, Pallas kernels, attend(): pl.pallas_call(attend_kernel, grid=(queries.shape[0],), out_shape=outs, i...  4.74 us
    ppermute x2, waiting for transfers between devices, permuted(): lax.ppermute(array, axes, [(i, target(i)) for i in range(lax.axis_size(ax...  3.04 us
  transfers between devices with their start and end apart: 5, of which 3 were waited for; matrix products, arithmetic and copies ran while one was open for 0% of the time, Pallas kernels for 4%

profile of v3, /device:TPU:1, one launch (start us, length us, event | category | flops | bytes accessed | tf_op | source)
XLA Modules:
  0.0 143.2 jit_solution(11820216061969491086)
XLA Ops:
  0.6 1.6 %broadcast_in_dim.3 = bf16[4,256,128]{2,1,0:T(8,128)(2,1)} broadcast(bf16[256,128]{1,0:T(8,128)(2,1)} %param.16), dimensions={1,2} | broadcast | bytes 327680 | tf_op jit(solution)/shard_map/weights/broadcast_in_dim | solution.py:190
  2.2 4.7 %all-to-all-start = ((bf16[4,256,128]{2,1,0:T(8,128)(2,1)}), bf16[4,256,128]{2,1,0:T(8,128)(2,1)S(1)}, u32[]{:S(2)}, u32[]{:S(2)}) async-start(bf16[4,256,128]{2,1,0:T(8,128)(2,1)} %broadcast_in_dim.3), calls=%async_computation | async-start | bytes 524288 | tf_op jit(solution)/shard_map/weights/all_to_all | solution.py:21
  6.9 4.7 %attention.4 = bf16[16,5,8,128]{3,2,1,0:T(8,128)(2,1)} custom-call(s32[4]{0:T(128)} %len_ref.1, bf16[4,4,4096]{2,1,0:T(4,128)(2,1)} %q_ref.1, bf16[4,16,128]{2,1,0:T(8,128)(2,1)} %bitcast.6, bf16[4,16,128]{2,1,0:T(8,128)(2,1)} %bitcast.7, bf16[4,1024,128]{2,1,0:T(8,128)(2,1)} %bitcast.4, bf16[4,1024,128]{2,1,0:T(8,128)(2,1)} %bitcast.5), custom_call_target="tpu_custom_call" | custom-call | flops 300000000 | bytes 2097152 | tf_op jit(solution)/shard_map/attention/pallas_call | solution.py:87
  11.6 0.0 all-to-all-done
  11.6 51.8 %collective-permute-start.1 = (bf16[4,256,128]{2,1,0:T(8,128)(2,1)S(1)}, bf16[4,256,128]{2,1,0:T(8,128)(2,1)S(1)}, u32[]{:S(2)}, u32[]{:S(2)}) collective-permute-start(bf16[4,256,128]{2,1,0:T(8,128)(2,1)S(1)} %all-to-all-done), channel_id=1, source_target_pairs={{0,0},{1,16},{2,32},{3,48},{4,64},{5,80},{6,96},{7,112},{8,128},{9... | collective-permute-start | bytes 786440 | tf_op jit(solution)/shard_map/attention/ppermute | solution.py:26
  63.4 12.7 %all_to_all.25.parts_ref = bf16[16,5,8,128]{3,2,1,0:T(8,128)(2,1)S(1)} all-to-all(bf16[16,5,8,128]{3,2,1,0:T(8,128)(2,1)} %attention.4), channel_id=1, replica_groups=mesh['ra'=4,'rb'=4,'rc'=4,'tp'=16] {'tp'}, dimensions={0} | all-to-all | bytes 327680 | tf_op jit(solution)/shard_map/attention/all_to_all | solution.py:21
  76.1 0.3 attention.5
  76.3 1.9 %collective-permute-start = (bf16[16,256]{1,0:T(8,128)(2,1)S(1)}, bf16[16,256]{1,0:T(8,128)(2,1)S(1)}, u32[]{:S(2)}, u32[]{:S(2)}) collective-permute-start(bf16[16,256]{1,0:T(8,128)(2,1)S(1)} %attention.5), channel_id=1, source_target_pairs={{0,0},{1,16},{2,32},{3,48},{4,64},{5,80},{6,96},{7,112},{8,128},{9... | collective-permute-start | bytes 24584 | tf_op jit(solution)/shard_map/attention/ppermute | solution.py:26
  78.3 3.0 %collective-permute-done.in_ref = bf16[16,256]{1,0:T(8,128)(2,1)S(1)} collective-permute-done((bf16[16,256]{1,0:T(8,128)(2,1)S(1)}, bf16[16,256]{1,0:T(8,128)(2,1)S(1)}, u32[]{:S(2)}, u32[]{:S(2)}) %collective-permute-start) | collective-permute-done | bytes 8224 | tf_op jit(solution)/shard_map/attention/ppermute | solution.py:26
  81.3 0.7 attention.6
  82.0 19.5 %all-to-all-start.2 = ((bf16[16,16,256]{2,1,0:T(8,128)(2,1)}), bf16[16,16,256]{2,1,0:T(8,128)(2,1)S(1)}, u32[]{:S(2)}, u32[]{:S(2)}) async-start(bf16[16,16,256]{2,1,0:T(8,128)(2,1)} %attention.6), calls=%async_computation.2 | async-start | bytes 262144 | tf_op jit(solution)/shard_map/attention/all_to_all | solution.py:21
  101.4 0.0 collective-permute-done.1.blocks_ref
  101.5 7.6 %all-to-all-done.2.x_ref = bf16[16,16,256]{2,1,0:T(8,128)(2,1)S(1)} async-done(((bf16[16,16,256]{2,1,0:T(8,128)(2,1)}), bf16[16,16,256]{2,1,0:T(8,128)(2,1)S(1)}, u32[]{:S(2)}, u32[]{:S(2)}) %all-to-all-start.2) | async-done | bytes 131104 | tf_op jit(solution)/shard_map/attention/all_to_all | solution.py:21
  109.1 0.2 projection.1
  109.3 0.0 copy-start
  109.3 16.3 %all_to_all.26.partials_ref = bf16[16,16,512]{2,1,0:T(8,128)(2,1)S(1)} all-to-all(bf16[16,16,512]{2,1,0:T(8,128)(2,1)S(1)} %projection.1), channel_id=1, replica_groups=mesh['ra'=4,'rb'=4,'rc'=4,'tp'=16] {'rb','rc'}, dimensions={0} | all-to-all | bytes 524288 | tf_op jit(solution)/shard_map/projection/all_to_all | solution.py:21
  125.6 0.0 copy-done
  125.7 0.7 norm.2
  126.3 0.0 copy-start.1
  126.3 8.4 %all-to-all-start.4 = ((f32[16,16,128]{2,1,0:T(8,128)}), f32[16,16,128]{2,1,0:T(8,128)S(1)}, u32[]{:S(2)}, u32[]{:S(2)}) async-start(f32[16,16,128]{2,1,0:T(8,128)} %get-tuple-element.8), calls=%async_computation.4 | async-start | bytes 262144 | tf_op jit(solution)/shard_map/norm/all_to_all | solution.py:21
  134.8 0.0 copy-done.1
  134.8 7.7 %all-to-all-done.4.squares_ref = f32[16,16,128]{2,1,0:T(8,128)S(1)} async-done(((f32[16,16,128]{2,1,0:T(8,128)}), f32[16,16,128]{2,1,0:T(8,128)S(1)}, u32[]{:S(2)}, u32[]{:S(2)}) %all-to-all-start.4) | async-done | bytes 131104 | tf_op jit(solution)/shard_map/norm/all_to_all | solution.py:21
  142.5 0.7 norm.3
  (2 shorter events, 0.1 us)
Async XLA Ops:
  2.2 9.4 %all-to-all-start = ((bf16[4,256,128]{2,1,0:T(8,128)(2,1)}), bf16[4,256,128]{2,1,0:T(8,128)(2,1)S(1)}, u32[]{:S(2)}, u32[]{:S(2)}) async-start(bf16[4,256,128]{2,1,0:T(8,128)(2,1)} %broadcast_in_dim.3), calls=%async_computation | async-start | bytes 524288 | tf_op jit(solution)/shard_map/weights/all_to_all | solution.py:21
  11.6 89.8 %collective-permute-start.1 = (bf16[4,256,128]{2,1,0:T(8,128)(2,1)S(1)}, bf16[4,256,128]{2,1,0:T(8,128)(2,1)S(1)}, u32[]{:S(2)}, u32[]{:S(2)}) collective-permute-start(bf16[4,256,128]{2,1,0:T(8,128)(2,1)S(1)} %all-to-all-done), channel_id=1, source_target_pairs={{0,0},{1,16},{2,32},{3,48},{4,64},{5,80},{6,96},{7,112},{8,128},{9... | collective-permute-start | bytes 786440 | tf_op jit(solution)/shard_map/attention/ppermute | solution.py:26
  76.3 5.0 %collective-permute-start = (bf16[16,256]{1,0:T(8,128)(2,1)S(1)}, bf16[16,256]{1,0:T(8,128)(2,1)S(1)}, u32[]{:S(2)}, u32[]{:S(2)}) collective-permute-start(bf16[16,256]{1,0:T(8,128)(2,1)S(1)} %attention.5), channel_id=1, source_target_pairs={{0,0},{1,16},{2,32},{3,48},{4,64},{5,80},{6,96},{7,112},{8,128},{9... | collective-permute-start | bytes 24584 | tf_op jit(solution)/shard_map/attention/ppermute | solution.py:26
  82.0 27.1 %all-to-all-start.2 = ((bf16[16,16,256]{2,1,0:T(8,128)(2,1)}), bf16[16,16,256]{2,1,0:T(8,128)(2,1)S(1)}, u32[]{:S(2)}, u32[]{:S(2)}) async-start(bf16[16,16,256]{2,1,0:T(8,128)(2,1)} %attention.6), calls=%async_computation.2 | async-start | bytes 262144 | tf_op jit(solution)/shard_map/attention/all_to_all | solution.py:21
  109.3 16.3 %copy-start = (bf16[4,4,512]{2,1,0:T(4,128)(2,1)S(1)}, bf16[4,4,512]{2,1,0:T(4,128)(2,1)}, u32[]{:S(2)}) copy-start(bf16[4,4,512]{2,1,0:T(4,128)(2,1)} %stream_ref.1) | copy-start | bytes 49156
  126.3 8.4 %copy-start.1 = (bf16[512]{0:T(512)(128)(2,1)S(1)}, bf16[512]{0:T(512)(128)(2,1)}, u32[]{:S(2)}) copy-start(bf16[512]{0:T(512)(128)(2,1)} %param.17) | copy-start | bytes 3076
  126.3 16.2 %all-to-all-start.4 = ((f32[16,16,128]{2,1,0:T(8,128)}), f32[16,16,128]{2,1,0:T(8,128)S(1)}, u32[]{:S(2)}, u32[]{:S(2)}) async-start(f32[16,16,128]{2,1,0:T(8,128)} %get-tuple-element.8), calls=%async_computation.4 | async-start | bytes 262144 | tf_op jit(solution)/shard_map/norm/all_to_all | solution.py:21

commit v4 on v2

--- a/solution.py
+++ b/solution.py
@@ -31,6 +31,27 @@
 
 def stacked(pieces, axis=0):
     return jnp.concatenate(pieces, axis=axis)
+
+
+def copies_kernel(in_ref, out_ref, sems):
+    sends = [
+        pltpu.make_async_copy(in_ref, out_ref.at[i], sems.at[i]) for i in range(out_ref.shape[0])
+    ]
+    for send in sends:
+        send.start()
+    for send in sends:
+        send.wait()
+
+
+def copies(array, count):
+    return pl.pallas_call(
+        copies_kernel,
+        out_shape=jax.ShapeDtypeStruct((count, *array.shape), array.dtype),
+        in_specs=[pl.BlockSpec(memory_space=pl.ANY)],
+        out_specs=pl.BlockSpec(memory_space=pl.ANY),
+        scratch_shapes=[pltpu.SemaphoreType.DMA((count,))],
+        compiler_params=pltpu.CompilerParams(vmem_limit_bytes=60 * 1024 * 1024),
+    )(array)
 
 
 def attend_kernel(len_ref, q_ref, nk_ref, nv_ref, k_ref, v_ref, out_ref, stats_ref):
@@ -46,22 +67,20 @@
     to_log2 = math.log2(math.e) / math.sqrt(head_dim)
     tp = lax.axis_index("tp")
 
-    def own_head(count):
-        row = lax.broadcasted_iota(jnp.int32, (rows, count), 0)
-        column = lax.broadcasted_iota(jnp.int32, (rows, count), 1)
-        same = (column % kv_heads) == (row // (rows // kv_heads))
-        return row, column // kv_heads, same
-
-    def masked(key_ref, visible):
-        return jnp.where(visible, dot_rows(q, key_ref[0]) * to_log2, MASKED)
-
-    _, position, same = own_head(columns)
-    visible = same & (position < len_ref[b] - tp * block_len)
-    row, fresh_at, same = own_head(nk_ref.shape[1])
-    fresh_visible = same & (fresh_at <= row % steps) & (tp == 0)
+    def masked(key_ref, limit):
+        count = key_ref.shape[1]
+        head = lax.broadcasted_iota(jnp.int32, (kv_heads, 1, count), 0)
+        column = lax.broadcasted_iota(jnp.int32, (kv_heads, 1, count), 2)
+        visible = (column % kv_heads == head) & (column // kv_heads < limit)
+        bias = jnp.where(visible, 0.0, MASKED)
+        scores = (dot_rows(q, key_ref[0]) * to_log2).reshape(kv_heads, -1, count)
+        return (scores + bias).reshape(rows, count)
+
     wide = q_ref[0].astype(F32)
     q = stacked([wide[:, h * head_dim : (h + 1) * head_dim] for h in range(heads)]).astype(BF16)
-    scores, fresh = masked(k_ref, visible), masked(nk_ref, fresh_visible)
+    scores = masked(k_ref, len_ref[b] - tp * block_len)
+    step = lax.broadcasted_iota(jnp.int32, (1, rows // kv_heads, 1), 1) % steps
+    fresh = masked(nk_ref, jnp.where(tp == 0, step + 1, 0))
     top = jnp.maximum(scores.max(1, keepdims=True), fresh.max(1, keepdims=True))
     shift = jnp.maximum(top, NONE_VISIBLE).astype(BF16).astype(F32)
     weights, fresh_weights = jnp.exp2(scores - shift), jnp.exp2(fresh - shift)
@@ -180,18 +199,18 @@
     share = width // n_tp
 
     with jax.named_scope("weights"):
-        quad = exchanged(jnp.broadcast_to(out_weight, (n_quad, *out_weight.shape)), QUAD)
+        quad = exchanged(copies(out_weight, n_quad), QUAD)
+        lengths, quad = lax.optimization_barrier((lengths, quad))
+        weight = permuted(quad, REP, n_rep, lambda r: (r % n_quad) * n_arc + r // n_quad)
+        weight = call(
+            side_by_side_kernel, jax.ShapeDtypeStruct((share, columns), BF16), weight, flops=20_000_000_000
+        )
 
     with jax.named_scope("attention"):
         flat = lambda a: a.reshape(rows_b, -1, head_dim)
         parts = attend(
             queries, flat(new_keys), flat(new_values), flat(key_cache), flat(value_cache), lengths,
             jax.ShapeDtypeStruct((n_tp, rows_b + 1, 8, head_dim), BF16),
-        )
-        parts, quad = lax.optimization_barrier((parts, quad))
-        weight = permuted(quad, REP, n_rep, lambda r: (r % n_quad) * n_arc + r // n_quad)
-        weight = call(
-            side_by_side_kernel, jax.ShapeDtypeStruct((share, columns), BF16), weight, flops=20_000_000_000
         )
         parts = exchanged(parts, "tp")
         attended = call(combine_kernel, jax.ShapeDtypeStruct((n_arc, rows, share), BF16), parts)

time: 124 us -> 131 us (1.056)
  Pallas kernels: 7.33 us -> 16.3 us
  blocking collectives: 32.9 us -> 39.8 us
  waiting for transfers between devices: 26.1 us -> 20.8 us
  starting transfers between devices: 54.7 us -> 52.7 us
  local copies, waits for them, and re-layouts: 1.6 us -> 0.01 us
    pallas_call x0 -> x1, Pallas kernels: none -> 9.08 us  [copies(): pl.pallas_call(copies_kernel, out_shape=jax.ShapeDtypeStruct((count, *arr...]
    all_to_all x2 -> x3, blocking collectives: 32.9 us -> 39.8 us  [exchanged(): return lax.all_to_all(pieces, axes, split_axis=0, concat_axis=0, tiled=True)]
    all_to_all x3 -> x2, waiting for transfers between devices: 23 us -> 18.2 us  [exchanged(): return lax.all_to_all(pieces, axes, split_axis=0, concat_axis=0, tiled=True)]
    all_to_all x3 -> x2, starting transfers between devices: 50.9 us -> 48.3 us  [exchanged(): return lax.all_to_all(pieces, axes, split_axis=0, concat_axis=0, tiled=True)]
    broadcast_in_dim x1 -> x0, local copies, waits for them, and re-layouts: 1.59 us -> none  [on_device(): jnp.broadcast_to(out_weight, (n_quad, *out_weight.shape))]
  transfers between devices with their start and end apart: 5 -> 4, of which waited for: 3 -> 3; matrix products, arithmetic and copies ran while one was open for 0% -> 0% of each run, Pallas kernels for 5% -> 4%
where the time goes in v4:
time: 131 us; the launch traced here: 130 us
  starting transfers between devices  52.7 us (40%)
  blocking collectives  39.8 us (30%)
  waiting for transfers between devices  20.8 us (16%)
  Pallas kernels  16.3 us (12%)
    all_to_all x2, starting transfers between devices, exchanged(): return lax.all_to_all(pieces, axes, split_axis=0, concat_axis=0, tiled=True)  48.3 us
    all_to_all x3, blocking collectives, exchanged(): return lax.all_to_all(pieces, axes, split_axis=0, concat_axis=0, tiled=True)  39.8 us
    all_to_all x2, waiting for transfers between devices, exchanged(): return lax.all_to_all(pieces, axes, split_axis=0, concat_axis=0, tiled=True)  18.2 us
    pallas_call x1, Pallas kernels, copies(): pl.pallas_call(copies_kernel, out_shape=jax.ShapeDtypeStruct((count, *arr...  9.08 us
    pallas_call x1, Pallas kernels, attend(): pl.pallas_call(attend_kernel, grid=(queries.shape[0],), out_shape=outs, i...  4.67 us
    ppermute x2, starting transfers between devices, permuted(): return lax.ppermute(array, axes, [(i, target(i)) for i in range(count)])  4.36 us
  transfers between devices with their start and end apart: 4, of which 3 were waited for; matrix products, arithmetic and copies ran while one was open for 0% of the time, Pallas kernels for 4%

profile of v4, /device:TPU:257, one launch (start us, length us, event | category | flops | bytes accessed | tf_op | source)
XLA Modules:
  0.0 130.4 jit_solution(4889513049071204805)
XLA Ops:
  0.6 9.1 %weights.2 = bf16[4,256,128]{2,1,0:T(8,128)(2,1)} custom-call(bf16[256,128]{1,0:T(8,128)(2,1)} %in_ref.1), custom_call_target="tpu_custom_call" | custom-call | tf_op jit(solution)/shard_map/weights/pallas_call | solution.py:47
  9.7 8.5 %all_to_all.25 = bf16[4,256,128]{2,1,0:T(8,128)(2,1)S(1)} all-to-all(bf16[4,256,128]{2,1,0:T(8,128)(2,1)} %weights.2), channel_id=1, replica_groups=mesh['ra'=4,'rb'=4,'rc'=4,'tp'=16] {'rc'}, dimensions={0} | all-to-all | bytes 524288 | tf_op jit(solution)/shard_map/weights/all_to_all | solution.py:21
  18.2 1.9 %collective-permute-start = (bf16[4,256,128]{2,1,0:T(8,128)(2,1)S(1)}, bf16[4,256,128]{2,1,0:T(8,128)(2,1)S(1)}, u32[]{:S(2)}, u32[]{:S(2)}) collective-permute-start(bf16[4,256,128]{2,1,0:T(8,128)(2,1)S(1)} %all_to_all.25), channel_id=1, source_target_pairs={{0,0},{16,256},{32,512},{48,768},{64,16},{80,272},{96,528},{112,78... | collective-permute-start | bytes 786440 | tf_op jit(solution)/shard_map/weights/ppermute | solution.py:25
  20.2 4.7 %attention.2 = bf16[16,5,8,128]{3,2,1,0:T(8,128)(2,1)} custom-call(s32[4]{0:T(128)} %len_ref, bf16[4,4,4096]{2,1,0:T(4,128)(2,1)} %q_ref.1, bf16[4,16,128]{2,1,0:T(8,128)(2,1)} %bitcast.6, bf16[4,16,128]{2,1,0:T(8,128)(2,1)} %bitcast.7, bf16[4,1024,128]{2,1,0:T(8,128)(2,1)} %bitcast.4, bf16[4,1024,128]{2,1,0:T(8,128)(2,1)} %bitcast.5), custom_call_target="tpu_custom_call" | custom-call | flops 300000000 | bytes 2097152 | tf_op jit(solution)/shard_map/attention/pallas_call | solution.py:105
  24.8 16.6 %all_to_all.26.parts_ref = bf16[16,5,8,128]{3,2,1,0:T(8,128)(2,1)S(1)} all-to-all(bf16[16,5,8,128]{3,2,1,0:T(8,128)(2,1)} %attention.2), channel_id=1, replica_groups=mesh['ra'=4,'rb'=4,'rc'=4,'tp'=16] {'tp'}, dimensions={0} | all-to-all | bytes 327680 | tf_op jit(solution)/shard_map/attention/all_to_all | solution.py:21
  41.4 0.9 attention.3
  42.3 25.0 %all-to-all-start.2 = ((bf16[16,16,256]{2,1,0:T(8,128)(2,1)}), bf16[16,16,256]{2,1,0:T(8,128)(2,1)S(1)}, u32[]{:S(2)}, u32[]{:S(2)}) async-start(bf16[16,16,256]{2,1,0:T(8,128)(2,1)} %attention.3), calls=%async_computation.2 | async-start | bytes 262144 | tf_op jit(solution)/shard_map/attention/all_to_all | solution.py:21
  67.3 0.0 collective-permute-done.blocks_ref
  67.4 10.6 %all-to-all-done.2.x_ref = bf16[16,16,256]{2,1,0:T(8,128)(2,1)S(1)} async-done(((bf16[16,16,256]{2,1,0:T(8,128)(2,1)}), bf16[16,16,256]{2,1,0:T(8,128)(2,1)S(1)}, u32[]{:S(2)}, u32[]{:S(2)}) %all-to-all-start.2) | async-done | bytes 131104 | tf_op jit(solution)/shard_map/attention/all_to_all | solution.py:21
  78.0 0.2 projection.2
  78.2 14.7 %all_to_all.27.parts_ref = bf16[16,16,512]{2,1,0:T(8,128)(2,1)S(1)} all-to-all(bf16[16,16,512]{2,1,0:T(8,128)(2,1)S(1)} %projection.2), channel_id=1, replica_groups=mesh['ra'=4,'rb'=4,'rc'=4,'tp'=16] {'tp'}, dimensions={0} | all-to-all | bytes 524288 | tf_op jit(solution)/shard_map/projection/all_to_all | solution.py:21
  92.9 0.0 copy-start
  93.0 2.5 %collective-permute-start.1 = (bf16[16,512]{1,0:T(8,128)(2,1)S(1)}, bf16[16,512]{1,0:T(8,128)(2,1)S(1)}, u32[]{:S(2)}, u32[]{:S(2)}) collective-permute-start(bf16[16,512]{1,0:T(8,128)(2,1)S(1)} %projection.3), channel_id=1, source_target_pairs={{0,0},{1,16},{2,32},{3,48},{4,64},{5,80},{6,96},{7,112},{8,128},{9... | collective-permute-start | bytes 49160 | tf_op jit(solution)/shard_map/projection/ppermute | solution.py:25
  95.4 2.6 %collective-permute-done.1.summed_ref = bf16[16,512]{1,0:T(8,128)(2,1)S(1)} collective-permute-done((bf16[16,512]{1,0:T(8,128)(2,1)S(1)}, bf16[16,512]{1,0:T(8,128)(2,1)S(1)}, u32[]{:S(2)}, u32[]{:S(2)}) %collective-permute-start.1) | collective-permute-done | bytes 16416 | tf_op jit(solution)/shard_map/projection/ppermute | solution.py:25
  98.0 0.0 copy-done
  98.0 0.7 norm.2
  98.7 0.0 copy-start.1
  98.7 23.3 %all-to-all-start.4 = ((f32[16,16,128]{2,1,0:T(8,128)}), f32[16,16,128]{2,1,0:T(8,128)S(1)}, u32[]{:S(2)}, u32[]{:S(2)}) async-start(f32[16,16,128]{2,1,0:T(8,128)} %get-tuple-element.8), calls=%async_computation.4 | async-start | bytes 262144 | tf_op jit(solution)/shard_map/norm/all_to_all | solution.py:21
  122.0 0.0 copy-done.1
  122.1 7.6 %all-to-all-done.4.squares_ref = f32[16,16,128]{2,1,0:T(8,128)S(1)} async-done(((f32[16,16,128]{2,1,0:T(8,128)}), f32[16,16,128]{2,1,0:T(8,128)S(1)}, u32[]{:S(2)}, u32[]{:S(2)}) %all-to-all-start.4) | async-done | bytes 131104 | tf_op jit(solution)/shard_map/norm/all_to_all | solution.py:21
  129.7 0.7 norm.3
  (3 shorter events, 0.1 us)
Async XLA Ops:
  18.2 49.1 %collective-permute-start = (bf16[4,256,128]{2,1,0:T(8,128)(2,1)S(1)}, bf16[4,256,128]{2,1,0:T(8,128)(2,1)S(1)}, u32[]{:S(2)}, u32[]{:S(2)}) collective-permute-start(bf16[4,256,128]{2,1,0:T(8,128)(2,1)S(1)} %all_to_all.25), channel_id=1, source_target_pairs={{0,0},{16,256},{32,512},{48,768},{64,16},{80,272},{96,528},{112,78... | collective-permute-start | bytes 786440 | tf_op jit(solution)/shard_map/weights/ppermute | solution.py:25
  42.3 35.6 %all-to-all-start.2 = ((bf16[16,16,256]{2,1,0:T(8,128)(2,1)}), bf16[16,16,256]{2,1,0:T(8,128)(2,1)S(1)}, u32[]{:S(2)}, u32[]{:S(2)}) async-start(bf16[16,16,256]{2,1,0:T(8,128)(2,1)} %attention.3), calls=%async_computation.2 | async-start | bytes 262144 | tf_op jit(solution)/shard_map/attention/all_to_all | solution.py:21
  92.9 5.1 %copy-start = (bf16[4,4,512]{2,1,0:T(4,128)(2,1)S(1)}, bf16[4,4,512]{2,1,0:T(4,128)(2,1)}, u32[]{:S(2)}) copy-start(bf16[4,4,512]{2,1,0:T(4,128)(2,1)} %stream_ref.1) | copy-start | bytes 49156
  93.0 5.1 %collective-permute-start.1 = (bf16[16,512]{1,0:T(8,128)(2,1)S(1)}, bf16[16,512]{1,0:T(8,128)(2,1)S(1)}, u32[]{:S(2)}, u32[]{:S(2)}) collective-permute-start(bf16[16,512]{1,0:T(8,128)(2,1)S(1)} %projection.3), channel_id=1, source_target_pairs={{0,0},{1,16},{2,32},{3,48},{4,64},{5,80},{6,96},{7,112},{8,128},{9... | collective-permute-start | bytes 49160 | tf_op jit(solution)/shard_map/projection/ppermute | solution.py:25
  98.7 23.3 %copy-start.1 = (bf16[512]{0:T(512)(128)(2,1)S(1)}, bf16[512]{0:T(512)(128)(2,1)}, u32[]{:S(2)}) copy-start(bf16[512]{0:T(512)(128)(2,1)} %param.17) | copy-start | bytes 3076
  98.7 31.0 %all-to-all-start.4 = ((f32[16,16,128]{2,1,0:T(8,128)}), f32[16,16,128]{2,1,0:T(8,128)S(1)}, u32[]{:S(2)}, u32[]{:S(2)}) async-start(f32[16,16,128]{2,1,0:T(8,128)} %get-tuple-element.8), calls=%async_computation.4 | async-start | bytes 262144 | tf_op jit(solution)/shard_map/norm/all_to_all | solution.py:21

commit v5 on v2

--- a/solution.py
+++ b/solution.py
@@ -194,7 +194,7 @@
             side_by_side_kernel, jax.ShapeDtypeStruct((share, columns), BF16), weight, flops=20_000_000_000
         )
         parts = exchanged(parts, "tp")
-        attended = call(combine_kernel, jax.ShapeDtypeStruct((n_arc, rows, share), BF16), parts)
+        attended = call(combine_kernel, jax.ShapeDtypeStruct((n_arc, rows, share), BF16), parts, flops=4_000_000_000)
         attended = exchanged(attended, ARC)
 
     with jax.named_scope("projection"):

time: 124 us -> 132 us (1.065)
  waiting for transfers between devices: 26.1 us -> 42.9 us
  blocking collectives: 32.9 us -> 16.8 us
  starting transfers between devices: 54.7 us -> 62.3 us
    all_to_all x2 -> x1, blocking collectives: 32.9 us -> 16.8 us  [exchanged(): return lax.all_to_all(pieces, axes, split_axis=0, concat_axis=0, tiled=True)]
    ppermute x2, waiting for transfers between devices: 3.13 us -> 16 us  [permuted(): return lax.ppermute(array, axes, [(i, target(i)) for i in range(count)])]
    all_to_all x3 -> x4, starting transfers between devices: 50.9 us -> 56.8 us  [exchanged(): return lax.all_to_all(pieces, axes, split_axis=0, concat_axis=0, tiled=True)]
    all_to_all x3 -> x4, waiting for transfers between devices: 23 us -> 26.9 us  [exchanged(): return lax.all_to_all(pieces, axes, split_axis=0, concat_axis=0, tiled=True)]
    ppermute x2, starting transfers between devices: 3.83 us -> 5.49 us  [permuted(): return lax.ppermute(array, axes, [(i, target(i)) for i in range(count)])]
  transfers between devices with their start and end apart: 5 -> 6, of which waited for: 3 -> 5; matrix products, arithmetic and copies ran while one was open for 0% -> 0% of each run, Pallas kernels for 5% -> 4%
where the time goes in v5:
time: 132 us
  starting transfers between devices  62.3 us (47%)
  waiting for transfers between devices  42.9 us (32%)
  blocking collectives  16.8 us (13%)
  Pallas kernels  7.34 us (6%)
  local copies, waits for them, and re-layouts  1.59 us (1%)
    all_to_all x4, starting transfers between devices, exchanged(): return lax.all_to_all(pieces, axes, split_axis=0, concat_axis=0, tiled=True)  56.8 us
    all_to_all x4, waiting for transfers between devices, exchanged(): return lax.all_to_all(pieces, axes, split_axis=0, concat_axis=0, tiled=True)  26.9 us
    all_to_all x1, blocking collectives, exchanged(): return lax.all_to_all(pieces, axes, split_axis=0, concat_axis=0, tiled=True)  16.8 us
    ppermute x2, waiting for transfers between devices, permuted(): return lax.ppermute(array, axes, [(i, target(i)) for i in range(count)])  16 us
    ppermute x2, starting transfers between devices, permuted(): return lax.ppermute(array, axes, [(i, target(i)) for i in range(count)])  5.49 us
    pallas_call x1, Pallas kernels, attend(): pl.pallas_call(attend_kernel, grid=(queries.shape[0],), out_shape=outs, i...  4.74 us
  transfers between devices with their start and end apart: 6, of which 5 were waited for; matrix products, arithmetic and copies ran while one was open for 0% of the time, Pallas kernels for 4%

profile of v5, /device:TPU:257, one launch (start us, length us, event | category | flops | bytes accessed | tf_op | source)
XLA Modules:
  0.0 131.6 jit_solution(6640348614218419379)
XLA Ops:
  0.6 1.6 %broadcast_in_dim.3 = bf16[4,256,128]{2,1,0:T(8,128)(2,1)} broadcast(bf16[256,128]{1,0:T(8,128)(2,1)} %param.16), dimensions={1,2} | broadcast | bytes 327680 | tf_op jit(solution)/shard_map/weights/broadcast_in_dim | solution.py:183
  2.2 3.8 %all-to-all-start = ((bf16[4,256,128]{2,1,0:T(8,128)(2,1)}), bf16[4,256,128]{2,1,0:T(8,128)(2,1)S(1)}, u32[]{:S(2)}, u32[]{:S(2)}) async-start(bf16[4,256,128]{2,1,0:T(8,128)(2,1)} %broadcast_in_dim.3), calls=%async_computation | async-start | bytes 524288 | tf_op jit(solution)/shard_map/weights/all_to_all | solution.py:21
  6.0 4.7 %attention.3 = bf16[16,5,8,128]{3,2,1,0:T(8,128)(2,1)} custom-call(s32[4]{0:T(128)} %len_ref.1, bf16[4,4,4096]{2,1,0:T(4,128)(2,1)} %q_ref.1, bf16[4,16,128]{2,1,0:T(8,128)(2,1)} %bitcast.6, bf16[4,16,128]{2,1,0:T(8,128)(2,1)} %bitcast.7, bf16[4,1024,128]{2,1,0:T(8,128)(2,1)} %bitcast.4, bf16[4,1024,128]{2,1,0:T(8,128)(2,1)} %bitcast.5), custom_call_target="tpu_custom_call" | custom-call | flops 300000000 | bytes 2097152 | tf_op jit(solution)/shard_map/attention/pallas_call | solution.py:86
  10.8 0.0 all-to-all-done
  10.8 8.2 %all-to-all-start.1 = ((bf16[16,5,8,128]{3,2,1,0:T(8,128)(2,1)}), bf16[16,5,8,128]{3,2,1,0:T(8,128)(2,1)S(1)}, u32[]{:S(2)}, u32[]{:S(2)}) async-start(bf16[16,5,8,128]{3,2,1,0:T(8,128)(2,1)} %attention.3), calls=%async_computation.1 | async-start | bytes 327680 | tf_op jit(solution)/shard_map/attention/all_to_all | solution.py:21
  19.0 1.9 %collective-permute-start = (bf16[4,256,128]{2,1,0:T(8,128)(2,1)S(1)}, bf16[4,256,128]{2,1,0:T(8,128)(2,1)S(1)}, u32[]{:S(2)}, u32[]{:S(2)}) collective-permute-start(bf16[4,256,128]{2,1,0:T(8,128)(2,1)S(1)} %all-to-all-done), channel_id=1, source_target_pairs={{0,0},{16,256},{32,512},{48,768},{64,16},{80,272},{96,528},{112,78... | collective-permute-start | bytes 786440 | tf_op jit(solution)/shard_map/attention/ppermute | solution.py:25
  20.9 6.0 %all-to-all-done.1.parts_ref = bf16[16,5,8,128]{3,2,1,0:T(8,128)(2,1)S(1)} async-done(((bf16[16,5,8,128]{3,2,1,0:T(8,128)(2,1)}), bf16[16,5,8,128]{3,2,1,0:T(8,128)(2,1)S(1)}, u32[]{:S(2)}, u32[]{:S(2)}) %all-to-all-start.1) | async-done | bytes 163872 | tf_op jit(solution)/shard_map/attention/all_to_all | solution.py:21
  27.0 0.9 attention.4
  27.9 15.2 %all-to-all-start.2 = ((bf16[16,16,256]{2,1,0:T(8,128)(2,1)}), bf16[16,16,256]{2,1,0:T(8,128)(2,1)S(1)}, u32[]{:S(2)}, u32[]{:S(2)}) async-start(bf16[16,16,256]{2,1,0:T(8,128)(2,1)} %attention.4), calls=%async_computation.2 | async-start | bytes 262144 | tf_op jit(solution)/shard_map/attention/all_to_all | solution.py:21
  43.1 14.6 %collective-permute-done.blocks_ref = bf16[4,256,128]{2,1,0:T(8,128)(2,1)S(1)} collective-permute-done((bf16[4,256,128]{2,1,0:T(8,128)(2,1)S(1)}, bf16[4,256,128]{2,1,0:T(8,128)(2,1)S(1)}, u32[]{:S(2)}, u32[]{:S(2)}) %collective-permute-start) | collective-permute-done | bytes 262176 | tf_op jit(solution)/shard_map/attention/ppermute | solution.py:25
  57.7 13.2 %all-to-all-done.2.x_ref = bf16[16,16,256]{2,1,0:T(8,128)(2,1)S(1)} async-done(((bf16[16,16,256]{2,1,0:T(8,128)(2,1)}), bf16[16,16,256]{2,1,0:T(8,128)(2,1)S(1)}, u32[]{:S(2)}, u32[]{:S(2)}) %all-to-all-start.2) | async-done | bytes 131104 | tf_op jit(solution)/shard_map/attention/all_to_all | solution.py:21
  70.9 0.2 projection.2
  71.1 16.8 %all_to_all.25.parts_ref = bf16[16,16,512]{2,1,0:T(8,128)(2,1)S(1)} all-to-all(bf16[16,16,512]{2,1,0:T(8,128)(2,1)S(1)} %projection.2), channel_id=1, replica_groups=mesh['ra'=4,'rb'=4,'rc'=4,'tp'=16] {'tp'}, dimensions={0} | all-to-all | bytes 524288 | tf_op jit(solution)/shard_map/projection/all_to_all | solution.py:21
  87.9 0.0 copy-start
  87.9 3.6 %collective-permute-start.1 = (bf16[16,512]{1,0:T(8,128)(2,1)S(1)}, bf16[16,512]{1,0:T(8,128)(2,1)S(1)}, u32[]{:S(2)}, u32[]{:S(2)}) collective-permute-start(bf16[16,512]{1,0:T(8,128)(2,1)S(1)} %projection.3), channel_id=1, source_target_pairs={{0,0},{1,16},{2,32},{3,48},{4,64},{5,80},{6,96},{7,112},{8,128},{9... | collective-permute-start | bytes 49160 | tf_op jit(solution)/shard_map/projection/ppermute | solution.py:25
  91.5 1.5 %collective-permute-done.1.summed_ref = bf16[16,512]{1,0:T(8,128)(2,1)S(1)} collective-permute-done((bf16[16,512]{1,0:T(8,128)(2,1)S(1)}, bf16[16,512]{1,0:T(8,128)(2,1)S(1)}, u32[]{:S(2)}, u32[]{:S(2)}) %collective-permute-start.1) | collective-permute-done | bytes 16416 | tf_op jit(solution)/shard_map/projection/ppermute | solution.py:25
  93.0 0.0 copy-done
  93.0 0.7 norm.2
  93.7 0.0 copy-start.1
  93.7 29.6 %all-to-all-start.4 = ((f32[16,16,128]{2,1,0:T(8,128)}), f32[16,16,128]{2,1,0:T(8,128)S(1)}, u32[]{:S(2)}, u32[]{:S(2)}) async-start(f32[16,16,128]{2,1,0:T(8,128)} %get-tuple-element.8), calls=%async_computation.4 | async-start | bytes 262144 | tf_op jit(solution)/shard_map/norm/all_to_all | solution.py:21
  123.3 0.0 copy-done.1
  123.3 7.6 %all-to-all-done.4.squares_ref = f32[16,16,128]{2,1,0:T(8,128)S(1)} async-done(((f32[16,16,128]{2,1,0:T(8,128)}), f32[16,16,128]{2,1,0:T(8,128)S(1)}, u32[]{:S(2)}, u32[]{:S(2)}) %all-to-all-start.4) | async-done | bytes 131104 | tf_op jit(solution)/shard_map/norm/all_to_all | solution.py:21
  130.9 0.7 norm.3
  (3 shorter events, 0.1 us)
Async XLA Ops:
  2.2 8.6 %all-to-all-start = ((bf16[4,256,128]{2,1,0:T(8,128)(2,1)}), bf16[4,256,128]{2,1,0:T(8,128)(2,1)S(1)}, u32[]{:S(2)}, u32[]{:S(2)}) async-start(bf16[4,256,128]{2,1,0:T(8,128)(2,1)} %broadcast_in_dim.3), calls=%async_computation | async-start | bytes 524288 | tf_op jit(solution)/shard_map/weights/all_to_all | solution.py:21
  10.8 16.2 %all-to-all-start.1 = ((bf16[16,5,8,128]{3,2,1,0:T(8,128)(2,1)}), bf16[16,5,8,128]{3,2,1,0:T(8,128)(2,1)S(1)}, u32[]{:S(2)}, u32[]{:S(2)}) async-start(bf16[16,5,8,128]{3,2,1,0:T(8,128)(2,1)} %attention.3), calls=%async_computation.1 | async-start | bytes 327680 | tf_op jit(solution)/shard_map/attention/all_to_all | solution.py:21
  19.0 38.6 %collective-permute-start = (bf16[4,256,128]{2,1,0:T(8,128)(2,1)S(1)}, bf16[4,256,128]{2,1,0:T(8,128)(2,1)S(1)}, u32[]{:S(2)}, u32[]{:S(2)}) collective-permute-start(bf16[4,256,128]{2,1,0:T(8,128)(2,1)S(1)} %all-to-all-done), channel_id=1, source_target_pairs={{0,0},{16,256},{32,512},{48,768},{64,16},{80,272},{96,528},{112,78... | collective-permute-start | bytes 786440 | tf_op jit(solution)/shard_map/attention/ppermute | solution.py:25
  27.9 43.0 %all-to-all-start.2 = ((bf16[16,16,256]{2,1,0:T(8,128)(2,1)}), bf16[16,16,256]{2,1,0:T(8,128)(2,1)S(1)}, u32[]{:S(2)}, u32[]{:S(2)}) async-start(bf16[16,16,256]{2,1,0:T(8,128)(2,1)} %attention.4), calls=%async_computation.2 | async-start | bytes 262144 | tf_op jit(solution)/shard_map/attention/all_to_all | solution.py:21
  87.9 5.1 %copy-start = (bf16[4,4,512]{2,1,0:T(4,128)(2,1)S(1)}, bf16[4,4,512]{2,1,0:T(4,128)(2,1)}, u32[]{:S(2)}) copy-start(bf16[4,4,512]{2,1,0:T(4,128)(2,1)} %stream_ref.1) | copy-start | bytes 49156
  87.9 5.1 %collective-permute-start.1 = (bf16[16,512]{1,0:T(8,128)(2,1)S(1)}, bf16[16,512]{1,0:T(8,128)(2,1)S(1)}, u32[]{:S(2)}, u32[]{:S(2)}) collective-permute-start(bf16[16,512]{1,0:T(8,128)(2,1)S(1)} %projection.3), channel_id=1, source_target_pairs={{0,0},{1,16},{2,32},{3,48},{4,64},{5,80},{6,96},{7,112},{8,128},{9... | collective-permute-start | bytes 49160 | tf_op jit(solution)/shard_map/projection/ppermute | solution.py:25
  93.7 29.6 %copy-start.1 = (bf16[512]{0:T(512)(128)(2,1)S(1)}, bf16[512]{0:T(512)(128)(2,1)}, u32[]{:S(2)}) copy-start(bf16[512]{0:T(512)(128)(2,1)} %param.17) | copy-start | bytes 3076
  93.7 37.3 %all-to-all-start.4 = ((f32[16,16,128]{2,1,0:T(8,128)}), f32[16,16,128]{2,1,0:T(8,128)S(1)}, u32[]{:S(2)}, u32[]{:S(2)}) async-start(f32[16,16,128]{2,1,0:T(8,128)} %get-tuple-element.8), calls=%async_computation.4 | async-start | bytes 262144 | tf_op jit(solution)/shard_map/norm/all_to_all | solution.py:21

commit v6 on v2

--- a/solution.py
+++ b/solution.py
@@ -1,3 +1,4 @@
+import functools
 import math
 
 import jax
@@ -33,9 +34,10 @@
     return jnp.concatenate(pieces, axis=axis)
 
 
-def attend_kernel(len_ref, q_ref, nk_ref, nv_ref, k_ref, v_ref, out_ref, stats_ref):
-    b = pl.program_id(0)
-    rows_b = pl.num_programs(0)
+def attend_kernel(first, len_ref, q_ref, nk_ref, nv_ref, k_ref, v_ref, *refs):
+    *earlier_ref, out_ref, stats_ref = refs
+    b = first + pl.program_id(0)
+    rows_b = out_ref.shape[1] - 1
     _, steps, width = q_ref.shape
     head_dim = k_ref.shape[2]
     kv_heads = nk_ref.shape[1] // steps
@@ -71,7 +73,16 @@
     out_ref[:, b] = numerator.astype(BF16).reshape(-1, 8, head_dim)
     high = total.astype(BF16).astype(F32)
     lane = lax.broadcasted_iota(jnp.int32, (rows, head_dim), 1)
-    stats = jnp.where(b == 0, jnp.zeros((rows, head_dim), F32), stats_ref[...])
+    if earlier_ref:
+        earlier = earlier_ref[0][:, first].astype(F32).reshape(rows, head_dim)
+
+        @pl.when(b == first)
+        def _():
+            out_ref[:, :first] = earlier_ref[0][:, :first]
+
+    else:
+        earlier = jnp.zeros((rows, head_dim), F32)
+    stats = jnp.where(b == first, earlier, stats_ref[...])
     stats = jnp.where(lane == 3 * b, shift, stats)
     stats = jnp.where(lane == 3 * b + 1, high, stats)
     stats = jnp.where(lane == 3 * b + 2, total - high, stats)
@@ -79,25 +90,29 @@
     out_ref[:, rows_b] = stats.astype(BF16).reshape(-1, 8, head_dim)
 
 
-def attend(queries, new_keys, new_values, keys, values, lengths, outs):
-    def of_row(a):
-        return pl.BlockSpec((1, *a.shape[1:]), lambda b: (b, 0, 0))
-
+def attend(queries, new_keys, new_values, keys, values, lengths, first, last, *earlier):
+    arrays = (queries, new_keys, new_values, keys, values)
+    head_dim = keys.shape[2]
+    pieces = queries.shape[2] * queries.shape[1] // head_dim // 8
+    outs = jax.ShapeDtypeStruct((pieces, last + 1, 8, head_dim), BF16)
+    whole = pl.BlockSpec(outs.shape, lambda b: (0, 0, 0, 0))
+    before = [pl.BlockSpec(a.shape, lambda b: (0, 0, 0, 0)) for a in earlier]
     return pl.pallas_call(
-        attend_kernel,
-        grid=(queries.shape[0],),
+        functools.partial(attend_kernel, first),
+        grid=(last - first,),
         out_shape=outs,
         in_specs=[
             pl.BlockSpec(memory_space=pltpu.SMEM),
-            *(of_row(a) for a in (queries, new_keys, new_values, keys, values)),
+            *(pl.BlockSpec((1, *a.shape[1:]), lambda b: (first + b, 0, 0)) for a in arrays),
+            *before,
         ],
-        out_specs=pl.BlockSpec(outs.shape, lambda b: (0, 0, 0, 0)),
-        scratch_shapes=[pltpu.VMEM((outs.shape[0] * outs.shape[2], outs.shape[3]), F32)],
+        out_specs=whole,
+        scratch_shapes=[pltpu.VMEM((pieces * 8, head_dim), F32)],
         compiler_params=pltpu.CompilerParams(vmem_limit_bytes=60 * 1024 * 1024),
         cost_estimate=pl.CostEstimate(
-            flops=300_000_000, bytes_accessed=2 * keys.size * 2, transcendentals=600_000
+            flops=150_000_000, bytes_accessed=keys.size * 2, transcendentals=300_000
         ),
-    )(lengths, queries, new_keys, new_values, keys, values)
+    )(lengths, *arrays, *earlier)
 
 
 def combine_kernel(parts_ref, out_ref):
@@ -184,11 +199,11 @@
 
     with jax.named_scope("attention"):
         flat = lambda a: a.reshape(rows_b, -1, head_dim)
-        parts = attend(
-            queries, flat(new_keys), flat(new_values), flat(key_cache), flat(value_cache), lengths,
-            jax.ShapeDtypeStruct((n_tp, rows_b + 1, 8, head_dim), BF16),
-        )
+        cached = (flat(new_keys), flat(new_values), flat(key_cache), flat(value_cache))
+        half = rows_b // 2
+        parts = attend(queries, *cached, lengths, 0, half)
         parts, quad = lax.optimization_barrier((parts, quad))
+        parts = attend(queries, *cached, lengths, half, rows_b, parts)
         weight = permuted(quad, REP, n_rep, lambda r: (r % n_quad) * n_arc + r // n_quad)
         weight = call(
             side_by_side_kernel, jax.ShapeDtypeStruct((share, columns), BF16), weight, flops=20_000_000_000

time: 124 us -> 124 us (level)
  waiting for transfers between devices: 26.1 us -> 22.6 us
  blocking collectives: 32.9 us -> 35 us
  Pallas kernels: 7.33 us -> 8.74 us
    all_to_all x3, waiting for transfers between devices: 23 us -> 19.5 us  [exchanged(): return lax.all_to_all(pieces, axes, split_axis=0, concat_axis=0, tiled=True)]
    all_to_all x2, blocking collectives: 32.9 us -> 35 us  [exchanged(): return lax.all_to_all(pieces, axes, split_axis=0, concat_axis=0, tiled=True)]
    pallas_call x1 -> x2, Pallas kernels: 4.75 us -> 6.15 us  [attend(): pl.pallas_call(functools.partial(attend_kernel, first), grid=(last - firs...]
  transfers between devices with their start and end apart: 5 -> 5, of which waited for: 3 -> 4; matrix products, arithmetic and copies ran while one was open for 0% -> 0% of each run, Pallas kernels for 5% -> 6%
where the time goes in v6:
time: 124 us; the launch traced here: 123 us
  starting transfers between devices  54.3 us (44%)
  blocking collectives  35 us (28%)
  waiting for transfers between devices  22.6 us (18%)
  Pallas kernels  8.74 us (7%)
  local copies, waits for them, and re-layouts  1.6 us (1%)
    all_to_all x3, starting transfers between devices, exchanged(): return lax.all_to_all(pieces, axes, split_axis=0, concat_axis=0, tiled=True)  50.5 us
    all_to_all x2, blocking collectives, exchanged(): return lax.all_to_all(pieces, axes, split_axis=0, concat_axis=0, tiled=True)  35 us
    all_to_all x3, waiting for transfers between devices, exchanged(): return lax.all_to_all(pieces, axes, split_axis=0, concat_axis=0, tiled=True)  19.5 us
    pallas_call x2, Pallas kernels, attend(): pl.pallas_call(functools.partial(attend_kernel, first), grid=(last - firs...  6.15 us
    ppermute x2, starting transfers between devices, permuted(): return lax.ppermute(array, axes, [(i, target(i)) for i in range(count)])  3.83 us
    ppermute x2, waiting for transfers between devices, permuted(): return lax.ppermute(array, axes, [(i, target(i)) for i in range(count)])  3.13 us
    pallas_call x6, Pallas kernels, call(): pl.pallas_call(kernel, out_shape=outs, in_specs=[vmem] * len(args), out_s...  2.59 us
  transfers between devices with their start and end apart: 5, of which 4 were waited for; matrix products, arithmetic and copies ran while one was open for 0% of the time, Pallas kernels for 6%

profile of v6, /device:TPU:257, one launch (start us, length us, event | category | flops | bytes accessed | tf_op | source)
XLA Modules:
  0.0 123.0 jit_solution(13559914899063544637)
XLA Ops:
  0.6 1.6 %broadcast_in_dim.3 = bf16[4,256,128]{2,1,0:T(8,128)(2,1)} broadcast(bf16[256,128]{1,0:T(8,128)(2,1)} %param.16), dimensions={1,2} | broadcast | bytes 327680 | tf_op jit(solution)/shard_map/weights/broadcast_in_dim | solution.py:198
  2.2 3.8 %all-to-all-start = ((bf16[4,256,128]{2,1,0:T(8,128)(2,1)}), bf16[4,256,128]{2,1,0:T(8,128)(2,1)S(1)}, u32[]{:S(2)}, u32[]{:S(2)}) async-start(bf16[4,256,128]{2,1,0:T(8,128)(2,1)} %broadcast_in_dim.3), calls=%async_computation | async-start | bytes 524288 | tf_op jit(solution)/shard_map/weights/all_to_all | solution.py:22
  6.0 3.0 %attention.4.refs_0_ = bf16[16,3,8,128]{3,2,1,0:T(8,128)(2,1)} custom-call(s32[4]{0:T(128)} %len_ref.3, bf16[4,4,4096]{2,1,0:T(4,128)(2,1)} %q_ref.3, bf16[4,16,128]{2,1,0:T(8,128)(2,1)} %bitcast.8, bf16[4,16,128]{2,1,0:T(8,128)(2,1)} %bitcast.10, bf16[4,1024,128]{2,1,0:T(8,128)(2,1)} %bitcast.4, bf16[4,1024,128]{2,1,0:T(8,128)(2,1)} %bitcast.6), custom_call_target="tpu_custom_call" | custom-call | flops 150000000 | bytes 1048576 | tf_op jit(solution)/shard_map/attention/pallas_call | solution.py:100
  9.0 1.3 %all-to-all-done = bf16[4,256,128]{2,1,0:T(8,128)(2,1)S(1)} async-done(((bf16[4,256,128]{2,1,0:T(8,128)(2,1)}), bf16[4,256,128]{2,1,0:T(8,128)(2,1)S(1)}, u32[]{:S(2)}, u32[]{:S(2)}) %all-to-all-start) | async-done | bytes 262176 | tf_op jit(solution)/shard_map/weights/all_to_all | solution.py:22
  10.3 1.9 %collective-permute-start = (bf16[4,256,128]{2,1,0:T(8,128)(2,1)S(1)}, bf16[4,256,128]{2,1,0:T(8,128)(2,1)S(1)}, u32[]{:S(2)}, u32[]{:S(2)}) collective-permute-start(bf16[4,256,128]{2,1,0:T(8,128)(2,1)S(1)} %all-to-all-done), channel_id=1, source_target_pairs={{0,0},{16,256},{32,512},{48,768},{64,16},{80,272},{96,528},{112,78... | collective-permute-start | bytes 786440 | tf_op jit(solution)/shard_map/attention/ppermute | solution.py:26
  12.2 3.2 %attention.5 = bf16[16,5,8,128]{3,2,1,0:T(8,128)(2,1)} custom-call(s32[4]{0:T(128)} %len_ref.3, bf16[4,4,4096]{2,1,0:T(4,128)(2,1)} %q_ref.3, bf16[4,16,128]{2,1,0:T(8,128)(2,1)} %bitcast.9, bf16[4,16,128]{2,1,0:T(8,128)(2,1)} %bitcast.11, bf16[4,1024,128]{2,1,0:T(8,128)(2,1)} %bitcast.5, bf16[4,1024,128]{2,1,0:T(8,128)(2,1)} %bitcast.7, ...), custom_call_target="tpu_custom_call" | custom-call | flops 150000000 | bytes 1048576 | tf_op jit(solution)/shard_map/attention/pallas_call | solution.py:100
  15.4 16.7 %all_to_all.25.parts_ref = bf16[16,5,8,128]{3,2,1,0:T(8,128)(2,1)S(1)} all-to-all(bf16[16,5,8,128]{3,2,1,0:T(8,128)(2,1)} %attention.5), channel_id=1, replica_groups=mesh['ra'=4,'rb'=4,'rc'=4,'tp'=16] {'tp'}, dimensions={0} | all-to-all | bytes 327680 | tf_op jit(solution)/shard_map/attention/all_to_all | solution.py:22
  32.1 0.9 attention.6
  33.0 20.8 %all-to-all-start.2 = ((bf16[16,16,256]{2,1,0:T(8,128)(2,1)}), bf16[16,16,256]{2,1,0:T(8,128)(2,1)S(1)}, u32[]{:S(2)}, u32[]{:S(2)}) async-start(bf16[16,16,256]{2,1,0:T(8,128)(2,1)} %attention.6), calls=%async_computation.2 | async-start | bytes 262144 | tf_op jit(solution)/shard_map/attention/all_to_all | solution.py:22
  53.8 0.0 collective-permute-done.blocks_ref
  53.9 10.6 %all-to-all-done.2.x_ref = bf16[16,16,256]{2,1,0:T(8,128)(2,1)S(1)} async-done(((bf16[16,16,256]{2,1,0:T(8,128)(2,1)}), bf16[16,16,256]{2,1,0:T(8,128)(2,1)S(1)}, u32[]{:S(2)}, u32[]{:S(2)}) %all-to-all-start.2) | async-done | bytes 131104 | tf_op jit(solution)/shard_map/attention/all_to_all | solution.py:22
  64.5 0.2 projection.2
  64.7 18.4 %all_to_all.26.parts_ref = bf16[16,16,512]{2,1,0:T(8,128)(2,1)S(1)} all-to-all(bf16[16,16,512]{2,1,0:T(8,128)(2,1)S(1)} %projection.2), channel_id=1, replica_groups=mesh['ra'=4,'rb'=4,'rc'=4,'tp'=16] {'tp'}, dimensions={0} | all-to-all | bytes 524288 | tf_op jit(solution)/shard_map/projection/all_to_all | solution.py:22
  83.1 0.0 copy-start
  83.1 1.9 %collective-permute-start.1 = (bf16[16,512]{1,0:T(8,128)(2,1)S(1)}, bf16[16,512]{1,0:T(8,128)(2,1)S(1)}, u32[]{:S(2)}, u32[]{:S(2)}) collective-permute-start(bf16[16,512]{1,0:T(8,128)(2,1)S(1)} %projection.3), channel_id=1, source_target_pairs={{0,0},{1,16},{2,32},{3,48},{4,64},{5,80},{6,96},{7,112},{8,128},{9... | collective-permute-start | bytes 49160 | tf_op jit(solution)/shard_map/projection/ppermute | solution.py:26
  85.0 3.1 %collective-permute-done.1.summed_ref = bf16[16,512]{1,0:T(8,128)(2,1)S(1)} collective-permute-done((bf16[16,512]{1,0:T(8,128)(2,1)S(1)}, bf16[16,512]{1,0:T(8,128)(2,1)S(1)}, u32[]{:S(2)}, u32[]{:S(2)}) %collective-permute-start.1) | collective-permute-done | bytes 16416 | tf_op jit(solution)/shard_map/projection/ppermute | solution.py:26
  88.2 0.0 copy-done
  88.2 0.7 norm.2
  88.8 0.0 copy-start.1
  88.8 25.8 %all-to-all-start.4 = ((f32[16,16,128]{2,1,0:T(8,128)}), f32[16,16,128]{2,1,0:T(8,128)S(1)}, u32[]{:S(2)}, u32[]{:S(2)}) async-start(f32[16,16,128]{2,1,0:T(8,128)} %get-tuple-element.8), calls=%async_computation.4 | async-start | bytes 262144 | tf_op jit(solution)/shard_map/norm/all_to_all | solution.py:22
  114.7 0.0 copy-done.1
  114.7 7.6 %all-to-all-done.4.squares_ref = f32[16,16,128]{2,1,0:T(8,128)S(1)} async-done(((f32[16,16,128]{2,1,0:T(8,128)}), f32[16,16,128]{2,1,0:T(8,128)S(1)}, u32[]{:S(2)}, u32[]{:S(2)}) %all-to-all-start.4) | async-done | bytes 131104 | tf_op jit(solution)/shard_map/norm/all_to_all | solution.py:22
  122.3 0.7 norm.3
  (3 shorter events, 0.1 us)
Async XLA Ops:
  2.2 8.1 %all-to-all-start = ((bf16[4,256,128]{2,1,0:T(8,128)(2,1)}), bf16[4,256,128]{2,1,0:T(8,128)(2,1)S(1)}, u32[]{:S(2)}, u32[]{:S(2)}) async-start(bf16[4,256,128]{2,1,0:T(8,128)(2,1)} %broadcast_in_dim.3), calls=%async_computation | async-start | bytes 524288 | tf_op jit(solution)/shard_map/weights/all_to_all | solution.py:22
  10.3 43.5 %collective-permute-start = (bf16[4,256,128]{2,1,0:T(8,128)(2,1)S(1)}, bf16[4,256,128]{2,1,0:T(8,128)(2,1)S(1)}, u32[]{:S(2)}, u32[]{:S(2)}) collective-permute-start(bf16[4,256,128]{2,1,0:T(8,128)(2,1)S(1)} %all-to-all-done), channel_id=1, source_target_pairs={{0,0},{16,256},{32,512},{48,768},{64,16},{80,272},{96,528},{112,78... | collective-permute-start | bytes 786440 | tf_op jit(solution)/shard_map/attention/ppermute | solution.py:26
  33.0 31.5 %all-to-all-start.2 = ((bf16[16,16,256]{2,1,0:T(8,128)(2,1)}), bf16[16,16,256]{2,1,0:T(8,128)(2,1)S(1)}, u32[]{:S(2)}, u32[]{:S(2)}) async-start(bf16[16,16,256]{2,1,0:T(8,128)(2,1)} %attention.6), calls=%async_computation.2 | async-start | bytes 262144 | tf_op jit(solution)/shard_map/attention/all_to_all | solution.py:22
  83.1 5.1 %copy-start = (bf16[4,4,512]{2,1,0:T(4,128)(2,1)S(1)}, bf16[4,4,512]{2,1,0:T(4,128)(2,1)}, u32[]{:S(2)}) copy-start(bf16[4,4,512]{2,1,0:T(4,128)(2,1)} %stream_ref.1) | copy-start | bytes 49156
  83.1 5.1 %collective-permute-start.1 = (bf16[16,512]{1,0:T(8,128)(2,1)S(1)}, bf16[16,512]{1,0:T(8,128)(2,1)S(1)}, u32[]{:S(2)}, u32[]{:S(2)}) collective-permute-start(bf16[16,512]{1,0:T(8,128)(2,1)S(1)} %projection.3), channel_id=1, source_target_pairs={{0,0},{1,16},{2,32},{3,48},{4,64},{5,80},{6,96},{7,112},{8,128},{9... | collective-permute-start | bytes 49160 | tf_op jit(solution)/shard_map/projection/ppermute | solution.py:26
  88.8 25.8 %copy-start.1 = (bf16[512]{0:T(512)(128)(2,1)S(1)}, bf16[512]{0:T(512)(128)(2,1)}, u32[]{:S(2)}) copy-start(bf16[512]{0:T(512)(128)(2,1)} %param.17) | copy-start | bytes 3076
  88.8 33.5 %all-to-all-start.4 = ((f32[16,16,128]{2,1,0:T(8,128)}), f32[16,16,128]{2,1,0:T(8,128)S(1)}, u32[]{:S(2)}, u32[]{:S(2)}) async-start(f32[16,16,128]{2,1,0:T(8,128)} %get-tuple-element.8), calls=%async_computation.4 | async-start | bytes 262144 | tf_op jit(solution)/shard_map/norm/all_to_all | solution.py:22

commit v7 on v6

--- a/solution.py
+++ b/solution.py
@@ -34,10 +34,15 @@
     return jnp.concatenate(pieces, axis=axis)
 
 
-def attend_kernel(first, len_ref, q_ref, nk_ref, nv_ref, k_ref, v_ref, *refs):
+def tiled(wide):
+    rows, columns = wide.shape
+    cut = [wide[:, j : j + 128].reshape(rows, 1, 128) for j in range(0, columns, 128)]
+    return stacked([*cut, jnp.zeros((rows, 8 - len(cut), 128), wide.dtype)], 1)
+
+
+def attend_kernel(first, last, len_ref, q_ref, nk_ref, nv_ref, k_ref, v_ref, *refs):
     *earlier_ref, out_ref, stats_ref = refs
     b = first + pl.program_id(0)
-    rows_b = out_ref.shape[1] - 1
     _, steps, width = q_ref.shape
     head_dim = k_ref.shape[2]
     kv_heads = nk_ref.shape[1] // steps
@@ -79,6 +84,8 @@
         @pl.when(b == first)
         def _():
             out_ref[:, :first] = earlier_ref[0][:, :first]
+            stream = stacked([earlier_ref[1][r].astype(F32) for r in range(last)])
+            out_ref[:, last + 1] = tiled(stream).astype(BF16)
 
     else:
         earlier = jnp.zeros((rows, head_dim), F32)
@@ -87,18 +94,22 @@
     stats = jnp.where(lane == 3 * b + 1, high, stats)
     stats = jnp.where(lane == 3 * b + 2, total - high, stats)
     stats_ref[...] = stats
-    out_ref[:, rows_b] = stats.astype(BF16).reshape(-1, 8, head_dim)
+    out_ref[:, last] = stats.astype(BF16).reshape(-1, 8, head_dim)
+
+
+def zeros(count, _):
+    return (0,) * count
 
 
 def attend(queries, new_keys, new_values, keys, values, lengths, first, last, *earlier):
     arrays = (queries, new_keys, new_values, keys, values)
     head_dim = keys.shape[2]
     pieces = queries.shape[2] * queries.shape[1] // head_dim // 8
-    outs = jax.ShapeDtypeStruct((pieces, last + 1, 8, head_dim), BF16)
+    outs = jax.ShapeDtypeStruct((pieces, last + 1 + (len(earlier) > 1), 8, head_dim), BF16)
     whole = pl.BlockSpec(outs.shape, lambda b: (0, 0, 0, 0))
-    before = [pl.BlockSpec(a.shape, lambda b: (0, 0, 0, 0)) for a in earlier]
+    before = [pl.BlockSpec(a.shape, functools.partial(zeros, a.ndim)) for a in earlier]
     return pl.pallas_call(
-        functools.partial(attend_kernel, first),
+        functools.partial(attend_kernel, first, last),
         grid=(last - first,),
         out_shape=outs,
         in_specs=[
@@ -115,8 +126,8 @@
     )(lengths, *arrays, *earlier)
 
 
-def combine_kernel(parts_ref, out_ref):
-    rows_b = parts_ref.shape[1] - 1
+def combine_kernel(parts_ref, out_ref, stream_ref):
+    rows_b = parts_ref.shape[1] - 2
     half = parts_ref.shape[2] // 2
     stats = parts_ref[:, rows_b].astype(F32)
     first, second = [], []
@@ -131,6 +142,7 @@
     attended = stacked([stacked(first), stacked(second)], 1).astype(BF16)
     for i in range(out_ref.shape[0]):
         out_ref[i] = attended
+    stream_ref[...] = parts_ref[:, rows_b + 1].astype(F32)
 
 
 def side_by_side_kernel(blocks_ref, out_ref):
@@ -139,30 +151,29 @@
 
 
 def project_kernel(x_ref, w_ref, out_ref):
-    x = x_ref[...].reshape(-1, x_ref.shape[2])
-    projected = jnp.dot(x, w_ref[...], preferred_element_type=F32)
+    x = jnp.swapaxes(x_ref[...].astype(F32), 0, 1).astype(BF16)
+    projected = jnp.dot(x.reshape(-1, x.shape[2]), w_ref[...], preferred_element_type=F32)
     out_ref[...] = projected.astype(BF16).reshape(out_ref.shape)
 
 
 def sum_kernel(parts_ref, out_ref):
-    out_ref[...] = jnp.sum(parts_ref[...].astype(F32), axis=0).astype(BF16)
-
-
-def hidden_kernel(summed_ref, stream_ref, hidden_ref, squares_ref):
-    stream = stacked([stream_ref[b].astype(F32) for b in range(stream_ref.shape[0])])
-    hidden = stream + summed_ref[...].astype(F32)
-    hidden_ref[...] = hidden
-    squares = hidden * hidden
-    squares = sum(squares[:, j : j + 128] for j in range(0, squares.shape[1], 128))
-    for i in range(squares_ref.shape[0]):
-        squares_ref[i] = squares
-
-
-def norm_kernel(squares_ref, hidden_ref, gain_ref, stream_ref, normed_ref):
-    squares = jnp.sum(jnp.sum(squares_ref[...], axis=0), axis=1, keepdims=True)
-    hidden = hidden_ref[...]
-    normed = hidden * lax.rsqrt(squares / D + 1e-06) * gain_ref[...].astype(F32)
-    rows_b, steps, _ = stream_ref.shape
+    out_ref[...] = tiled(jnp.sum(parts_ref[...].astype(F32), axis=0))
+
+
+def hidden_kernel(summed_ref, stream_ref, out_ref):
+    hidden = summed_ref[...] + stream_ref[...]
+    squares = jnp.sum(hidden * hidden, axis=0)
+    squares = jnp.sum(jnp.sum(squares, axis=0, keepdims=True), axis=1, keepdims=True)
+    inverse = lax.rsqrt(squares / D + 1e-06).reshape(1, 1, 1)
+    line = lax.broadcasted_iota(jnp.int32, hidden.shape, 1)
+    out_ref[...] = jnp.where(line == hidden.shape[1] - 1, inverse, hidden)
+
+
+def norm_kernel(tiles_ref, gain_ref, stream_ref, normed_ref):
+    rows_b, steps, columns = stream_ref.shape
+    hidden = stacked([tiles_ref[:, j, :] for j in range(columns // 128)], 1)
+    inverse = tiles_ref[:, tiles_ref.shape[1] - 1, :][:, :1]
+    normed = hidden * inverse * gain_ref[...].astype(F32)
     for b in range(rows_b):
         stream_ref[b] = hidden[b * steps : (b + 1) * steps].astype(BF16)
         normed_ref[b] = normed[b * steps : (b + 1) * steps].astype(BF16)
@@ -203,41 +214,30 @@
         half = rows_b // 2
         parts = attend(queries, *cached, lengths, 0, half)
         parts, quad = lax.optimization_barrier((parts, quad))
-        parts = attend(queries, *cached, lengths, half, rows_b, parts)
+        parts = attend(queries, *cached, lengths, half, rows_b, parts, stream_in)
         weight = permuted(quad, REP, n_rep, lambda r: (r % n_quad) * n_arc + r // n_quad)
         weight = call(
             side_by_side_kernel, jax.ShapeDtypeStruct((share, columns), BF16), weight, flops=20_000_000_000
         )
         parts = exchanged(parts, "tp")
-        attended = call(combine_kernel, jax.ShapeDtypeStruct((n_arc, rows, share), BF16), parts)
+        tiles = jax.ShapeDtypeStruct((n_tp, 8, 128), F32)
+        attended, stream = call(
+            combine_kernel, [jax.ShapeDtypeStruct((n_arc, rows, share), BF16), tiles], parts
+        )
         attended = exchanged(attended, ARC)
 
     with jax.named_scope("projection"):
         projected = call(
-            project_kernel, jax.ShapeDtypeStruct((n_arc, rows, columns), BF16), attended, weight,
+            project_kernel, jax.ShapeDtypeStruct((rows, n_arc, columns), BF16), attended, weight,
             flops=2 * n_arc * rows * share * columns,
         )
         partials = exchanged(projected, "tp")
-        summed = call(sum_kernel, jax.ShapeDtypeStruct((rows, columns), BF16), partials)
-
-        def home(i):
-            r, p = i // n_tp, i % n_tp
-            return (r // n_arc * n_arc + p) * n_tp + r % n_arc
-
-        summed = permuted(summed, (*REP, "tp"), n_rep * n_tp, home)
+        summed = exchanged(call(sum_kernel, tiles, partials), ARC)
 
     with jax.named_scope("norm"):
-        hidden, squares = call(
-            hidden_kernel,
-            [
-                jax.ShapeDtypeStruct((rows, columns), F32),
-                jax.ShapeDtypeStruct((n_tp, rows, 128), F32),
-            ],
-            summed, stream_in,
-        )
-        squares = exchanged(squares, "tp")
+        hidden = exchanged(call(hidden_kernel, tiles, summed, stream), "tp")
         out = jax.ShapeDtypeStruct(stream_in.shape, BF16)
-        return tuple(call(norm_kernel, [out, out], squares, hidden, norm_gain.reshape(1, -1)))
+        return tuple(call(norm_kernel, [out, out], hidden, norm_gain.reshape(1, -1)))
 
 
 def solution(mesh):

time: 124 us -> 129 us (1.040)
  blocking collectives: 35 us -> 63.3 us
  starting transfers between devices: 54.3 us -> 34.7 us
  waiting for transfers between devices: 22.6 us -> 19.2 us
    all_to_all x2 -> x3, blocking collectives: 35 us -> 63.3 us  [exchanged(): return lax.all_to_all(pieces, axes, split_axis=0, concat_axis=0, tiled=True)]
    all_to_all x3, starting transfers between devices: 50.5 us -> 32.8 us  [exchanged(): return lax.all_to_all(pieces, axes, split_axis=0, concat_axis=0, tiled=True)]
    ppermute x2 -> x1, waiting for transfers between devices: 3.13 us -> 0.01 us  [permuted(): return lax.ppermute(array, axes, [(i, target(i)) for i in range(count)])]
    ppermute x2 -> x1, starting transfers between devices: 3.83 us -> 1.91 us  [permuted(): return lax.ppermute(array, axes, [(i, target(i)) for i in range(count)])]
  transfers between devices with their start and end apart: 5 -> 4, of which waited for: 4 -> 3; matrix products, arithmetic and copies ran while one was open for 0% -> 0% of each run, Pallas kernels for 6% -> 6%
where the time goes in v7:
time: 129 us; the launch traced here: 128 us
  blocking collectives  63.3 us (49%)
  starting transfers between devices  34.7 us (27%)
  waiting for transfers between devices  19.2 us (15%)
  Pallas kernels  8.92 us (7%)
  local copies, waits for them, and re-layouts  1.58 us (1%)
    all_to_all x3, blocking collectives, exchanged(): return lax.all_to_all(pieces, axes, split_axis=0, concat_axis=0, tiled=True)  63.3 us
    all_to_all x3, starting transfers between devices, exchanged(): return lax.all_to_all(pieces, axes, split_axis=0, concat_axis=0, tiled=True)  32.8 us
    all_to_all x3, waiting for transfers between devices, exchanged(): return lax.all_to_all(pieces, axes, split_axis=0, concat_axis=0, tiled=True)  19.2 us
    pallas_call x2, Pallas kernels, attend(): pl.pallas_call(functools.partial(attend_kernel, first, last), grid=(last...  6.22 us
    pallas_call x6, Pallas kernels, call(): pl.pallas_call(kernel, out_shape=outs, in_specs=[vmem] * len(args), out_s...  2.7 us
  transfers between devices with their start and end apart: 4, of which 3 were waited for; matrix products, arithmetic and copies ran while one was open for 0% of the time, Pallas kernels for 6%

profile of v7, /device:TPU:257, one launch (start us, length us, event | category | flops | bytes accessed | tf_op | source)
XLA Modules:
  0.0 128.5 jit_solution(1824684781314303070)
XLA Ops:
  0.6 1.6 %broadcast_in_dim.3 = bf16[4,256,128]{2,1,0:T(8,128)(2,1)} broadcast(bf16[256,128]{1,0:T(8,128)(2,1)} %param.16), dimensions={1,2} | broadcast | bytes 327680 | tf_op jit(solution)/shard_map/weights/broadcast_in_dim | solution.py:209
  2.2 3.8 %all-to-all-start = ((bf16[4,256,128]{2,1,0:T(8,128)(2,1)}), bf16[4,256,128]{2,1,0:T(8,128)(2,1)S(1)}, u32[]{:S(2)}, u32[]{:S(2)}) async-start(bf16[4,256,128]{2,1,0:T(8,128)(2,1)} %broadcast_in_dim.3), calls=%async_computation | async-start | bytes 524288 | tf_op jit(solution)/shard_map/weights/all_to_all | solution.py:22
  6.0 3.0 %attention.4.refs_0_ = bf16[16,3,8,128]{3,2,1,0:T(8,128)(2,1)} custom-call(s32[4]{0:T(128)} %len_ref.3, bf16[4,4,4096]{2,1,0:T(4,128)(2,1)} %q_ref.3, bf16[4,16,128]{2,1,0:T(8,128)(2,1)} %bitcast.8, bf16[4,16,128]{2,1,0:T(8,128)(2,1)} %bitcast.10, bf16[4,1024,128]{2,1,0:T(8,128)(2,1)} %bitcast.4, bf16[4,1024,128]{2,1,0:T(8,128)(2,1)} %bitcast.6), custom_call_target="tpu_custom_call" | custom-call | flops 150000000 | bytes 1048576 | tf_op jit(solution)/shard_map/attention/pallas_call | solution.py:111
  9.0 1.3 all-to-all-done
  10.3 1.9 %collective-permute-start = (bf16[4,256,128]{2,1,0:T(8,128)(2,1)S(1)}, bf16[4,256,128]{2,1,0:T(8,128)(2,1)S(1)}, u32[]{:S(2)}, u32[]{:S(2)}) collective-permute-start(bf16[4,256,128]{2,1,0:T(8,128)(2,1)S(1)} %all-to-all-done), channel_id=1, source_target_pairs={{0,0},{16,256},{32,512},{48,768},{64,16},{80,272},{96,528},{112,78... | collective-permute-start | bytes 786440 | tf_op jit(solution)/shard_map/attention/ppermute | solution.py:26
  12.2 3.2 %attention.5 = bf16[16,6,8,128]{3,2,1,0:T(8,128)(2,1)} custom-call(s32[4]{0:T(128)} %len_ref.3, bf16[4,4,4096]{2,1,0:T(4,128)(2,1)} %q_ref.3, bf16[4,16,128]{2,1,0:T(8,128)(2,1)} %bitcast.9, bf16[4,16,128]{2,1,0:T(8,128)(2,1)} %bitcast.11, bf16[4,1024,128]{2,1,0:T(8,128)(2,1)} %bitcast.5, bf16[4,1024,128]{2,1,0:T(8,128)(2,1)} %bitcast.7, ...), custom_call_target="tpu_custom_call" | custom-call | flops 150000000 | bytes 1048576 | tf_op jit(solution)/shard_map/attention/pallas_call | solution.py:111
  15.4 16.9 %all_to_all.30.parts_ref = bf16[16,6,8,128]{3,2,1,0:T(8,128)(2,1)S(1)} all-to-all(bf16[16,6,8,128]{3,2,1,0:T(8,128)(2,1)} %attention.5), channel_id=1, replica_groups=mesh['ra'=4,'rb'=4,'rc'=4,'tp'=16] {'tp'}, dimensions={0} | all-to-all | bytes 393216 | tf_op jit(solution)/shard_map/attention/all_to_all | solution.py:22
  32.3 0.9 attention.6
  33.2 23.2 %all-to-all-start.2 = ((bf16[16,16,256]{2,1,0:T(8,128)(2,1)}), bf16[16,16,256]{2,1,0:T(8,128)(2,1)S(1)}, u32[]{:S(2)}, u32[]{:S(2)}) async-start(bf16[16,16,256]{2,1,0:T(8,128)(2,1)} %get-tuple-element.7), calls=%async_computation.2 | async-start | bytes 262144 | tf_op jit(solution)/shard_map/attention/all_to_all | solution.py:22
  56.4 0.0 collective-permute-done.blocks_ref
  56.5 10.6 %all-to-all-done.2.x_ref = bf16[16,16,256]{2,1,0:T(8,128)(2,1)S(1)} async-done(((bf16[16,16,256]{2,1,0:T(8,128)(2,1)}), bf16[16,16,256]{2,1,0:T(8,128)(2,1)S(1)}, u32[]{:S(2)}, u32[]{:S(2)}) %all-to-all-start.2) | async-done | bytes 131104 | tf_op jit(solution)/shard_map/attention/all_to_all | solution.py:22
  67.1 0.2 projection.2
  67.3 15.8 %all_to_all.31.parts_ref = bf16[16,16,512]{2,1,0:T(8,128)(2,1)S(1)} all-to-all(bf16[16,16,512]{2,1,0:T(8,128)(2,1)S(1)} %projection.2), channel_id=1, replica_groups=mesh['ra'=4,'rb'=4,'rc'=4,'tp'=16] {'tp'}, dimensions={0} | all-to-all | bytes 524288 | tf_op jit(solution)/shard_map/projection/all_to_all | solution.py:22
  83.1 0.1 projection.3
  83.2 30.6 %all_to_all.32.summed_ref = f32[16,8,128]{2,1,0:T(8,128)S(1)} all-to-all(f32[16,8,128]{2,1,0:T(8,128)S(1)} %projection.3), channel_id=1, replica_groups=mesh['ra'=4,'rb'=4,'rc'=4,'tp'=16] {'rb','rc'}, dimensions={0} | all-to-all | bytes 131072 | tf_op jit(solution)/shard_map/projection/all_to_all | solution.py:22
  113.8 0.7 norm.2
  114.6 0.0 copy-start
  114.6 5.8 %all-to-all-start.5 = ((f32[16,8,128]{2,1,0:T(8,128)}), f32[16,8,128]{2,1,0:T(8,128)S(1)}, u32[]{:S(2)}, u32[]{:S(2)}) async-start(f32[16,8,128]{2,1,0:T(8,128)} %norm.2), calls=%async_computation.5 | async-start | bytes 131072 | tf_op jit(solution)/shard_map/norm/all_to_all | solution.py:22
  120.4 0.0 copy-done
  120.4 7.4 %all-to-all-done.5.tiles_ref = f32[16,8,128]{2,1,0:T(8,128)S(1)} async-done(((f32[16,8,128]{2,1,0:T(8,128)}), f32[16,8,128]{2,1,0:T(8,128)S(1)}, u32[]{:S(2)}, u32[]{:S(2)}) %all-to-all-start.5) | async-done | bytes 65568 | tf_op jit(solution)/shard_map/norm/all_to_all | solution.py:22
  127.8 0.7 norm.3
  (2 shorter events, 0.1 us)
Async XLA Ops:
  2.2 8.1 %all-to-all-start = ((bf16[4,256,128]{2,1,0:T(8,128)(2,1)}), bf16[4,256,128]{2,1,0:T(8,128)(2,1)S(1)}, u32[]{:S(2)}, u32[]{:S(2)}) async-start(bf16[4,256,128]{2,1,0:T(8,128)(2,1)} %broadcast_in_dim.3), calls=%async_computation | async-start | bytes 524288 | tf_op jit(solution)/shard_map/weights/all_to_all | solution.py:22
  10.3 46.2 %collective-permute-start = (bf16[4,256,128]{2,1,0:T(8,128)(2,1)S(1)}, bf16[4,256,128]{2,1,0:T(8,128)(2,1)S(1)}, u32[]{:S(2)}, u32[]{:S(2)}) collective-permute-start(bf16[4,256,128]{2,1,0:T(8,128)(2,1)S(1)} %all-to-all-done), channel_id=1, source_target_pairs={{0,0},{16,256},{32,512},{48,768},{64,16},{80,272},{96,528},{112,78... | collective-permute-start | bytes 786440 | tf_op jit(solution)/shard_map/attention/ppermute | solution.py:26
  33.2 33.8 %all-to-all-start.2 = ((bf16[16,16,256]{2,1,0:T(8,128)(2,1)}), bf16[16,16,256]{2,1,0:T(8,128)(2,1)S(1)}, u32[]{:S(2)}, u32[]{:S(2)}) async-start(bf16[16,16,256]{2,1,0:T(8,128)(2,1)} %get-tuple-element.7), calls=%async_computation.2 | async-start | bytes 262144 | tf_op jit(solution)/shard_map/attention/all_to_all | solution.py:22
  114.6 5.8 %copy-start = (bf16[512]{0:T(512)(128)(2,1)S(1)}, bf16[512]{0:T(512)(128)(2,1)}, u32[]{:S(2)}) copy-start(bf16[512]{0:T(512)(128)(2,1)} %param.17) | copy-start | bytes 3076
  114.6 13.2 %all-to-all-start.5 = ((f32[16,8,128]{2,1,0:T(8,128)}), f32[16,8,128]{2,1,0:T(8,128)S(1)}, u32[]{:S(2)}, u32[]{:S(2)}) async-start(f32[16,8,128]{2,1,0:T(8,128)} %norm.2), calls=%async_computation.5 | async-start | bytes 131072 | tf_op jit(solution)/shard_map/norm/all_to_all | solution.py:22

commit v8 on v2

--- a/solution.py
+++ b/solution.py
@@ -179,6 +179,17 @@
     columns = stream_in.shape[2]
     share = width // n_tp
 
+    def place_of(arc, quad):
+        return (quad - arc * n_quad + 6) % n_arc
+
+    def columns_of(arc, place):
+        return (place - 6 + arc * n_quad) % n_arc
+
+    def weight_home(r):
+        quad, member = r // n_quad, r % n_quad
+        arc = (quad // n_quad - member) % n_quad
+        return arc * n_arc + place_of(arc, quad)
+
     with jax.named_scope("weights"):
         quad = exchanged(jnp.broadcast_to(out_weight, (n_quad, *out_weight.shape)), QUAD)
 
@@ -189,7 +200,7 @@
             jax.ShapeDtypeStruct((n_tp, rows_b + 1, 8, head_dim), BF16),
         )
         parts, quad = lax.optimization_barrier((parts, quad))
-        weight = permuted(quad, REP, n_rep, lambda r: (r % n_quad) * n_arc + r // n_quad)
+        weight = permuted(quad, REP, n_rep, weight_home)
         weight = call(
             side_by_side_kernel, jax.ShapeDtypeStruct((share, columns), BF16), weight, flops=20_000_000_000
         )
@@ -206,8 +217,8 @@
         summed = call(sum_kernel, jax.ShapeDtypeStruct((rows, columns), BF16), partials)
 
         def home(i):
-            r, p = i // n_tp, i % n_tp
-            return (r // n_arc * n_arc + p) * n_tp + r % n_arc
+            arc, place, p = i // (n_arc * n_tp), i // n_tp % n_arc, i % n_tp
+            return (arc * n_arc + p) * n_tp + columns_of(arc, place)
 
         summed = permuted(summed, (*REP, "tp"), n_rep * n_tp, home)
 

time: 124 us -> 113 us (0.911)
  the two profiles are of different devices: /device:TPU:257 before, /device:TPU:1 now
where the time goes in v8:
time: 113 us; the launch traced here: 112 us
  starting transfers between devices  45 us (40%)
  blocking collectives  34.8 us (31%)
  waiting for transfers between devices  22.5 us (20%)
  Pallas kernels  7.33 us (6%)
  local copies, waits for them, and re-layouts  1.6 us (1%)
    all_to_all x3, starting transfers between devices, exchanged(): return lax.all_to_all(pieces, axes, split_axis=0, concat_axis=0, tiled=True)  35.5 us
    all_to_all x2, blocking collectives, exchanged(): return lax.all_to_all(pieces, axes, split_axis=0, concat_axis=0, tiled=True)  34.8 us
    all_to_all x3, waiting for transfers between devices, exchanged(): return lax.all_to_all(pieces, axes, split_axis=0, concat_axis=0, tiled=True)  18.2 us
    ppermute x2, starting transfers between devices, permuted(): return lax.ppermute(array, axes, [(i, target(i)) for i in range(count)])  9.59 us
    pallas_call x1, Pallas kernels, attend(): pl.pallas_call(attend_kernel, grid=(queries.shape[0],), out_shape=outs, i...  4.74 us
    ppermute x2, waiting for transfers between devices, permuted(): return lax.ppermute(array, axes, [(i, target(i)) for i in range(count)])  4.23 us
    pallas_call x6, Pallas kernels, call(): pl.pallas_call(kernel, out_shape=outs, in_specs=[vmem] * len(args), out_s...  2.58 us
  transfers between devices with their start and end apart: 5, of which 3 were waited for; matrix products, arithmetic and copies ran while one was open for 0% of the time, Pallas kernels for 5%

profile of v8, /device:TPU:1, one launch (start us, length us, event | category | flops | bytes accessed | tf_op | source)
XLA Modules:
  0.0 112.0 jit_solution(11279196924825260648)
XLA Ops:
  0.6 1.6 %broadcast_in_dim.3 = bf16[4,256,128]{2,1,0:T(8,128)(2,1)} broadcast(bf16[256,128]{1,0:T(8,128)(2,1)} %param.16), dimensions={1,2} | broadcast | bytes 327680 | tf_op jit(solution)/shard_map/weights/broadcast_in_dim | solution.py:194
  2.2 4.7 %all-to-all-start = ((bf16[4,256,128]{2,1,0:T(8,128)(2,1)}), bf16[4,256,128]{2,1,0:T(8,128)(2,1)S(1)}, u32[]{:S(2)}, u32[]{:S(2)}) async-start(bf16[4,256,128]{2,1,0:T(8,128)(2,1)} %broadcast_in_dim.3), calls=%async_computation | async-start | bytes 524288 | tf_op jit(solution)/shard_map/weights/all_to_all | solution.py:21
  6.9 4.7 %attention.3 = bf16[16,5,8,128]{3,2,1,0:T(8,128)(2,1)} custom-call(s32[4]{0:T(128)} %len_ref.1, bf16[4,4,4096]{2,1,0:T(4,128)(2,1)} %q_ref.1, bf16[4,16,128]{2,1,0:T(8,128)(2,1)} %bitcast.6, bf16[4,16,128]{2,1,0:T(8,128)(2,1)} %bitcast.7, bf16[4,1024,128]{2,1,0:T(8,128)(2,1)} %bitcast.4, bf16[4,1024,128]{2,1,0:T(8,128)(2,1)} %bitcast.5), custom_call_target="tpu_custom_call" | custom-call | flops 300000000 | bytes 2097152 | tf_op jit(solution)/shard_map/attention/pallas_call | solution.py:86
  11.6 0.0 all-to-all-done
  11.6 6.1 %collective-permute-start = (bf16[4,256,128]{2,1,0:T(8,128)(2,1)S(1)}, bf16[4,256,128]{2,1,0:T(8,128)(2,1)S(1)}, u32[]{:S(2)}, u32[]{:S(2)}) collective-permute-start(bf16[4,256,128]{2,1,0:T(8,128)(2,1)S(1)} %all-to-all-done), channel_id=1, source_target_pairs={{0,96},{16,928},{32,736},{48,288},{64,112},{80,944},{96,752},{112,... | collective-permute-start | bytes 786440 | tf_op jit(solution)/shard_map/attention/ppermute | solution.py:25
  17.7 20.6 %all_to_all.25.parts_ref = bf16[16,5,8,128]{3,2,1,0:T(8,128)(2,1)S(1)} all-to-all(bf16[16,5,8,128]{3,2,1,0:T(8,128)(2,1)} %attention.3), channel_id=1, replica_groups=mesh['ra'=4,'rb'=4,'rc'=4,'tp'=16] {'tp'}, dimensions={0} | all-to-all | bytes 327680 | tf_op jit(solution)/shard_map/attention/all_to_all | solution.py:21
  38.3 0.9 attention.4
  39.2 20.9 %all-to-all-start.2 = ((bf16[16,16,256]{2,1,0:T(8,128)(2,1)}), bf16[16,16,256]{2,1,0:T(8,128)(2,1)S(1)}, u32[]{:S(2)}, u32[]{:S(2)}) async-start(bf16[16,16,256]{2,1,0:T(8,128)(2,1)} %attention.4), calls=%async_computation.2 | async-start | bytes 262144 | tf_op jit(solution)/shard_map/attention/all_to_all | solution.py:21
  60.1 0.0 collective-permute-done.blocks_ref
  60.2 10.6 %all-to-all-done.2.x_ref = bf16[16,16,256]{2,1,0:T(8,128)(2,1)S(1)} async-done(((bf16[16,16,256]{2,1,0:T(8,128)(2,1)}), bf16[16,16,256]{2,1,0:T(8,128)(2,1)S(1)}, u32[]{:S(2)}, u32[]{:S(2)}) %all-to-all-start.2) | async-done | bytes 131104 | tf_op jit(solution)/shard_map/attention/all_to_all | solution.py:21
  70.8 0.2 projection.2
  71.0 14.2 %all_to_all.26.parts_ref = bf16[16,16,512]{2,1,0:T(8,128)(2,1)S(1)} all-to-all(bf16[16,16,512]{2,1,0:T(8,128)(2,1)S(1)} %projection.2), channel_id=1, replica_groups=mesh['ra'=4,'rb'=4,'rc'=4,'tp'=16] {'tp'}, dimensions={0} | all-to-all | bytes 524288 | tf_op jit(solution)/shard_map/projection/all_to_all | solution.py:21
  85.2 0.0 copy-start
  85.2 3.5 %collective-permute-start.1 = (bf16[16,512]{1,0:T(8,128)(2,1)S(1)}, bf16[16,512]{1,0:T(8,128)(2,1)S(1)}, u32[]{:S(2)}, u32[]{:S(2)}) collective-permute-start(bf16[16,512]{1,0:T(8,128)(2,1)S(1)} %projection.3), channel_id=1, source_target_pairs={{0,10},{1,26},{2,42},{3,58},{4,74},{5,90},{6,106},{7,122},{8,138},... | collective-permute-start | bytes 49160 | tf_op jit(solution)/shard_map/projection/ppermute | solution.py:25
  88.8 4.2 %collective-permute-done.1.summed_ref = bf16[16,512]{1,0:T(8,128)(2,1)S(1)} collective-permute-done((bf16[16,512]{1,0:T(8,128)(2,1)S(1)}, bf16[16,512]{1,0:T(8,128)(2,1)S(1)}, u32[]{:S(2)}, u32[]{:S(2)}) %collective-permute-start.1) | collective-permute-done | bytes 16416 | tf_op jit(solution)/shard_map/projection/ppermute | solution.py:25
  93.0 0.0 copy-done
  93.0 0.7 norm.2
  93.7 0.0 copy-start.1
  93.7 9.9 %all-to-all-start.4 = ((f32[16,16,128]{2,1,0:T(8,128)}), f32[16,16,128]{2,1,0:T(8,128)S(1)}, u32[]{:S(2)}, u32[]{:S(2)}) async-start(f32[16,16,128]{2,1,0:T(8,128)} %get-tuple-element.8), calls=%async_computation.4 | async-start | bytes 262144 | tf_op jit(solution)/shard_map/norm/all_to_all | solution.py:21
  103.6 0.0 copy-done.1
  103.6 7.6 %all-to-all-done.4.squares_ref = f32[16,16,128]{2,1,0:T(8,128)S(1)} async-done(((f32[16,16,128]{2,1,0:T(8,128)}), f32[16,16,128]{2,1,0:T(8,128)S(1)}, u32[]{:S(2)}, u32[]{:S(2)}) %all-to-all-start.4) | async-done | bytes 131104 | tf_op jit(solution)/shard_map/norm/all_to_all | solution.py:21
  111.3 0.7 norm.3
  (3 shorter events, 0.1 us)
Async XLA Ops:
  2.2 9.4 %all-to-all-start = ((bf16[4,256,128]{2,1,0:T(8,128)(2,1)}), bf16[4,256,128]{2,1,0:T(8,128)(2,1)S(1)}, u32[]{:S(2)}, u32[]{:S(2)}) async-start(bf16[4,256,128]{2,1,0:T(8,128)(2,1)} %broadcast_in_dim.3), calls=%async_computation | async-start | bytes 524288 | tf_op jit(solution)/shard_map/weights/all_to_all | solution.py:21
  11.6 48.5 %collective-permute-start = (bf16[4,256,128]{2,1,0:T(8,128)(2,1)S(1)}, bf16[4,256,128]{2,1,0:T(8,128)(2,1)S(1)}, u32[]{:S(2)}, u32[]{:S(2)}) collective-permute-start(bf16[4,256,128]{2,1,0:T(8,128)(2,1)S(1)} %all-to-all-done), channel_id=1, source_target_pairs={{0,96},{16,928},{32,736},{48,288},{64,112},{80,944},{96,752},{112,... | collective-permute-start | bytes 786440 | tf_op jit(solution)/shard_map/attention/ppermute | solution.py:25
  39.2 31.5 %all-to-all-start.2 = ((bf16[16,16,256]{2,1,0:T(8,128)(2,1)}), bf16[16,16,256]{2,1,0:T(8,128)(2,1)S(1)}, u32[]{:S(2)}, u32[]{:S(2)}) async-start(bf16[16,16,256]{2,1,0:T(8,128)(2,1)} %attention.4), calls=%async_computation.2 | async-start | bytes 262144 | tf_op jit(solution)/shard_map/attention/all_to_all | solution.py:21
  85.2 7.8 %copy-start = (bf16[4,4,512]{2,1,0:T(4,128)(2,1)S(1)}, bf16[4,4,512]{2,1,0:T(4,128)(2,1)}, u32[]{:S(2)}) copy-start(bf16[4,4,512]{2,1,0:T(4,128)(2,1)} %stream_ref.1) | copy-start | bytes 49156
  85.2 7.8 %collective-permute-start.1 = (bf16[16,512]{1,0:T(8,128)(2,1)S(1)}, bf16[16,512]{1,0:T(8,128)(2,1)S(1)}, u32[]{:S(2)}, u32[]{:S(2)}) collective-permute-start(bf16[16,512]{1,0:T(8,128)(2,1)S(1)} %projection.3), channel_id=1, source_target_pairs={{0,10},{1,26},{2,42},{3,58},{4,74},{5,90},{6,106},{7,122},{8,138},... | collective-permute-start | bytes 49160 | tf_op jit(solution)/shard_map/projection/ppermute | solution.py:25
  93.7 10.0 %copy-start.1 = (bf16[512]{0:T(512)(128)(2,1)S(1)}, bf16[512]{0:T(512)(128)(2,1)}, u32[]{:S(2)}) copy-start(bf16[512]{0:T(512)(128)(2,1)} %param.17) | copy-start | bytes 3076
  93.7 17.6 %all-to-all-start.4 = ((f32[16,16,128]{2,1,0:T(8,128)}), f32[16,16,128]{2,1,0:T(8,128)S(1)}, u32[]{:S(2)}, u32[]{:S(2)}) async-start(f32[16,16,128]{2,1,0:T(8,128)} %get-tuple-element.8), calls=%async_computation.4 | async-start | bytes 262144 | tf_op jit(solution)/shard_map/norm/all_to_all | solution.py:21

commit v9 on v8

--- a/solution.py
+++ b/solution.py
@@ -205,7 +205,7 @@
             side_by_side_kernel, jax.ShapeDtypeStruct((share, columns), BF16), weight, flops=20_000_000_000
         )
         parts = exchanged(parts, "tp")
-        attended = call(combine_kernel, jax.ShapeDtypeStruct((n_arc, rows, share), BF16), parts)
+        attended = call(combine_kernel, jax.ShapeDtypeStruct((n_arc, rows, share), BF16), parts, flops=4_000_000_000)
         attended = exchanged(attended, ARC)
 
     with jax.named_scope("projection"):

time: 113 us -> 116 us (1.027)
  the two profiles are of different devices: /device:TPU:1 before, /device:TPU:3 now
where the time goes in v9:
time: 116 us
  starting transfers between devices  56 us (48%)
  waiting for transfers between devices  25.8 us (22%)
  blocking collectives  24.4 us (21%)
  Pallas kernels  7.34 us (6%)
  local copies, waits for them, and re-layouts  1.59 us (1%)
    all_to_all x4, starting transfers between devices, exchanged(): return lax.all_to_all(pieces, axes, split_axis=0, concat_axis=0, tiled=True)  42.5 us
    all_to_all x1, blocking collectives, exchanged(): return lax.all_to_all(pieces, axes, split_axis=0, concat_axis=0, tiled=True)  24.4 us
    ppermute x2, waiting for transfers between devices, permuted(): return lax.ppermute(array, axes, [(i, target(i)) for i in range(count)])  18.2 us
    ppermute x2, starting transfers between devices, permuted(): return lax.ppermute(array, axes, [(i, target(i)) for i in range(count)])  13.5 us
    all_to_all x4, waiting for transfers between devices, exchanged(): return lax.all_to_all(pieces, axes, split_axis=0, concat_axis=0, tiled=True)  7.64 us
    pallas_call x1, Pallas kernels, attend(): pl.pallas_call(attend_kernel, grid=(queries.shape[0],), out_shape=outs, i...  4.74 us
    pallas_call x6, Pallas kernels, call(): pl.pallas_call(kernel, out_shape=outs, in_specs=[vmem] * len(args), out_s...  2.6 us
  transfers between devices with their start and end apart: 6, of which 3 were waited for; matrix products, arithmetic and copies ran while one was open for 0% of the time, Pallas kernels for 5%

profile of v9, /device:TPU:3, one launch (start us, length us, event | category | flops | bytes accessed | tf_op | source)
XLA Modules:
  0.0 115.8 jit_solution(14958671111319110578)
XLA Ops:
  0.6 1.6 %broadcast_in_dim.3 = bf16[4,256,128]{2,1,0:T(8,128)(2,1)} broadcast(bf16[256,128]{1,0:T(8,128)(2,1)} %param.16), dimensions={1,2} | broadcast | bytes 327680 | tf_op jit(solution)/shard_map/weights/broadcast_in_dim | solution.py:194
  2.2 4.1 %all-to-all-start = ((bf16[4,256,128]{2,1,0:T(8,128)(2,1)}), bf16[4,256,128]{2,1,0:T(8,128)(2,1)S(1)}, u32[]{:S(2)}, u32[]{:S(2)}) async-start(bf16[4,256,128]{2,1,0:T(8,128)(2,1)} %broadcast_in_dim.3), calls=%async_computation | async-start | bytes 524288 | tf_op jit(solution)/shard_map/weights/all_to_all | solution.py:21
  6.3 4.7 %attention.3 = bf16[16,5,8,128]{3,2,1,0:T(8,128)(2,1)} custom-call(s32[4]{0:T(128)} %len_ref.1, bf16[4,4,4096]{2,1,0:T(4,128)(2,1)} %q_ref.1, bf16[4,16,128]{2,1,0:T(8,128)(2,1)} %bitcast.6, bf16[4,16,128]{2,1,0:T(8,128)(2,1)} %bitcast.7, bf16[4,1024,128]{2,1,0:T(8,128)(2,1)} %bitcast.4, bf16[4,1024,128]{2,1,0:T(8,128)(2,1)} %bitcast.5), custom_call_target="tpu_custom_call" | custom-call | flops 300000000 | bytes 2097152 | tf_op jit(solution)/shard_map/attention/pallas_call | solution.py:86
  11.0 0.0 all-to-all-done
  11.0 16.5 %all-to-all-start.1 = ((bf16[16,5,8,128]{3,2,1,0:T(8,128)(2,1)}), bf16[16,5,8,128]{3,2,1,0:T(8,128)(2,1)S(1)}, u32[]{:S(2)}, u32[]{:S(2)}) async-start(bf16[16,5,8,128]{3,2,1,0:T(8,128)(2,1)} %attention.3), calls=%async_computation.1 | async-start | bytes 327680 | tf_op jit(solution)/shard_map/attention/all_to_all | solution.py:21
  27.5 10.9 %collective-permute-start = (bf16[4,256,128]{2,1,0:T(8,128)(2,1)S(1)}, bf16[4,256,128]{2,1,0:T(8,128)(2,1)S(1)}, u32[]{:S(2)}, u32[]{:S(2)}) collective-permute-start(bf16[4,256,128]{2,1,0:T(8,128)(2,1)S(1)} %all-to-all-done), channel_id=1, source_target_pairs={{0,96},{16,928},{32,736},{48,288},{64,112},{80,944},{96,752},{112,... | collective-permute-start | bytes 786440 | tf_op jit(solution)/shard_map/attention/ppermute | solution.py:25
  38.4 0.0 all-to-all-done.1.parts_ref
  38.4 0.9 attention.4
  39.3 11.1 %all-to-all-start.2 = ((bf16[16,16,256]{2,1,0:T(8,128)(2,1)}), bf16[16,16,256]{2,1,0:T(8,128)(2,1)S(1)}, u32[]{:S(2)}, u32[]{:S(2)}) async-start(bf16[16,16,256]{2,1,0:T(8,128)(2,1)} %attention.4), calls=%async_computation.2 | async-start | bytes 262144 | tf_op jit(solution)/shard_map/attention/all_to_all | solution.py:21
  50.4 14.5 %collective-permute-done.blocks_ref = bf16[4,256,128]{2,1,0:T(8,128)(2,1)S(1)} collective-permute-done((bf16[4,256,128]{2,1,0:T(8,128)(2,1)S(1)}, bf16[4,256,128]{2,1,0:T(8,128)(2,1)S(1)}, u32[]{:S(2)}, u32[]{:S(2)}) %collective-permute-start) | collective-permute-done | bytes 262176 | tf_op jit(solution)/shard_map/attention/ppermute | solution.py:25
  64.9 0.0 all-to-all-done.2.x_ref
  65.0 0.2 projection.2
  65.2 24.4 %all_to_all.25.parts_ref = bf16[16,16,512]{2,1,0:T(8,128)(2,1)S(1)} all-to-all(bf16[16,16,512]{2,1,0:T(8,128)(2,1)S(1)} %projection.2), channel_id=1, replica_groups=mesh['ra'=4,'rb'=4,'rc'=4,'tp'=16] {'tp'}, dimensions={0} | all-to-all | bytes 524288 | tf_op jit(solution)/shard_map/projection/all_to_all | solution.py:21
  89.6 0.0 copy-start
  89.6 2.6 %collective-permute-start.1 = (bf16[16,512]{1,0:T(8,128)(2,1)S(1)}, bf16[16,512]{1,0:T(8,128)(2,1)S(1)}, u32[]{:S(2)}, u32[]{:S(2)}) collective-permute-start(bf16[16,512]{1,0:T(8,128)(2,1)S(1)} %projection.3), channel_id=1, source_target_pairs={{0,10},{1,26},{2,42},{3,58},{4,74},{5,90},{6,106},{7,122},{8,138},... | collective-permute-start | bytes 49160 | tf_op jit(solution)/shard_map/projection/ppermute | solution.py:25
  92.2 3.7 %collective-permute-done.1.summed_ref = bf16[16,512]{1,0:T(8,128)(2,1)S(1)} collective-permute-done((bf16[16,512]{1,0:T(8,128)(2,1)S(1)}, bf16[16,512]{1,0:T(8,128)(2,1)S(1)}, u32[]{:S(2)}, u32[]{:S(2)}) %collective-permute-start.1) | collective-permute-done | bytes 16416 | tf_op jit(solution)/shard_map/projection/ppermute | solution.py:25
  95.9 0.0 copy-done
  95.9 0.7 norm.2
  96.6 0.0 copy-start.1
  96.6 10.9 %all-to-all-start.4 = ((f32[16,16,128]{2,1,0:T(8,128)}), f32[16,16,128]{2,1,0:T(8,128)S(1)}, u32[]{:S(2)}, u32[]{:S(2)}) async-start(f32[16,16,128]{2,1,0:T(8,128)} %get-tuple-element.8), calls=%async_computation.4 | async-start | bytes 262144 | tf_op jit(solution)/shard_map/norm/all_to_all | solution.py:21
  107.5 0.0 copy-done.1
  107.5 7.6 %all-to-all-done.4.squares_ref = f32[16,16,128]{2,1,0:T(8,128)S(1)} async-done(((f32[16,16,128]{2,1,0:T(8,128)}), f32[16,16,128]{2,1,0:T(8,128)S(1)}, u32[]{:S(2)}, u32[]{:S(2)}) %all-to-all-start.4) | async-done | bytes 131104 | tf_op jit(solution)/shard_map/norm/all_to_all | solution.py:21
  115.1 0.7 norm.3
  (3 shorter events, 0.1 us)
Async XLA Ops:
  2.2 8.8 %all-to-all-start = ((bf16[4,256,128]{2,1,0:T(8,128)(2,1)}), bf16[4,256,128]{2,1,0:T(8,128)(2,1)S(1)}, u32[]{:S(2)}, u32[]{:S(2)}) async-start(bf16[4,256,128]{2,1,0:T(8,128)(2,1)} %broadcast_in_dim.3), calls=%async_computation | async-start | bytes 524288 | tf_op jit(solution)/shard_map/weights/all_to_all | solution.py:21
  11.0 27.3 %all-to-all-start.1 = ((bf16[16,5,8,128]{3,2,1,0:T(8,128)(2,1)}), bf16[16,5,8,128]{3,2,1,0:T(8,128)(2,1)S(1)}, u32[]{:S(2)}, u32[]{:S(2)}) async-start(bf16[16,5,8,128]{3,2,1,0:T(8,128)(2,1)} %attention.3), calls=%async_computation.1 | async-start | bytes 327680 | tf_op jit(solution)/shard_map/attention/all_to_all | solution.py:21
  27.5 37.4 %collective-permute-start = (bf16[4,256,128]{2,1,0:T(8,128)(2,1)S(1)}, bf16[4,256,128]{2,1,0:T(8,128)(2,1)S(1)}, u32[]{:S(2)}, u32[]{:S(2)}) collective-permute-start(bf16[4,256,128]{2,1,0:T(8,128)(2,1)S(1)} %all-to-all-done), channel_id=1, source_target_pairs={{0,96},{16,928},{32,736},{48,288},{64,112},{80,944},{96,752},{112,... | collective-permute-start | bytes 786440 | tf_op jit(solution)/shard_map/attention/ppermute | solution.py:25
  39.3 25.6 %all-to-all-start.2 = ((bf16[16,16,256]{2,1,0:T(8,128)(2,1)}), bf16[16,16,256]{2,1,0:T(8,128)(2,1)S(1)}, u32[]{:S(2)}, u32[]{:S(2)}) async-start(bf16[16,16,256]{2,1,0:T(8,128)(2,1)} %attention.4), calls=%async_computation.2 | async-start | bytes 262144 | tf_op jit(solution)/shard_map/attention/all_to_all | solution.py:21
  89.6 6.3 %copy-start = (bf16[4,4,512]{2,1,0:T(4,128)(2,1)S(1)}, bf16[4,4,512]{2,1,0:T(4,128)(2,1)}, u32[]{:S(2)}) copy-start(bf16[4,4,512]{2,1,0:T(4,128)(2,1)} %stream_ref.1) | copy-start | bytes 49156
  89.6 6.3 %collective-permute-start.1 = (bf16[16,512]{1,0:T(8,128)(2,1)S(1)}, bf16[16,512]{1,0:T(8,128)(2,1)S(1)}, u32[]{:S(2)}, u32[]{:S(2)}) collective-permute-start(bf16[16,512]{1,0:T(8,128)(2,1)S(1)} %projection.3), channel_id=1, source_target_pairs={{0,10},{1,26},{2,42},{3,58},{4,74},{5,90},{6,106},{7,122},{8,138},... | collective-permute-start | bytes 49160 | tf_op jit(solution)/shard_map/projection/ppermute | solution.py:25
  96.6 10.9 %copy-start.1 = (bf16[512]{0:T(512)(128)(2,1)S(1)}, bf16[512]{0:T(512)(128)(2,1)}, u32[]{:S(2)}) copy-start(bf16[512]{0:T(512)(128)(2,1)} %param.17) | copy-start | bytes 3076
  96.6 18.5 %all-to-all-start.4 = ((f32[16,16,128]{2,1,0:T(8,128)}), f32[16,16,128]{2,1,0:T(8,128)S(1)}, u32[]{:S(2)}, u32[]{:S(2)}) async-start(f32[16,16,128]{2,1,0:T(8,128)} %get-tuple-element.8), calls=%async_computation.4 | async-start | bytes 262144 | tf_op jit(solution)/shard_map/norm/all_to_all | solution.py:21

commit v10 on v8

--- a/solution.py
+++ b/solution.py
@@ -15,6 +15,14 @@
 MASKED = -1e30
 NONE_VISIBLE = -1e29
 F32, BF16 = jnp.float32, jnp.bfloat16
+
+
+def place_of(arc, quad, places=16, quads=4):
+    return (quad + (places - quads) * arc + 6) % places
+
+
+def columns_of(arc, place, places=16, quads=4):
+    return (place + quads * arc + places - 6) % places
 
 
 def exchanged(pieces, axes):
@@ -126,7 +134,9 @@
 def project_kernel(x_ref, w_ref, out_ref):
     x = x_ref[...].reshape(-1, x_ref.shape[2])
     projected = jnp.dot(x, w_ref[...], preferred_element_type=F32)
-    out_ref[...] = projected.astype(BF16).reshape(out_ref.shape)
+    projected = projected.astype(BF16).reshape(out_ref.shape)
+    for place in range(out_ref.shape[0]):
+        out_ref[columns_of(lax.axis_index("ra"), place)] = projected[place]
 
 
 def sum_kernel(parts_ref, out_ref):
@@ -179,12 +189,6 @@
     columns = stream_in.shape[2]
     share = width // n_tp
 
-    def place_of(arc, quad):
-        return (quad - arc * n_quad + 6) % n_arc
-
-    def columns_of(arc, place):
-        return (place - 6 + arc * n_quad) % n_arc
-
     def weight_home(r):
         quad, member = r // n_quad, r % n_quad
         arc = (quad // n_quad - member) % n_quad
@@ -218,7 +222,7 @@
 
         def home(i):
             arc, place, p = i // (n_arc * n_tp), i // n_tp % n_arc, i % n_tp
-            return (arc * n_arc + p) * n_tp + columns_of(arc, place)
+            return (arc * n_arc + place_of(arc, p)) * n_tp + columns_of(arc, place)
 
         summed = permuted(summed, (*REP, "tp"), n_rep * n_tp, home)
 

time: 113 us -> 114 us (level)
  waiting for transfers between devices: 22.5 us -> 24 us
    ppermute x2, waiting for transfers between devices: 4.23 us -> 5.82 us  [permuted(): return lax.ppermute(array, axes, [(i, target(i)) for i in range(count)])]
where the time goes in v10:
time: 114 us
  starting transfers between devices  45.3 us (40%)
  blocking collectives  34.8 us (31%)
  waiting for transfers between devices  24 us (21%)
  Pallas kernels  7.33 us (6%)
  local copies, waits for them, and re-layouts  1.6 us (1%)
    all_to_all x3, starting transfers between devices, exchanged(): return lax.all_to_all(pieces, axes, split_axis=0, concat_axis=0, tiled=True)  35.2 us
    all_to_all x2, blocking collectives, exchanged(): return lax.all_to_all(pieces, axes, split_axis=0, concat_axis=0, tiled=True)  34.8 us
    all_to_all x3, waiting for transfers between devices, exchanged(): return lax.all_to_all(pieces, axes, split_axis=0, concat_axis=0, tiled=True)  18.2 us
    ppermute x2, starting transfers between devices, permuted(): return lax.ppermute(array, axes, [(i, target(i)) for i in range(count)])  10.1 us
    ppermute x2, waiting for transfers between devices, permuted(): return lax.ppermute(array, axes, [(i, target(i)) for i in range(count)])  5.82 us
    pallas_call x1, Pallas kernels, attend(): pl.pallas_call(attend_kernel, grid=(queries.shape[0],), out_shape=outs, i...  4.74 us
    pallas_call x6, Pallas kernels, call(): pl.pallas_call(kernel, out_shape=outs, in_specs=[vmem] * len(args), out_s...  2.58 us
  transfers between devices with their start and end apart: 5, of which 3 were waited for; matrix products, arithmetic and copies ran while one was open for 0% of the time, Pallas kernels for 5%

profile of v10, /device:TPU:1, one launch (start us, length us, event | category | flops | bytes accessed | tf_op | source)
XLA Modules:
  0.0 113.8 jit_solution(2241572525645580904)
XLA Ops:
  0.6 1.6 %broadcast_in_dim.3 = bf16[4,256,128]{2,1,0:T(8,128)(2,1)} broadcast(bf16[256,128]{1,0:T(8,128)(2,1)} %param.16), dimensions={1,2} | broadcast | bytes 327680 | tf_op jit(solution)/shard_map/weights/broadcast_in_dim | solution.py:198
  2.2 4.7 %all-to-all-start = ((bf16[4,256,128]{2,1,0:T(8,128)(2,1)}), bf16[4,256,128]{2,1,0:T(8,128)(2,1)S(1)}, u32[]{:S(2)}, u32[]{:S(2)}) async-start(bf16[4,256,128]{2,1,0:T(8,128)(2,1)} %broadcast_in_dim.3), calls=%async_computation | async-start | bytes 524288 | tf_op jit(solution)/shard_map/weights/all_to_all | solution.py:29
  6.9 4.7 %attention.3 = bf16[16,5,8,128]{3,2,1,0:T(8,128)(2,1)} custom-call(s32[4]{0:T(128)} %len_ref.1, bf16[4,4,4096]{2,1,0:T(4,128)(2,1)} %q_ref.1, bf16[4,16,128]{2,1,0:T(8,128)(2,1)} %bitcast.6, bf16[4,16,128]{2,1,0:T(8,128)(2,1)} %bitcast.7, bf16[4,1024,128]{2,1,0:T(8,128)(2,1)} %bitcast.4, bf16[4,1024,128]{2,1,0:T(8,128)(2,1)} %bitcast.5), custom_call_target="tpu_custom_call" | custom-call | flops 300000000 | bytes 2097152 | tf_op jit(solution)/shard_map/attention/pallas_call | solution.py:94
  11.6 0.0 all-to-all-done
  11.6 6.1 %collective-permute-start = (bf16[4,256,128]{2,1,0:T(8,128)(2,1)S(1)}, bf16[4,256,128]{2,1,0:T(8,128)(2,1)S(1)}, u32[]{:S(2)}, u32[]{:S(2)}) collective-permute-start(bf16[4,256,128]{2,1,0:T(8,128)(2,1)S(1)} %all-to-all-done), channel_id=1, source_target_pairs={{0,96},{16,928},{32,736},{48,288},{64,112},{80,944},{96,752},{112,... | collective-permute-start | bytes 786440 | tf_op jit(solution)/shard_map/attention/ppermute | solution.py:33
  17.7 20.6 %all_to_all.25.parts_ref = bf16[16,5,8,128]{3,2,1,0:T(8,128)(2,1)S(1)} all-to-all(bf16[16,5,8,128]{3,2,1,0:T(8,128)(2,1)} %attention.3), channel_id=1, replica_groups=mesh['ra'=4,'rb'=4,'rc'=4,'tp'=16] {'tp'}, dimensions={0} | all-to-all | bytes 327680 | tf_op jit(solution)/shard_map/attention/all_to_all | solution.py:29
  38.3 0.9 attention.4
  39.2 20.9 %all-to-all-start.2 = ((bf16[16,16,256]{2,1,0:T(8,128)(2,1)}), bf16[16,16,256]{2,1,0:T(8,128)(2,1)S(1)}, u32[]{:S(2)}, u32[]{:S(2)}) async-start(bf16[16,16,256]{2,1,0:T(8,128)(2,1)} %attention.4), calls=%async_computation.2 | async-start | bytes 262144 | tf_op jit(solution)/shard_map/attention/all_to_all | solution.py:29
  60.1 0.0 collective-permute-done.blocks_ref
  60.2 10.6 %all-to-all-done.2.x_ref = bf16[16,16,256]{2,1,0:T(8,128)(2,1)S(1)} async-done(((bf16[16,16,256]{2,1,0:T(8,128)(2,1)}), bf16[16,16,256]{2,1,0:T(8,128)(2,1)S(1)}, u32[]{:S(2)}, u32[]{:S(2)}) %all-to-all-start.2) | async-done | bytes 131104 | tf_op jit(solution)/shard_map/attention/all_to_all | solution.py:29
  70.8 0.2 projection.2
  71.0 14.2 %all_to_all.26.parts_ref = bf16[16,16,512]{2,1,0:T(8,128)(2,1)S(1)} all-to-all(bf16[16,16,512]{2,1,0:T(8,128)(2,1)S(1)} %projection.2), channel_id=1, replica_groups=mesh['ra'=4,'rb'=4,'rc'=4,'tp'=16] {'tp'}, dimensions={0} | all-to-all | bytes 524288 | tf_op jit(solution)/shard_map/projection/all_to_all | solution.py:29
  85.2 0.0 copy-start
  85.2 4.0 %collective-permute-start.1 = (bf16[16,512]{1,0:T(8,128)(2,1)S(1)}, bf16[16,512]{1,0:T(8,128)(2,1)S(1)}, u32[]{:S(2)}, u32[]{:S(2)}) collective-permute-start(bf16[16,512]{1,0:T(8,128)(2,1)S(1)} %projection.3), channel_id=1, source_target_pairs={{0,106},{1,122},{2,138},{3,154},{4,170},{5,186},{6,202},{7,218},{8... | collective-permute-start | bytes 49160 | tf_op jit(solution)/shard_map/projection/ppermute | solution.py:33
  89.3 5.8 %collective-permute-done.1.summed_ref = bf16[16,512]{1,0:T(8,128)(2,1)S(1)} collective-permute-done((bf16[16,512]{1,0:T(8,128)(2,1)S(1)}, bf16[16,512]{1,0:T(8,128)(2,1)S(1)}, u32[]{:S(2)}, u32[]{:S(2)}) %collective-permute-start.1) | collective-permute-done | bytes 16416 | tf_op jit(solution)/shard_map/projection/ppermute | solution.py:33
  95.1 0.0 copy-done
  95.1 0.7 norm.2
  95.8 0.0 copy-start.1
  95.8 9.7 %all-to-all-start.4 = ((f32[16,16,128]{2,1,0:T(8,128)}), f32[16,16,128]{2,1,0:T(8,128)S(1)}, u32[]{:S(2)}, u32[]{:S(2)}) async-start(f32[16,16,128]{2,1,0:T(8,128)} %get-tuple-element.8), calls=%async_computation.4 | async-start | bytes 262144 | tf_op jit(solution)/shard_map/norm/all_to_all | solution.py:29
  105.4 0.0 copy-done.1
  105.4 7.6 %all-to-all-done.4.squares_ref = f32[16,16,128]{2,1,0:T(8,128)S(1)} async-done(((f32[16,16,128]{2,1,0:T(8,128)}), f32[16,16,128]{2,1,0:T(8,128)S(1)}, u32[]{:S(2)}, u32[]{:S(2)}) %all-to-all-start.4) | async-done | bytes 131104 | tf_op jit(solution)/shard_map/norm/all_to_all | solution.py:29
  113.1 0.7 norm.3
  (3 shorter events, 0.1 us)
Async XLA Ops:
  2.2 9.4 %all-to-all-start = ((bf16[4,256,128]{2,1,0:T(8,128)(2,1)}), bf16[4,256,128]{2,1,0:T(8,128)(2,1)S(1)}, u32[]{:S(2)}, u32[]{:S(2)}) async-start(bf16[4,256,128]{2,1,0:T(8,128)(2,1)} %broadcast_in_dim.3), calls=%async_computation | async-start | bytes 524288 | tf_op jit(solution)/shard_map/weights/all_to_all | solution.py:29
  11.6 48.5 %collective-permute-start = (bf16[4,256,128]{2,1,0:T(8,128)(2,1)S(1)}, bf16[4,256,128]{2,1,0:T(8,128)(2,1)S(1)}, u32[]{:S(2)}, u32[]{:S(2)}) collective-permute-start(bf16[4,256,128]{2,1,0:T(8,128)(2,1)S(1)} %all-to-all-done), channel_id=1, source_target_pairs={{0,96},{16,928},{32,736},{48,288},{64,112},{80,944},{96,752},{112,... | collective-permute-start | bytes 786440 | tf_op jit(solution)/shard_map/attention/ppermute | solution.py:33
  39.2 31.5 %all-to-all-start.2 = ((bf16[16,16,256]{2,1,0:T(8,128)(2,1)}), bf16[16,16,256]{2,1,0:T(8,128)(2,1)S(1)}, u32[]{:S(2)}, u32[]{:S(2)}) async-start(bf16[16,16,256]{2,1,0:T(8,128)(2,1)} %attention.4), calls=%async_computation.2 | async-start | bytes 262144 | tf_op jit(solution)/shard_map/attention/all_to_all | solution.py:29
  85.2 9.9 %copy-start = (bf16[4,4,512]{2,1,0:T(4,128)(2,1)S(1)}, bf16[4,4,512]{2,1,0:T(4,128)(2,1)}, u32[]{:S(2)}) copy-start(bf16[4,4,512]{2,1,0:T(4,128)(2,1)} %stream_ref.1) | copy-start | bytes 49156
  85.2 9.9 %collective-permute-start.1 = (bf16[16,512]{1,0:T(8,128)(2,1)S(1)}, bf16[16,512]{1,0:T(8,128)(2,1)S(1)}, u32[]{:S(2)}, u32[]{:S(2)}) collective-permute-start(bf16[16,512]{1,0:T(8,128)(2,1)S(1)} %projection.3), channel_id=1, source_target_pairs={{0,106},{1,122},{2,138},{3,154},{4,170},{5,186},{6,202},{7,218},{8... | collective-permute-start | bytes 49160 | tf_op jit(solution)/shard_map/projection/ppermute | solution.py:33
  95.8 9.7 %copy-start.1 = (bf16[512]{0:T(512)(128)(2,1)S(1)}, bf16[512]{0:T(512)(128)(2,1)}, u32[]{:S(2)}) copy-start(bf16[512]{0:T(512)(128)(2,1)} %param.17) | copy-start | bytes 3076
  95.8 17.3 %all-to-all-start.4 = ((f32[16,16,128]{2,1,0:T(8,128)}), f32[16,16,128]{2,1,0:T(8,128)S(1)}, u32[]{:S(2)}, u32[]{:S(2)}) async-start(f32[16,16,128]{2,1,0:T(8,128)} %get-tuple-element.8), calls=%async_computation.4 | async-start | bytes 262144 | tf_op jit(solution)/shard_map/norm/all_to_all | solution.py:29

commit v11 on v8

--- a/solution.py
+++ b/solution.py
@@ -179,15 +179,19 @@
     columns = stream_in.shape[2]
     share = width // n_tp
 
+    def swap(arc, quad):
+        return (quad // n_quad - arc) % n_quad % 2
+
     def place_of(arc, quad):
-        return (quad - arc * n_quad + 6) % n_arc
+        return (quad - arc * n_quad + 6) % n_arc ^ swap(arc, quad)
 
     def columns_of(arc, place):
-        return (place - 6 + arc * n_quad) % n_arc
+        quad = (place - 6 + arc * n_quad) % n_arc
+        return quad ^ swap(arc, quad)
 
     def weight_home(r):
         quad, member = r // n_quad, r % n_quad
-        arc = (quad // n_quad - member) % n_quad
+        arc = (quad // n_quad - (member ^ quad % 2)) % n_quad
         return arc * n_arc + place_of(arc, quad)
 
     with jax.named_scope("weights"):

time: 113 us -> 113 us (level)
  starting transfers between devices: 45 us -> 42.5 us
  waiting for transfers between devices: 22.5 us -> 24.2 us
    ppermute x2, waiting for transfers between devices: 4.23 us -> 6 us  [permuted(): return lax.ppermute(array, axes, [(i, target(i)) for i in range(count)])]
    ppermute x2, starting transfers between devices: 9.59 us -> 7.99 us  [permuted(): return lax.ppermute(array, axes, [(i, target(i)) for i in range(count)])]
where the time goes in v11:
time: 113 us; the launch traced here: 112 us
  starting transfers between devices  42.5 us (38%)
  blocking collectives  35.7 us (32%)
  waiting for transfers between devices  24.2 us (21%)
  Pallas kernels  7.34 us (6%)
  local copies, waits for them, and re-layouts  1.6 us (1%)
    all_to_all x2, blocking collectives, exchanged(): return lax.all_to_all(pieces, axes, split_axis=0, concat_axis=0, tiled=True)  35.7 us
    all_to_all x3, starting transfers between devices, exchanged(): return lax.all_to_all(pieces, axes, split_axis=0, concat_axis=0, tiled=True)  34.5 us
    all_to_all x3, waiting for transfers between devices, exchanged(): return lax.all_to_all(pieces, axes, split_axis=0, concat_axis=0, tiled=True)  18.2 us
    ppermute x2, starting transfers between devices, permuted(): return lax.ppermute(array, axes, [(i, target(i)) for i in range(count)])  7.99 us
    ppermute x2, waiting for transfers between devices, permuted(): return lax.ppermute(array, axes, [(i, target(i)) for i in range(count)])  6 us
    pallas_call x1, Pallas kernels, attend(): pl.pallas_call(attend_kernel, grid=(queries.shape[0],), out_shape=outs, i...  4.74 us
    pallas_call x6, Pallas kernels, call(): pl.pallas_call(kernel, out_shape=outs, in_specs=[vmem] * len(args), out_s...  2.59 us
  transfers between devices with their start and end apart: 5, of which 3 were waited for; matrix products, arithmetic and copies ran while one was open for 0% of the time, Pallas kernels for 5%

profile of v11, /device:TPU:1, one launch (start us, length us, event | category | flops | bytes accessed | tf_op | source)
XLA Modules:
  0.0 112.0 jit_solution(10639767690979632837)
XLA Ops:
  0.6 1.6 %broadcast_in_dim.3 = bf16[4,256,128]{2,1,0:T(8,128)(2,1)} broadcast(bf16[256,128]{1,0:T(8,128)(2,1)} %param.16), dimensions={1,2} | broadcast | bytes 327680 | tf_op jit(solution)/shard_map/weights/broadcast_in_dim | solution.py:198
  2.2 4.7 %all-to-all-start = ((bf16[4,256,128]{2,1,0:T(8,128)(2,1)}), bf16[4,256,128]{2,1,0:T(8,128)(2,1)S(1)}, u32[]{:S(2)}, u32[]{:S(2)}) async-start(bf16[4,256,128]{2,1,0:T(8,128)(2,1)} %broadcast_in_dim.3), calls=%async_computation | async-start | bytes 524288 | tf_op jit(solution)/shard_map/weights/all_to_all | solution.py:21
  6.9 4.7 %attention.3 = bf16[16,5,8,128]{3,2,1,0:T(8,128)(2,1)} custom-call(s32[4]{0:T(128)} %len_ref.1, bf16[4,4,4096]{2,1,0:T(4,128)(2,1)} %q_ref.1, bf16[4,16,128]{2,1,0:T(8,128)(2,1)} %bitcast.6, bf16[4,16,128]{2,1,0:T(8,128)(2,1)} %bitcast.7, bf16[4,1024,128]{2,1,0:T(8,128)(2,1)} %bitcast.4, bf16[4,1024,128]{2,1,0:T(8,128)(2,1)} %bitcast.5), custom_call_target="tpu_custom_call" | custom-call | flops 300000000 | bytes 2097152 | tf_op jit(solution)/shard_map/attention/pallas_call | solution.py:86
  11.6 0.0 all-to-all-done
  11.6 6.1 %collective-permute-start = (bf16[4,256,128]{2,1,0:T(8,128)(2,1)S(1)}, bf16[4,256,128]{2,1,0:T(8,128)(2,1)S(1)}, u32[]{:S(2)}, u32[]{:S(2)}) collective-permute-start(bf16[4,256,128]{2,1,0:T(8,128)(2,1)S(1)} %all-to-all-done), channel_id=1, source_target_pairs={{0,96},{16,944},{32,736},{48,304},{64,928},{80,112},{96,288},{112,... | collective-permute-start | bytes 786440 | tf_op jit(solution)/shard_map/attention/ppermute | solution.py:25
  17.7 20.6 %all_to_all.25.parts_ref = bf16[16,5,8,128]{3,2,1,0:T(8,128)(2,1)S(1)} all-to-all(bf16[16,5,8,128]{3,2,1,0:T(8,128)(2,1)} %attention.3), channel_id=1, replica_groups=mesh['ra'=4,'rb'=4,'rc'=4,'tp'=16] {'tp'}, dimensions={0} | all-to-all | bytes 327680 | tf_op jit(solution)/shard_map/attention/all_to_all | solution.py:21
  38.3 0.9 attention.4
  39.2 20.0 %all-to-all-start.2 = ((bf16[16,16,256]{2,1,0:T(8,128)(2,1)}), bf16[16,16,256]{2,1,0:T(8,128)(2,1)S(1)}, u32[]{:S(2)}, u32[]{:S(2)}) async-start(bf16[16,16,256]{2,1,0:T(8,128)(2,1)} %attention.4), calls=%async_computation.2 | async-start | bytes 262144 | tf_op jit(solution)/shard_map/attention/all_to_all | solution.py:21
  59.3 0.0 collective-permute-done.blocks_ref
  59.3 10.6 %all-to-all-done.2.x_ref = bf16[16,16,256]{2,1,0:T(8,128)(2,1)S(1)} async-done(((bf16[16,16,256]{2,1,0:T(8,128)(2,1)}), bf16[16,16,256]{2,1,0:T(8,128)(2,1)S(1)}, u32[]{:S(2)}, u32[]{:S(2)}) %all-to-all-start.2) | async-done | bytes 131104 | tf_op jit(solution)/shard_map/attention/all_to_all | solution.py:21
  69.9 0.2 projection.2
  70.2 15.0 %all_to_all.26.parts_ref = bf16[16,16,512]{2,1,0:T(8,128)(2,1)S(1)} all-to-all(bf16[16,16,512]{2,1,0:T(8,128)(2,1)S(1)} %projection.2), channel_id=1, replica_groups=mesh['ra'=4,'rb'=4,'rc'=4,'tp'=16] {'tp'}, dimensions={0} | all-to-all | bytes 524288 | tf_op jit(solution)/shard_map/projection/all_to_all | solution.py:21
  85.2 0.0 copy-start
  85.2 1.9 %collective-permute-start.1 = (bf16[16,512]{1,0:T(8,128)(2,1)S(1)}, bf16[16,512]{1,0:T(8,128)(2,1)S(1)}, u32[]{:S(2)}, u32[]{:S(2)}) collective-permute-start(bf16[16,512]{1,0:T(8,128)(2,1)S(1)} %projection.3), channel_id=1, source_target_pairs={{0,10},{1,26},{2,42},{3,58},{4,74},{5,90},{6,106},{7,122},{8,138},... | collective-permute-start | bytes 49160 | tf_op jit(solution)/shard_map/projection/ppermute | solution.py:25
  87.2 6.0 %collective-permute-done.1.summed_ref = bf16[16,512]{1,0:T(8,128)(2,1)S(1)} collective-permute-done((bf16[16,512]{1,0:T(8,128)(2,1)S(1)}, bf16[16,512]{1,0:T(8,128)(2,1)S(1)}, u32[]{:S(2)}, u32[]{:S(2)}) %collective-permute-start.1) | collective-permute-done | bytes 16416 | tf_op jit(solution)/shard_map/projection/ppermute | solution.py:25
  93.2 0.0 copy-done
  93.2 0.7 norm.2
  93.8 0.0 copy-start.1
  93.8 9.8 %all-to-all-start.4 = ((f32[16,16,128]{2,1,0:T(8,128)}), f32[16,16,128]{2,1,0:T(8,128)S(1)}, u32[]{:S(2)}, u32[]{:S(2)}) async-start(f32[16,16,128]{2,1,0:T(8,128)} %get-tuple-element.8), calls=%async_computation.4 | async-start | bytes 262144 | tf_op jit(solution)/shard_map/norm/all_to_all | solution.py:21
  103.6 0.0 copy-done.1
  103.6 7.6 %all-to-all-done.4.squares_ref = f32[16,16,128]{2,1,0:T(8,128)S(1)} async-done(((f32[16,16,128]{2,1,0:T(8,128)}), f32[16,16,128]{2,1,0:T(8,128)S(1)}, u32[]{:S(2)}, u32[]{:S(2)}) %all-to-all-start.4) | async-done | bytes 131104 | tf_op jit(solution)/shard_map/norm/all_to_all | solution.py:21
  111.3 0.7 norm.3
  (3 shorter events, 0.1 us)
Async XLA Ops:
  2.2 9.4 %all-to-all-start = ((bf16[4,256,128]{2,1,0:T(8,128)(2,1)}), bf16[4,256,128]{2,1,0:T(8,128)(2,1)S(1)}, u32[]{:S(2)}, u32[]{:S(2)}) async-start(bf16[4,256,128]{2,1,0:T(8,128)(2,1)} %broadcast_in_dim.3), calls=%async_computation | async-start | bytes 524288 | tf_op jit(solution)/shard_map/weights/all_to_all | solution.py:21
  11.6 47.7 %collective-permute-start = (bf16[4,256,128]{2,1,0:T(8,128)(2,1)S(1)}, bf16[4,256,128]{2,1,0:T(8,128)(2,1)S(1)}, u32[]{:S(2)}, u32[]{:S(2)}) collective-permute-start(bf16[4,256,128]{2,1,0:T(8,128)(2,1)S(1)} %all-to-all-done), channel_id=1, source_target_pairs={{0,96},{16,944},{32,736},{48,304},{64,928},{80,112},{96,288},{112,... | collective-permute-start | bytes 786440 | tf_op jit(solution)/shard_map/attention/ppermute | solution.py:25
  39.2 30.7 %all-to-all-start.2 = ((bf16[16,16,256]{2,1,0:T(8,128)(2,1)}), bf16[16,16,256]{2,1,0:T(8,128)(2,1)S(1)}, u32[]{:S(2)}, u32[]{:S(2)}) async-start(bf16[16,16,256]{2,1,0:T(8,128)(2,1)} %attention.4), calls=%async_computation.2 | async-start | bytes 262144 | tf_op jit(solution)/shard_map/attention/all_to_all | solution.py:21
  85.2 8.0 %copy-start = (bf16[4,4,512]{2,1,0:T(4,128)(2,1)S(1)}, bf16[4,4,512]{2,1,0:T(4,128)(2,1)}, u32[]{:S(2)}) copy-start(bf16[4,4,512]{2,1,0:T(4,128)(2,1)} %stream_ref.1) | copy-start | bytes 49156
  85.2 7.9 %collective-permute-start.1 = (bf16[16,512]{1,0:T(8,128)(2,1)S(1)}, bf16[16,512]{1,0:T(8,128)(2,1)S(1)}, u32[]{:S(2)}, u32[]{:S(2)}) collective-permute-start(bf16[16,512]{1,0:T(8,128)(2,1)S(1)} %projection.3), channel_id=1, source_target_pairs={{0,10},{1,26},{2,42},{3,58},{4,74},{5,90},{6,106},{7,122},{8,138},... | collective-permute-start | bytes 49160 | tf_op jit(solution)/shard_map/projection/ppermute | solution.py:25
  93.8 9.8 %copy-start.1 = (bf16[512]{0:T(512)(128)(2,1)S(1)}, bf16[512]{0:T(512)(128)(2,1)}, u32[]{:S(2)}) copy-start(bf16[512]{0:T(512)(128)(2,1)} %param.17) | copy-start | bytes 3076
  93.8 17.4 %all-to-all-start.4 = ((f32[16,16,128]{2,1,0:T(8,128)}), f32[16,16,128]{2,1,0:T(8,128)S(1)}, u32[]{:S(2)}, u32[]{:S(2)}) async-start(f32[16,16,128]{2,1,0:T(8,128)} %get-tuple-element.8), calls=%async_computation.4 | async-start | bytes 262144 | tf_op jit(solution)/shard_map/norm/all_to_all | solution.py:21

commit v12 on v11

--- a/solution.py
+++ b/solution.py
@@ -139,12 +139,16 @@
     hidden_ref[...] = hidden
     squares = hidden * hidden
     squares = sum(squares[:, j : j + 128] for j in range(0, squares.shape[1], 128))
+    squares = squares[:, :64] + squares[:, 64:]
+    squares = stacked([squares[:8], squares[8:]], 1)
     for i in range(squares_ref.shape[0]):
         squares_ref[i] = squares
 
 
 def norm_kernel(squares_ref, hidden_ref, gain_ref, stream_ref, normed_ref):
-    squares = jnp.sum(jnp.sum(squares_ref[...], axis=0), axis=1, keepdims=True)
+    squares = jnp.sum(squares_ref[...], axis=0)
+    squares = stacked([squares[:, :64], squares[:, 64:]])
+    squares = jnp.sum(squares, axis=1, keepdims=True)
     hidden = hidden_ref[...]
     normed = hidden * lax.rsqrt(squares / D + 1e-06) * gain_ref[...].astype(F32)
     rows_b, steps, _ = stream_ref.shape
@@ -231,7 +235,7 @@
             hidden_kernel,
             [
                 jax.ShapeDtypeStruct((rows, columns), F32),
-                jax.ShapeDtypeStruct((n_tp, rows, 128), F32),
+                jax.ShapeDtypeStruct((n_tp, rows // 2, 128), F32),
             ],
             summed, stream_in,
         )

time: 113 us -> 113 us (level)
  no operation moved by 1% of the time
where the time goes in v12:
time: 113 us; the launch traced here: 112 us
  starting transfers between devices  42.5 us (38%)
  blocking collectives  35.7 us (32%)
  waiting for transfers between devices  23.9 us (21%)
  Pallas kernels  7.52 us (7%)
  local copies, waits for them, and re-layouts  1.6 us (1%)
    all_to_all x2, blocking collectives, exchanged(): return lax.all_to_all(pieces, axes, split_axis=0, concat_axis=0, tiled=True)  35.7 us
    all_to_all x3, starting transfers between devices, exchanged(): return lax.all_to_all(pieces, axes, split_axis=0, concat_axis=0, tiled=True)  34.5 us
    all_to_all x3, waiting for transfers between devices, exchanged(): return lax.all_to_all(pieces, axes, split_axis=0, concat_axis=0, tiled=True)  17.9 us
    ppermute x2, starting transfers between devices, permuted(): return lax.ppermute(array, axes, [(i, target(i)) for i in range(count)])  7.99 us
    ppermute x2, waiting for transfers between devices, permuted(): return lax.ppermute(array, axes, [(i, target(i)) for i in range(count)])  6 us
    pallas_call x1, Pallas kernels, attend(): pl.pallas_call(attend_kernel, grid=(queries.shape[0],), out_shape=outs, i...  4.74 us
    pallas_call x6, Pallas kernels, call(): pl.pallas_call(kernel, out_shape=outs, in_specs=[vmem] * len(args), out_s...  2.77 us
  transfers between devices with their start and end apart: 5, of which 3 were waited for; matrix products, arithmetic and copies ran while one was open for 0% of the time, Pallas kernels for 5%

profile of v12, /device:TPU:1, one launch (start us, length us, event | category | flops | bytes accessed | tf_op | source)
XLA Modules:
  0.0 111.8 jit_solution(5804639611211973608)
XLA Ops:
  0.6 1.6 %broadcast_in_dim.3 = bf16[4,256,128]{2,1,0:T(8,128)(2,1)} broadcast(bf16[256,128]{1,0:T(8,128)(2,1)} %param.16), dimensions={1,2} | broadcast | bytes 327680 | tf_op jit(solution)/shard_map/weights/broadcast_in_dim | solution.py:202
  2.2 4.7 %all-to-all-start = ((bf16[4,256,128]{2,1,0:T(8,128)(2,1)}), bf16[4,256,128]{2,1,0:T(8,128)(2,1)S(1)}, u32[]{:S(2)}, u32[]{:S(2)}) async-start(bf16[4,256,128]{2,1,0:T(8,128)(2,1)} %broadcast_in_dim.3), calls=%async_computation | async-start | bytes 524288 | tf_op jit(solution)/shard_map/weights/all_to_all | solution.py:21
  6.9 4.7 %attention.3 = bf16[16,5,8,128]{3,2,1,0:T(8,128)(2,1)} custom-call(s32[4]{0:T(128)} %len_ref.1, bf16[4,4,4096]{2,1,0:T(4,128)(2,1)} %q_ref.1, bf16[4,16,128]{2,1,0:T(8,128)(2,1)} %bitcast.6, bf16[4,16,128]{2,1,0:T(8,128)(2,1)} %bitcast.7, bf16[4,1024,128]{2,1,0:T(8,128)(2,1)} %bitcast.4, bf16[4,1024,128]{2,1,0:T(8,128)(2,1)} %bitcast.5), custom_call_target="tpu_custom_call" | custom-call | flops 300000000 | bytes 2097152 | tf_op jit(solution)/shard_map/attention/pallas_call | solution.py:86
  11.6 0.0 all-to-all-done
  11.6 6.1 %collective-permute-start = (bf16[4,256,128]{2,1,0:T(8,128)(2,1)S(1)}, bf16[4,256,128]{2,1,0:T(8,128)(2,1)S(1)}, u32[]{:S(2)}, u32[]{:S(2)}) collective-permute-start(bf16[4,256,128]{2,1,0:T(8,128)(2,1)S(1)} %all-to-all-done), channel_id=1, source_target_pairs={{0,96},{16,944},{32,736},{48,304},{64,928},{80,112},{96,288},{112,... | collective-permute-start | bytes 786440 | tf_op jit(solution)/shard_map/attention/ppermute | solution.py:25
  17.7 20.6 %all_to_all.25.parts_ref = bf16[16,5,8,128]{3,2,1,0:T(8,128)(2,1)S(1)} all-to-all(bf16[16,5,8,128]{3,2,1,0:T(8,128)(2,1)} %attention.3), channel_id=1, replica_groups=mesh['ra'=4,'rb'=4,'rc'=4,'tp'=16] {'tp'}, dimensions={0} | all-to-all | bytes 327680 | tf_op jit(solution)/shard_map/attention/all_to_all | solution.py:21
  38.3 0.9 attention.4
  39.2 20.0 %all-to-all-start.2 = ((bf16[16,16,256]{2,1,0:T(8,128)(2,1)}), bf16[16,16,256]{2,1,0:T(8,128)(2,1)S(1)}, u32[]{:S(2)}, u32[]{:S(2)}) async-start(bf16[16,16,256]{2,1,0:T(8,128)(2,1)} %attention.4), calls=%async_computation.2 | async-start | bytes 262144 | tf_op jit(solution)/shard_map/attention/all_to_all | solution.py:21
  59.3 0.0 collective-permute-done.blocks_ref
  59.3 10.6 %all-to-all-done.2.x_ref = bf16[16,16,256]{2,1,0:T(8,128)(2,1)S(1)} async-done(((bf16[16,16,256]{2,1,0:T(8,128)(2,1)}), bf16[16,16,256]{2,1,0:T(8,128)(2,1)S(1)}, u32[]{:S(2)}, u32[]{:S(2)}) %all-to-all-start.2) | async-done | bytes 131104 | tf_op jit(solution)/shard_map/attention/all_to_all | solution.py:21
  69.9 0.2 projection.2
  70.2 15.0 %all_to_all.26.parts_ref = bf16[16,16,512]{2,1,0:T(8,128)(2,1)S(1)} all-to-all(bf16[16,16,512]{2,1,0:T(8,128)(2,1)S(1)} %projection.2), channel_id=1, replica_groups=mesh['ra'=4,'rb'=4,'rc'=4,'tp'=16] {'tp'}, dimensions={0} | all-to-all | bytes 524288 | tf_op jit(solution)/shard_map/projection/all_to_all | solution.py:21
  85.2 0.0 copy-start
  85.2 1.9 %collective-permute-start.1 = (bf16[16,512]{1,0:T(8,128)(2,1)S(1)}, bf16[16,512]{1,0:T(8,128)(2,1)S(1)}, u32[]{:S(2)}, u32[]{:S(2)}) collective-permute-start(bf16[16,512]{1,0:T(8,128)(2,1)S(1)} %projection.3), channel_id=1, source_target_pairs={{0,10},{1,26},{2,42},{3,58},{4,74},{5,90},{6,106},{7,122},{8,138},... | collective-permute-start | bytes 49160 | tf_op jit(solution)/shard_map/projection/ppermute | solution.py:25
  87.2 6.0 %collective-permute-done.1.summed_ref = bf16[16,512]{1,0:T(8,128)(2,1)S(1)} collective-permute-done((bf16[16,512]{1,0:T(8,128)(2,1)S(1)}, bf16[16,512]{1,0:T(8,128)(2,1)S(1)}, u32[]{:S(2)}, u32[]{:S(2)}) %collective-permute-start.1) | collective-permute-done | bytes 16416 | tf_op jit(solution)/shard_map/projection/ppermute | solution.py:25
  93.2 0.0 copy-done
  93.2 0.8 norm.2
  93.9 0.0 copy-start.1
  93.9 9.8 %all-to-all-start.4 = ((f32[16,8,128]{2,1,0:T(8,128)}), f32[16,8,128]{2,1,0:T(8,128)S(1)}, u32[]{:S(2)}, u32[]{:S(2)}) async-start(f32[16,8,128]{2,1,0:T(8,128)} %get-tuple-element.8), calls=%async_computation.4 | async-start | bytes 131072 | tf_op jit(solution)/shard_map/norm/all_to_all | solution.py:21
  103.7 0.0 copy-done.1
  103.8 7.3 %all-to-all-done.4.squares_ref = f32[16,8,128]{2,1,0:T(8,128)S(1)} async-done(((f32[16,8,128]{2,1,0:T(8,128)}), f32[16,8,128]{2,1,0:T(8,128)S(1)}, u32[]{:S(2)}, u32[]{:S(2)}) %all-to-all-start.4) | async-done | bytes 65568 | tf_op jit(solution)/shard_map/norm/all_to_all | solution.py:21
  111.1 0.8 norm.3
  (3 shorter events, 0.1 us)
Async XLA Ops:
  2.2 9.4 %all-to-all-start = ((bf16[4,256,128]{2,1,0:T(8,128)(2,1)}), bf16[4,256,128]{2,1,0:T(8,128)(2,1)S(1)}, u32[]{:S(2)}, u32[]{:S(2)}) async-start(bf16[4,256,128]{2,1,0:T(8,128)(2,1)} %broadcast_in_dim.3), calls=%async_computation | async-start | bytes 524288 | tf_op jit(solution)/shard_map/weights/all_to_all | solution.py:21
  11.6 47.7 %collective-permute-start = (bf16[4,256,128]{2,1,0:T(8,128)(2,1)S(1)}, bf16[4,256,128]{2,1,0:T(8,128)(2,1)S(1)}, u32[]{:S(2)}, u32[]{:S(2)}) collective-permute-start(bf16[4,256,128]{2,1,0:T(8,128)(2,1)S(1)} %all-to-all-done), channel_id=1, source_target_pairs={{0,96},{16,944},{32,736},{48,304},{64,928},{80,112},{96,288},{112,... | collective-permute-start | bytes 786440 | tf_op jit(solution)/shard_map/attention/ppermute | solution.py:25
  39.2 30.7 %all-to-all-start.2 = ((bf16[16,16,256]{2,1,0:T(8,128)(2,1)}), bf16[16,16,256]{2,1,0:T(8,128)(2,1)S(1)}, u32[]{:S(2)}, u32[]{:S(2)}) async-start(bf16[16,16,256]{2,1,0:T(8,128)(2,1)} %attention.4), calls=%async_computation.2 | async-start | bytes 262144 | tf_op jit(solution)/shard_map/attention/all_to_all | solution.py:21
  85.2 8.0 %copy-start = (bf16[4,4,512]{2,1,0:T(4,128)(2,1)S(1)}, bf16[4,4,512]{2,1,0:T(4,128)(2,1)}, u32[]{:S(2)}) copy-start(bf16[4,4,512]{2,1,0:T(4,128)(2,1)} %stream_ref.1) | copy-start | bytes 49156
  85.2 7.9 %collective-permute-start.1 = (bf16[16,512]{1,0:T(8,128)(2,1)S(1)}, bf16[16,512]{1,0:T(8,128)(2,1)S(1)}, u32[]{:S(2)}, u32[]{:S(2)}) collective-permute-start(bf16[16,512]{1,0:T(8,128)(2,1)S(1)} %projection.3), channel_id=1, source_target_pairs={{0,10},{1,26},{2,42},{3,58},{4,74},{5,90},{6,106},{7,122},{8,138},... | collective-permute-start | bytes 49160 | tf_op jit(solution)/shard_map/projection/ppermute | solution.py:25
  93.9 9.8 %copy-start.1 = (bf16[512]{0:T(512)(128)(2,1)S(1)}, bf16[512]{0:T(512)(128)(2,1)}, u32[]{:S(2)}) copy-start(bf16[512]{0:T(512)(128)(2,1)} %param.17) | copy-start | bytes 3076
  93.9 17.1 %all-to-all-start.4 = ((f32[16,8,128]{2,1,0:T(8,128)}), f32[16,8,128]{2,1,0:T(8,128)S(1)}, u32[]{:S(2)}, u32[]{:S(2)}) async-start(f32[16,8,128]{2,1,0:T(8,128)} %get-tuple-element.8), calls=%async_computation.4 | async-start | bytes 131072 | tf_op jit(solution)/shard_map/norm/all_to_all | solution.py:21
